TPU v7x, 512 devices: a whole 4x4x16 slice. The times are simulated.
512 devices in a mesh: seq: 32 (over z, core), coarse: 4 (over y), exp: 4 (over x).
Axes of the slice: x: 4, y: 4, z: 16, core: 2. Of those that a mesh axis runs over, the one named last changes fastest.
Arguments:
- bytes_in: bfloat16 [4, 16384, 1024], P('exp', 'seq'), may hold values from -6 to 6
- norm_gain: float32 [1024], replicated, may hold values from 0.5 to 1.5
- qkv_weight: bfloat16 [3, 1024, 1024], P(None, None, 'coarse'), may hold values from -0.1875 to 0.1875
- gate_weight_enc: bfloat16 [2, 1024, 8], P(None, None, 'coarse'), may hold values from -0.1875 to 0.1875
- decay_rate: float32 [8], P('coarse'), may hold values from 0 to 0.05
- write_bias: float32 [8], P('coarse')
- head_gain: float32 [1024], P('coarse'), may hold values from 0.25 to 1.75
- boundaries: int32 [4, 16384], P('exp', 'seq'), may hold values from 0 to 1, as said below
- picks: int32 [4, 4096, 8], P('exp', ('seq', 'coarse')), may hold values from 0 to 127, as said below
- pick_gates: float32 [4, 4096, 8], P('exp', ('seq', 'coarse')), may hold values from 0.05 to 0.5
- extension: bfloat16 [1024], replicated, may hold values from -6 to 6
- expert_gate: bfloat16 [128, 2048, 512], P(('seq', 'exp'), 'coarse'), may hold values from -0.125 to 0.125
- expert_up: bfloat16 [128, 2048, 512], P(('seq', 'exp'), 'coarse'), may hold values from -0.125 to 0.125
- expert_down: bfloat16 [128, 512, 1024], P(('seq', 'exp'), None, 'coarse'), may hold values from -0.25 to 0.25
Outputs:
- mixed: bfloat16 [4, 16384, 1024], P('exp', 'seq', 'coarse')
Inputs may be any that keep to these rules, and one draw needn't show every extreme that they name: Byte 0 of every sequence is a boundary. Each byte block holds 64 to 128 boundaries, and in every sequence some block holds exactly 128. `picks`: row b * 128 + s belongs to the s-th boundary of byte block b; rows past the block's number of boundaries are unused. Each row names 8 different experts. Within each aligned run of 32 rows no expert is named more than 2 times by used rows, and a run whose rows are all used names every expert exactly 2 times.
All inputs are finite; a program needn't handle non-finite values.
Results may differ from a plain program's by a relative error of at most 0.0063.
Values may be sent and summed in bfloat16 or wider, within the bound.
No kernel may reach another device: no remote copies, remote signals or barrier semaphores. Data moves between devices by JAX's collectives and lax.ppermute only.
A program may use at most 64 MiB of HBM per device.

v0:
```python
import jax
import jax.numpy as jnp
from jax import lax
from jax.sharding import PartitionSpec as P

BLOCK = 64


precise = lax.Precision.HIGHEST


def passed_along(x, axis, by):
    count = lax.axis_size(axis)
    pairs = [(i, i + by) for i in range(count) if 0 <= i + by < count]
    return lax.ppermute(x, axis, pairs)


def block_terms(queries, key_vecs, write_rate, log_decay):
    block_len = write_rate.shape[-1]
    positions = jnp.arange(block_len)
    causal = positions[:, None] >= positions[None, :]
    strict = positions[:, None] > positions[None, :]
    cum_decay = jnp.cumsum(log_decay, axis=-1)
    gap_log = cum_decay[..., :, None] - cum_decay[..., None, :]
    decay_mat = jnp.where(causal, jnp.exp(jnp.where(causal, gap_log, 0.0)), 0.0)
    key_gram = jnp.einsum("...td,...sd->...ts", key_vecs, key_vecs, precision=precise)
    unit_lower = jnp.where(strict, write_rate[..., :, None] * decay_mat * key_gram, 0.0) + jnp.eye(
        block_len, dtype=jnp.float32
    )
    attend_mat = jnp.einsum("...td,...sd->...ts", queries, key_vecs, precision=precise) * decay_mat
    growth = jnp.exp(cum_decay)
    block_decay = growth[..., -1]
    key_decayed = key_vecs * jnp.exp(cum_decay[..., -1:] - cum_decay)[..., None]
    return (unit_lower, attend_mat, growth, key_decayed, block_decay)


def lower_solve(unit_lower, right_side):
    return lax.linalg.triangular_solve(
        unit_lower, right_side, left_side=True, lower=True, unit_diagonal=True
    )


def batched_mm(first_mat, second_mat):
    return jnp.einsum("hij,hjk->hik", first_mat, second_mat, precision=precise)


def shards(
    bytes_in,
    norm_gain,
    qkv_weight,
    gate_weight_enc,
    decay_rate,
    write_bias,
    head_gain,
    boundaries,
    picks,
    pick_gates,
    extension,
    expert_gate,
    expert_up,
    expert_down,
):
    byte_rows = bytes_in[0]
    byte_total, model_width = byte_rows.shape
    byte_float = byte_rows.astype(jnp.float32)
    normed = (
        byte_float
        * lax.rsqrt(jnp.mean(byte_float * byte_float, -1, keepdims=True) + 1e-05)
        * norm_gain
    ).astype(jnp.bfloat16)
    heads_local = decay_rate.shape[0]
    head_dim = qkv_weight.shape[2] // heads_local
    block_total = byte_total // BLOCK
    coarse_index = lax.axis_index("coarse")
    coarse_total = lax.axis_size("coarse")
    full_gate, full_up, full_down = (
        lax.all_gather(expert_gate, "coarse", axis=1, tiled=True),
        lax.all_gather(expert_up, "coarse", axis=1, tiled=True),
        lax.all_gather(expert_down, "coarse", axis=2, tiled=True),
    )
    projected = jnp.einsum("td,cde->cte", normed, qkv_weight, preferred_element_type=jnp.float32)
    linear_gates = jnp.einsum(
        "td,cdh->cth", normed, gate_weight_enc, preferred_element_type=jnp.float32
    )

    def split_heads(array):
        return (
            array.reshape(byte_total, heads_local, head_dim)
            .transpose(1, 0, 2)
            .reshape(heads_local, block_total, BLOCK, head_dim)
        )

    def unit_rows(array):
        heads_form = split_heads(jax.nn.silu(array))
        return heads_form * lax.rsqrt(jnp.sum(heads_form * heads_form, -1, keepdims=True) + 1e-06)

    def per_head(array):
        return array.T.reshape(heads_local, block_total, BLOCK)

    queries = unit_rows(projected[0])
    key_vecs = unit_rows(projected[1])
    values = split_heads(jax.nn.silu(projected[2]))
    write_rate = per_head(jax.nn.sigmoid(linear_gates[1] + write_bias[None, :]))
    log_decay = per_head(-decay_rate[None, :] * jax.nn.softplus(linear_gates[0]))
    unit_lower, attend_mat, growth, key_decayed, block_decay = block_terms(
        queries, key_vecs, write_rate, log_decay
    )
    values_wide = jnp.concatenate([jnp.zeros_like(values), values], axis=-1)
    free_update = lower_solve(unit_lower, write_rate[..., None] * values_wide)
    state_weight = lower_solve(unit_lower, (write_rate * growth)[..., None] * key_vecs)
    query_grown = growth[..., None] * queries

    def advance(carry_state, inputs):
        free_b, weight_b, query_b, attend_b, decayed_b, scale_b = inputs
        update = free_b - jnp.einsum("htd,hde->hte", weight_b, carry_state, precision=precise)
        block_out = jnp.einsum("htd,hde->hte", query_b, carry_state, precision=precise)
        block_out = block_out + jnp.einsum("hts,hse->hte", attend_b, update, precision=precise)
        carry_state = scale_b[:, None, None] * carry_state + jnp.einsum(
            "hsd,hse->hde", decayed_b, update, precision=precise
        )
        return (carry_state, block_out)

    stacked = tuple(
        (
            jnp.moveaxis(array, 1, 0)
            for array in (
                free_update,
                state_weight,
                query_grown,
                attend_mat,
                key_decayed,
                block_decay,
            )
        )
    )
    identity_map = jnp.broadcast_to(
        jnp.eye(head_dim, dtype=jnp.float32), (heads_local, head_dim, head_dim)
    )
    start_state = jnp.concatenate([identity_map, jnp.zeros_like(identity_map)], axis=-1)
    block_end, block_outs = lax.scan(advance, start_state, stacked)
    block_outs = jnp.moveaxis(block_outs, 0, 1).reshape(heads_local, byte_total, 2 * head_dim)
    query_maps = block_outs[..., :head_dim]
    local_out = block_outs[..., head_dim:]
    carry_map = block_end[..., :head_dim]
    carry_add = block_end[..., head_dim:]

    def hand_on(turn_index, carry_state):
        outgoing = batched_mm(carry_map, carry_state) + carry_add
        return passed_along(outgoing, "seq", 1)

    state_in = lax.fori_loop(0, lax.axis_size("seq") - 1, hand_on, jnp.zeros_like(carry_add))
    head_out = local_out + jnp.einsum("htd,hde->hte", query_maps, state_in, precision=precise)
    head_norm = (
        head_out
        * lax.rsqrt(jnp.mean(head_out * head_out, -1, keepdims=True) + 1e-06)
        * head_gain.reshape(heads_local, head_dim)[:, None, :]
    )
    head_rows = (
        head_norm.transpose(1, 0, 2)
        .reshape(byte_total, heads_local * head_dim)
        .astype(jnp.bfloat16)
    )
    gathered = lax.all_gather(head_rows, "coarse", axis=1, tiled=True)
    hidden_bytes = (byte_float + gathered.astype(jnp.float32)).astype(jnp.bfloat16)
    bound_mask = boundaries[0]
    bound_count = jnp.sum(bound_mask)
    bound_rank = jnp.cumsum(bound_mask) - 1
    local_slots = picks.shape[1]
    pick_count = picks.shape[2]
    slot_total = local_slots * coarse_total
    experts_all = lax.axis_size(("seq", "exp"))
    capacity = local_slots * pick_count // experts_all
    slot_pos = (
        jnp.zeros((slot_total,), jnp.int32)
        .at[jnp.where(bound_mask == 1, bound_rank, slot_total)]
        .set(jnp.arange(byte_total, dtype=jnp.int32), mode="drop")
    )
    first_slot = coarse_index * local_slots
    own_pos = lax.dynamic_slice_in_dim(slot_pos, first_slot, local_slots, 0)
    stretch_rows = jnp.take(hidden_bytes, own_pos, axis=0)
    live_slots = first_slot + jnp.arange(local_slots) < bound_count
    expert_ids = picks[0].reshape(-1)
    live_flat = jnp.repeat(live_slots, pick_count)
    expert_hits = (
        (expert_ids[:, None] == jnp.arange(experts_all)[None, :]) & live_flat[:, None]
    ).astype(jnp.int32)
    arrival = jnp.sum(expert_hits * (jnp.cumsum(expert_hits, axis=0) - 1), axis=1)
    target = jnp.where(live_flat, expert_ids * capacity + arrival, experts_all * capacity)
    row_index = jnp.repeat(jnp.arange(local_slots, dtype=jnp.int32), pick_count)
    source_row = (
        jnp.full((experts_all * capacity,), local_slots, jnp.int32)
        .at[target]
        .set(row_index, mode="drop")
    )
    padded_rows = jnp.concatenate([stretch_rows, jnp.zeros((1, model_width), jnp.bfloat16)], axis=0)
    outgoing = jnp.take(padded_rows, source_row, axis=0).reshape(experts_all, capacity, model_width)
    lower_gate = full_gate[0, :model_width]
    lower_up = full_up[0, :model_width]
    gate_offset = jnp.dot(
        extension[None, :], full_gate[0, model_width:], preferred_element_type=jnp.float32
    )
    up_offset = jnp.dot(
        extension[None, :], full_up[0, model_width:], preferred_element_type=jnp.float32
    )
    received = lax.all_to_all(outgoing, ("seq", "exp"), split_axis=0, concat_axis=0, tiled=True)
    source_count = received.shape[0]
    slot_span = received.shape[1]
    flat_rows = received.reshape(source_count * slot_span, model_width)
    gate_sum = jnp.dot(flat_rows, lower_gate, preferred_element_type=jnp.float32) + gate_offset
    up_sum = jnp.dot(flat_rows, lower_up, preferred_element_type=jnp.float32) + up_offset
    hidden_act = (jax.nn.silu(gate_sum) * up_sum).astype(jnp.bfloat16)
    expert_value = jnp.dot(hidden_act, full_down[0], preferred_element_type=jnp.float32).astype(
        jnp.bfloat16
    )
    expert_value = expert_value.reshape(source_count, slot_span, model_width)
    returned = lax.all_to_all(expert_value, ("seq", "exp"), split_axis=0, concat_axis=0, tiled=True)
    flat_back = jnp.concatenate(
        [
            returned.reshape(experts_all * capacity, model_width),
            jnp.zeros((1, model_width), jnp.bfloat16),
        ],
        axis=0,
    )
    values_back = (
        jnp.take(flat_back, target, axis=0)
        .astype(jnp.float32)
        .reshape(local_slots, pick_count, model_width)
    )
    stretch_out = jnp.sum(pick_gates[0][..., None] * values_back, axis=1)
    all_stretches = lax.all_to_all(stretch_out, "coarse", split_axis=1, concat_axis=0, tiled=True)
    share_width = all_stretches.shape[1]
    last_row = lax.dynamic_index_in_dim(all_stretches, bound_count - 1, 0, keepdims=False)
    previous = passed_along(last_row, "seq", 1)
    lookup_rows = jnp.concatenate([all_stretches, previous[None, :]], axis=0)
    spread_rows = jnp.take(lookup_rows, jnp.where(bound_rank < 0, slot_total, bound_rank), axis=0)
    own_share = lax.dynamic_slice_in_dim(
        hidden_bytes, coarse_index * share_width, share_width, 1
    ).astype(jnp.float32)
    return (own_share + spread_rows).astype(jnp.bfloat16)[None]


def solution(mesh):
    placed = (
        P("exp", "seq", None),
        P(),
        P(None, None, "coarse"),
        P(None, None, "coarse"),
        P("coarse"),
        P("coarse"),
        P("coarse"),
        P("exp", "seq"),
        P("exp", ("seq", "coarse"), None),
        P("exp", ("seq", "coarse"), None),
        P(),
        P(("seq", "exp"), "coarse", None),
        P(("seq", "exp"), "coarse", None),
        P(("seq", "exp"), None, "coarse"),
    )
    return jax.shard_map(
        shards, mesh=mesh, in_specs=placed, out_specs=P("exp", "seq", "coarse"), check_vma=False
    )
```

profile of v0, /device:TPU:1, one launch (start us, length us, event | category | flops | bytes accessed | tf_op | source)
XLA Modules:
  0.0 626.6 jit_solution(8468830555310264354)
XLA Ops:
  8.3 2.3 convolution_bitcast_fusion
  15.6 2.1 fusion.25
  17.7 79.4 %custom-call.5 = f32[2,8,1,64,64]{3,4,2,1,0:T(8,128)S(1)} custom-call(f32[2,8,1,64,64]{4,3,2,1,0:T(8,128)} %fusion.25), custom_call_target="InvertDiagBlocksLowerTriangular" | custom-call | tf_op jit(solution)/shard_map/triangular_solve | solution.py:38
  99.5 2.1 copy.69
  102.8 2.1 convolution_bitcast_fusion.3
  104.8 2.3 convolution_bitcast_fusion.1
  110.2 36.5 %while.22 = (s32[]{:T(128)}, f32[2,128,256]{2,1,0:T(8,128)S(1)}, f32[8,2,64,256]{3,2,1,0:T(8,128)}, f32[8,2]{1,0:T(8,128)S(1)}, f32[8,2,64,128]{3,2,0,1:T(8,128)...) while((s32[]{:T(128)}, f32[2,128,256]{2,1,0:T(8,128)S(1)}, ...), condition=%wide.region_5.6_spmd, body=%wide.region_4.5_spmd.sunk | while | flops 176357376 | bytes 2231425 | solution.py:140
  148.1 222.8 %while.23 = (s32[]{:T(128)}, f32[2,128,128]{2,1,0:T(8,128)S(1)}, f32[2,128,128]{2,1,0:T(8,128)S(1)}, f32[2,128,128]{2,1,0:T(8,128)S(1)}, s32[]{:T(128)}) while((s32[]{:T(128)}, f32[2,128,128]{2,1,0:T(8,128)S(1)}, f32[2,128,128]{2,1,0:T(8,128)S(1)}, f32[2,128,128]{2,1,0:T(8,128)S(1)}, s32[]{:T(128)}) %tuple.53), condition=%wide.region_7.8_spmd, body=%wide.region_6.7_spmd.sunk | while | flops 50364416 | bytes 1048677 | solution.py:151
  148.4 4.9 collective-permute-start
  153.3 4.0 collective-permute-done
  157.6 2.2 collective-permute-start
  159.9 1.9 collective-permute-done
  162.1 4.4 collective-permute-start
  166.4 1.9 collective-permute-done
  168.6 4.4 collective-permute-start
  173.0 1.9 collective-permute-done
  175.2 4.4 collective-permute-start
  179.6 1.9 collective-permute-done
  181.8 4.4 collective-permute-start
  188.3 4.4 collective-permute-start
  194.9 4.4 collective-permute-start
  199.3 1.9 collective-permute-done
  201.5 4.4 collective-permute-start
  208.0 4.4 collective-permute-start
  214.6 4.4 collective-permute-start
  221.1 4.4 collective-permute-start
  225.5 1.9 collective-permute-done
  227.7 4.4 collective-permute-start
  234.3 4.4 collective-permute-start
  238.6 1.9 collective-permute-done
  240.8 4.4 collective-permute-start
  247.4 5.0 collective-permute-start
  254.6 5.6 collective-permute-start
  262.4 5.6 collective-permute-start
  270.1 5.6 collective-permute-start
  277.9 5.6 collective-permute-start
  283.5 1.9 collective-permute-done
  285.7 5.6 collective-permute-start
  291.2 1.9 collective-permute-done
  293.4 5.6 collective-permute-start
  301.2 5.6 collective-permute-start
  309.0 5.6 collective-permute-start
  316.8 5.6 collective-permute-start
  324.5 5.6 collective-permute-start
  332.3 5.6 collective-permute-start
  337.9 1.9 collective-permute-done
  340.1 5.6 collective-permute-start
  347.8 5.6 collective-permute-start
  355.6 5.6 collective-permute-start
  363.4 5.6 collective-permute-start
  380.0 2.4 scatter_custom_fusion.1
  382.6 46.6 %all-gather.5.cloned.1.call-done = bf16[512,1024]{1,0:T(8,128)(2,1)} async-done(((bf16[512,256]{1,0:T(8,128)(2,1)}), bf16[512,1024]{1,0:T(8,128)(2,1)}) %all-gather.5.cloned.1.call-update) | async-done | bytes 1048592 | tf_op jit(solution)/shard_map/all_gather | solution.py:163
  429.2 2.6 fusion.19
  431.8 2.0 gather_fusion
  436.7 17.5 %all-to-all-start = ((bf16[128,2,1024]{2,1,0:T(2,128)(2,1)}), bf16[128,2,1024]{2,1,0:T(2,128)(2,1)S(1)}, u32[]{:S(2)}, u32[]{:S(2)}) async-start(bf16[128,2,1024]{2,1,0:T(2,128)(2,1)} %broadcast_select_fusion), calls=%async_computation | async-start | bytes 1048576 | tf_op jit(solution)/shard_map/all_to_all | solution.py:205
  454.8 17.0 %all-gather.7.cloned.1.call-done = bf16[1,2048,512]{2,1,0:T(8,128)(2,1)} async-done(((bf16[1,512,512]{2,1,0:T(8,128)(2,1)}), bf16[1,2048,512]{2,1,0:T(8,128)(2,1)}) %all-gather.7.cloned.1.call-update) | async-done | bytes 2097168 | tf_op jit(solution)/shard_map/all_gather | solution.py:77
  473.2 39.3 %all-gather.9.cloned.1.call-done = bf16[1,2048,512]{2,1,0:T(8,128)(2,1)} async-done(((bf16[1,512,512]{2,1,0:T(8,128)(2,1)}), bf16[1,2048,512]{2,1,0:T(8,128)(2,1)}) %all-gather.9.cloned.1.call-update) | async-done | bytes 2097168 | tf_op jit(solution)/shard_map/all_gather | solution.py:78
  515.9 31.4 %all-gather.11.cloned.1.call-done = bf16[1,512,1024]{2,1,0:T(8,128)(2,1)} async-done(((bf16[1,512,256]{2,1,0:T(8,128)(2,1)}), bf16[1,512,1024]{2,1,0:T(8,128)(2,1)}) %all-gather.11.cloned.1.call-update) | async-done | bytes 1048592 | tf_op jit(solution)/shard_map/all_gather | solution.py:79
  547.3 2.4 convolution_convert_fusion
  550.7 17.5 %all-to-all-start.1 = ((bf16[128,2,1024]{2,1,0:T(2,128)(2,1)}), bf16[128,2,1024]{2,1,0:T(2,128)(2,1)S(1)}, u32[]{:S(2)}, u32[]{:S(2)}) async-start(bf16[128,2,1024]{2,1,0:T(2,128)(2,1)} %reshape.363), calls=%async_computation.1 | async-start | bytes 1048576 | tf_op jit(solution)/shard_map/all_to_all | solution.py:216
  568.4 33.3 %all-to-all-done.1 = bf16[128,2,1024]{2,1,0:T(2,128)(2,1)S(1)} async-done(((bf16[128,2,1024]{2,1,0:T(2,128)(2,1)}), bf16[128,2,1024]{2,1,0:T(2,128)(2,1)S(1)}, u32[]{:S(2)}, u32[]{:S(2)}) %all-to-all-start.1) | async-done | bytes 524320 | tf_op jit(solution)/shard_map/all_to_all | solution.py:216
  604.3 3.7 all-to-all-start.2
  609.1 4.2 all-to-all-done.2
  613.3 2.7 collective-permute-start.1
  (229 shorter events, 122.5 us)
Async XLA Ops:
  6.5 1.7 copy-start
  6.5 422.7 %all-gather.5.cloned.1.call-start = ((), (), s32[]{:S(2)}) async-start(), calls=%async_computation.3 | async-start | bytes 1310720 | tf_op jit(solution)/shard_map/all_gather | solution.py:163
  10.6 3.5 copy-start.1
  10.6 3.5 copy-start.10
  10.6 3.5 copy-start.11
  11.8 2.8 copy-start.12
  11.8 2.9 copy-start.9
  14.6 82.5 %copy-start.3 = (f32[1,512,256]{1,2,0:T(8,128)S(1)}, f32[1,512,256]{1,2,0:T(8,128)}, u32[]{:S(2)}) copy-start(f32[1,512,256]{1,2,0:T(8,128)} %get-tuple-element.139) | copy-start | bytes 1572868
  148.1 223.6 %copy-start.8 = (f32[256]{0:T(256)S(1)}, f32[256]{0:T(256)}, u32[]{:S(2)}) copy-start(f32[256]{0:T(256)} %param.24) | copy-start | bytes 3076
  148.4 9.0 %collective-permute-start = (f32[2,128,128]{2,1,0:T(8,128)S(1)}, f32[2,128,128]{2,1,0:T(8,128)S(1)}, u32[]{:S(2)}, u32[]{:S(2)}) collective-permute-start(f32[2,128,128]{2,1,0:T(8,128)S(1)} %convolution_add_fusion.9), channel_id=1, source_target_pairs={{0,16},{16,32},{32,48},{48,64},{64,80},{80,96},{96,112},{112,128},... | collective-permute-start | bytes 393224 | tf_op jit(solution)/shard_map/while/body/eval_jaxpr/ppermute | solution.py:15
  157.6 4.2 collective-permute-start
  162.1 6.3 %collective-permute-start = (f32[2,128,128]{2,1,0:T(8,128)S(1)}, f32[2,128,128]{2,1,0:T(8,128)S(1)}, u32[]{:S(2)}, u32[]{:S(2)}) collective-permute-start(f32[2,128,128]{2,1,0:T(8,128)S(1)} %convolution_add_fusion.9), channel_id=1, source_target_pairs={{0,16},{16,32},{32,48},{48,64},{64,80},{80,96},{96,112},{112,128},... | collective-permute-start | bytes 393224 | tf_op jit(solution)/shard_map/while/body/eval_jaxpr/ppermute | solution.py:15
  168.6 6.3 %collective-permute-start = (f32[2,128,128]{2,1,0:T(8,128)S(1)}, f32[2,128,128]{2,1,0:T(8,128)S(1)}, u32[]{:S(2)}, u32[]{:S(2)}) collective-permute-start(f32[2,128,128]{2,1,0:T(8,128)S(1)} %convolution_add_fusion.9), channel_id=1, source_target_pairs={{0,16},{16,32},{32,48},{48,64},{64,80},{80,96},{96,112},{112,128},... | collective-permute-start | bytes 393224 | tf_op jit(solution)/shard_map/while/body/eval_jaxpr/ppermute | solution.py:15
  175.2 6.3 %collective-permute-start = (f32[2,128,128]{2,1,0:T(8,128)S(1)}, f32[2,128,128]{2,1,0:T(8,128)S(1)}, u32[]{:S(2)}, u32[]{:S(2)}) collective-permute-start(f32[2,128,128]{2,1,0:T(8,128)S(1)} %convolution_add_fusion.9), channel_id=1, source_target_pairs={{0,16},{16,32},{32,48},{48,64},{64,80},{80,96},{96,112},{112,128},... | collective-permute-start | bytes 393224 | tf_op jit(solution)/shard_map/while/body/eval_jaxpr/ppermute | solution.py:15
  181.8 6.3 %collective-permute-start = (f32[2,128,128]{2,1,0:T(8,128)S(1)}, f32[2,128,128]{2,1,0:T(8,128)S(1)}, u32[]{:S(2)}, u32[]{:S(2)}) collective-permute-start(f32[2,128,128]{2,1,0:T(8,128)S(1)} %convolution_add_fusion.9), channel_id=1, source_target_pairs={{0,16},{16,32},{32,48},{48,64},{64,80},{80,96},{96,112},{112,128},... | collective-permute-start | bytes 393224 | tf_op jit(solution)/shard_map/while/body/eval_jaxpr/ppermute | solution.py:15
  188.3 6.3 %collective-permute-start = (f32[2,128,128]{2,1,0:T(8,128)S(1)}, f32[2,128,128]{2,1,0:T(8,128)S(1)}, u32[]{:S(2)}, u32[]{:S(2)}) collective-permute-start(f32[2,128,128]{2,1,0:T(8,128)S(1)} %convolution_add_fusion.9), channel_id=1, source_target_pairs={{0,16},{16,32},{32,48},{48,64},{64,80},{80,96},{96,112},{112,128},... | collective-permute-start | bytes 393224 | tf_op jit(solution)/shard_map/while/body/eval_jaxpr/ppermute | solution.py:15
  194.9 6.3 %collective-permute-start = (f32[2,128,128]{2,1,0:T(8,128)S(1)}, f32[2,128,128]{2,1,0:T(8,128)S(1)}, u32[]{:S(2)}, u32[]{:S(2)}) collective-permute-start(f32[2,128,128]{2,1,0:T(8,128)S(1)} %convolution_add_fusion.9), channel_id=1, source_target_pairs={{0,16},{16,32},{32,48},{48,64},{64,80},{80,96},{96,112},{112,128},... | collective-permute-start | bytes 393224 | tf_op jit(solution)/shard_map/while/body/eval_jaxpr/ppermute | solution.py:15
  201.5 6.3 %collective-permute-start = (f32[2,128,128]{2,1,0:T(8,128)S(1)}, f32[2,128,128]{2,1,0:T(8,128)S(1)}, u32[]{:S(2)}, u32[]{:S(2)}) collective-permute-start(f32[2,128,128]{2,1,0:T(8,128)S(1)} %convolution_add_fusion.9), channel_id=1, source_target_pairs={{0,16},{16,32},{32,48},{48,64},{64,80},{80,96},{96,112},{112,128},... | collective-permute-start | bytes 393224 | tf_op jit(solution)/shard_map/while/body/eval_jaxpr/ppermute | solution.py:15
  208.0 6.3 %collective-permute-start = (f32[2,128,128]{2,1,0:T(8,128)S(1)}, f32[2,128,128]{2,1,0:T(8,128)S(1)}, u32[]{:S(2)}, u32[]{:S(2)}) collective-permute-start(f32[2,128,128]{2,1,0:T(8,128)S(1)} %convolution_add_fusion.9), channel_id=1, source_target_pairs={{0,16},{16,32},{32,48},{48,64},{64,80},{80,96},{96,112},{112,128},... | collective-permute-start | bytes 393224 | tf_op jit(solution)/shard_map/while/body/eval_jaxpr/ppermute | solution.py:15
  214.6 6.3 %collective-permute-start = (f32[2,128,128]{2,1,0:T(8,128)S(1)}, f32[2,128,128]{2,1,0:T(8,128)S(1)}, u32[]{:S(2)}, u32[]{:S(2)}) collective-permute-start(f32[2,128,128]{2,1,0:T(8,128)S(1)} %convolution_add_fusion.9), channel_id=1, source_target_pairs={{0,16},{16,32},{32,48},{48,64},{64,80},{80,96},{96,112},{112,128},... | collective-permute-start | bytes 393224 | tf_op jit(solution)/shard_map/while/body/eval_jaxpr/ppermute | solution.py:15
  221.1 6.3 %collective-permute-start = (f32[2,128,128]{2,1,0:T(8,128)S(1)}, f32[2,128,128]{2,1,0:T(8,128)S(1)}, u32[]{:S(2)}, u32[]{:S(2)}) collective-permute-start(f32[2,128,128]{2,1,0:T(8,128)S(1)} %convolution_add_fusion.9), channel_id=1, source_target_pairs={{0,16},{16,32},{32,48},{48,64},{64,80},{80,96},{96,112},{112,128},... | collective-permute-start | bytes 393224 | tf_op jit(solution)/shard_map/while/body/eval_jaxpr/ppermute | solution.py:15
  227.7 6.3 %collective-permute-start = (f32[2,128,128]{2,1,0:T(8,128)S(1)}, f32[2,128,128]{2,1,0:T(8,128)S(1)}, u32[]{:S(2)}, u32[]{:S(2)}) collective-permute-start(f32[2,128,128]{2,1,0:T(8,128)S(1)} %convolution_add_fusion.9), channel_id=1, source_target_pairs={{0,16},{16,32},{32,48},{48,64},{64,80},{80,96},{96,112},{112,128},... | collective-permute-start | bytes 393224 | tf_op jit(solution)/shard_map/while/body/eval_jaxpr/ppermute | solution.py:15
  234.3 6.3 %collective-permute-start = (f32[2,128,128]{2,1,0:T(8,128)S(1)}, f32[2,128,128]{2,1,0:T(8,128)S(1)}, u32[]{:S(2)}, u32[]{:S(2)}) collective-permute-start(f32[2,128,128]{2,1,0:T(8,128)S(1)} %convolution_add_fusion.9), channel_id=1, source_target_pairs={{0,16},{16,32},{32,48},{48,64},{64,80},{80,96},{96,112},{112,128},... | collective-permute-start | bytes 393224 | tf_op jit(solution)/shard_map/while/body/eval_jaxpr/ppermute | solution.py:15
  240.8 6.3 %collective-permute-start = (f32[2,128,128]{2,1,0:T(8,128)S(1)}, f32[2,128,128]{2,1,0:T(8,128)S(1)}, u32[]{:S(2)}, u32[]{:S(2)}) collective-permute-start(f32[2,128,128]{2,1,0:T(8,128)S(1)} %convolution_add_fusion.9), channel_id=1, source_target_pairs={{0,16},{16,32},{32,48},{48,64},{64,80},{80,96},{96,112},{112,128},... | collective-permute-start | bytes 393224 | tf_op jit(solution)/shard_map/while/body/eval_jaxpr/ppermute | solution.py:15
  247.4 6.9 %collective-permute-start = (f32[2,128,128]{2,1,0:T(8,128)S(1)}, f32[2,128,128]{2,1,0:T(8,128)S(1)}, u32[]{:S(2)}, u32[]{:S(2)}) collective-permute-start(f32[2,128,128]{2,1,0:T(8,128)S(1)} %convolution_add_fusion.9), channel_id=1, source_target_pairs={{0,16},{16,32},{32,48},{48,64},{64,80},{80,96},{96,112},{112,128},... | collective-permute-start | bytes 393224 | tf_op jit(solution)/shard_map/while/body/eval_jaxpr/ppermute | solution.py:15
  254.6 7.5 %collective-permute-start = (f32[2,128,128]{2,1,0:T(8,128)S(1)}, f32[2,128,128]{2,1,0:T(8,128)S(1)}, u32[]{:S(2)}, u32[]{:S(2)}) collective-permute-start(f32[2,128,128]{2,1,0:T(8,128)S(1)} %convolution_add_fusion.9), channel_id=1, source_target_pairs={{0,16},{16,32},{32,48},{48,64},{64,80},{80,96},{96,112},{112,128},... | collective-permute-start | bytes 393224 | tf_op jit(solution)/shard_map/while/body/eval_jaxpr/ppermute | solution.py:15
  262.4 7.5 %collective-permute-start = (f32[2,128,128]{2,1,0:T(8,128)S(1)}, f32[2,128,128]{2,1,0:T(8,128)S(1)}, u32[]{:S(2)}, u32[]{:S(2)}) collective-permute-start(f32[2,128,128]{2,1,0:T(8,128)S(1)} %convolution_add_fusion.9), channel_id=1, source_target_pairs={{0,16},{16,32},{32,48},{48,64},{64,80},{80,96},{96,112},{112,128},... | collective-permute-start | bytes 393224 | tf_op jit(solution)/shard_map/while/body/eval_jaxpr/ppermute | solution.py:15
  270.1 7.5 %collective-permute-start = (f32[2,128,128]{2,1,0:T(8,128)S(1)}, f32[2,128,128]{2,1,0:T(8,128)S(1)}, u32[]{:S(2)}, u32[]{:S(2)}) collective-permute-start(f32[2,128,128]{2,1,0:T(8,128)S(1)} %convolution_add_fusion.9), channel_id=1, source_target_pairs={{0,16},{16,32},{32,48},{48,64},{64,80},{80,96},{96,112},{112,128},... | collective-permute-start | bytes 393224 | tf_op jit(solution)/shard_map/while/body/eval_jaxpr/ppermute | solution.py:15
  277.9 7.5 %collective-permute-start = (f32[2,128,128]{2,1,0:T(8,128)S(1)}, f32[2,128,128]{2,1,0:T(8,128)S(1)}, u32[]{:S(2)}, u32[]{:S(2)}) collective-permute-start(f32[2,128,128]{2,1,0:T(8,128)S(1)} %convolution_add_fusion.9), channel_id=1, source_target_pairs={{0,16},{16,32},{32,48},{48,64},{64,80},{80,96},{96,112},{112,128},... | collective-permute-start | bytes 393224 | tf_op jit(solution)/shard_map/while/body/eval_jaxpr/ppermute | solution.py:15
  285.7 7.5 %collective-permute-start = (f32[2,128,128]{2,1,0:T(8,128)S(1)}, f32[2,128,128]{2,1,0:T(8,128)S(1)}, u32[]{:S(2)}, u32[]{:S(2)}) collective-permute-start(f32[2,128,128]{2,1,0:T(8,128)S(1)} %convolution_add_fusion.9), channel_id=1, source_target_pairs={{0,16},{16,32},{32,48},{48,64},{64,80},{80,96},{96,112},{112,128},... | collective-permute-start | bytes 393224 | tf_op jit(solution)/shard_map/while/body/eval_jaxpr/ppermute | solution.py:15
  293.4 7.5 %collective-permute-start = (f32[2,128,128]{2,1,0:T(8,128)S(1)}, f32[2,128,128]{2,1,0:T(8,128)S(1)}, u32[]{:S(2)}, u32[]{:S(2)}) collective-permute-start(f32[2,128,128]{2,1,0:T(8,128)S(1)} %convolution_add_fusion.9), channel_id=1, source_target_pairs={{0,16},{16,32},{32,48},{48,64},{64,80},{80,96},{96,112},{112,128},... | collective-permute-start | bytes 393224 | tf_op jit(solution)/shard_map/while/body/eval_jaxpr/ppermute | solution.py:15
  301.2 7.5 %collective-permute-start = (f32[2,128,128]{2,1,0:T(8,128)S(1)}, f32[2,128,128]{2,1,0:T(8,128)S(1)}, u32[]{:S(2)}, u32[]{:S(2)}) collective-permute-start(f32[2,128,128]{2,1,0:T(8,128)S(1)} %convolution_add_fusion.9), channel_id=1, source_target_pairs={{0,16},{16,32},{32,48},{48,64},{64,80},{80,96},{96,112},{112,128},... | collective-permute-start | bytes 393224 | tf_op jit(solution)/shard_map/while/body/eval_jaxpr/ppermute | solution.py:15
  309.0 7.5 %collective-permute-start = (f32[2,128,128]{2,1,0:T(8,128)S(1)}, f32[2,128,128]{2,1,0:T(8,128)S(1)}, u32[]{:S(2)}, u32[]{:S(2)}) collective-permute-start(f32[2,128,128]{2,1,0:T(8,128)S(1)} %convolution_add_fusion.9), channel_id=1, source_target_pairs={{0,16},{16,32},{32,48},{48,64},{64,80},{80,96},{96,112},{112,128},... | collective-permute-start | bytes 393224 | tf_op jit(solution)/shard_map/while/body/eval_jaxpr/ppermute | solution.py:15
  316.8 7.5 %collective-permute-start = (f32[2,128,128]{2,1,0:T(8,128)S(1)}, f32[2,128,128]{2,1,0:T(8,128)S(1)}, u32[]{:S(2)}, u32[]{:S(2)}) collective-permute-start(f32[2,128,128]{2,1,0:T(8,128)S(1)} %convolution_add_fusion.9), channel_id=1, source_target_pairs={{0,16},{16,32},{32,48},{48,64},{64,80},{80,96},{96,112},{112,128},... | collective-permute-start | bytes 393224 | tf_op jit(solution)/shard_map/while/body/eval_jaxpr/ppermute | solution.py:15
  324.5 7.5 %collective-permute-start = (f32[2,128,128]{2,1,0:T(8,128)S(1)}, f32[2,128,128]{2,1,0:T(8,128)S(1)}, u32[]{:S(2)}, u32[]{:S(2)}) collective-permute-start(f32[2,128,128]{2,1,0:T(8,128)S(1)} %convolution_add_fusion.9), channel_id=1, source_target_pairs={{0,16},{16,32},{32,48},{48,64},{64,80},{80,96},{96,112},{112,128},... | collective-permute-start | bytes 393224 | tf_op jit(solution)/shard_map/while/body/eval_jaxpr/ppermute | solution.py:15
  332.3 7.5 %collective-permute-start = (f32[2,128,128]{2,1,0:T(8,128)S(1)}, f32[2,128,128]{2,1,0:T(8,128)S(1)}, u32[]{:S(2)}, u32[]{:S(2)}) collective-permute-start(f32[2,128,128]{2,1,0:T(8,128)S(1)} %convolution_add_fusion.9), channel_id=1, source_target_pairs={{0,16},{16,32},{32,48},{48,64},{64,80},{80,96},{96,112},{112,128},... | collective-permute-start | bytes 393224 | tf_op jit(solution)/shard_map/while/body/eval_jaxpr/ppermute | solution.py:15
  340.1 7.5 %collective-permute-start = (f32[2,128,128]{2,1,0:T(8,128)S(1)}, f32[2,128,128]{2,1,0:T(8,128)S(1)}, u32[]{:S(2)}, u32[]{:S(2)}) collective-permute-start(f32[2,128,128]{2,1,0:T(8,128)S(1)} %convolution_add_fusion.9), channel_id=1, source_target_pairs={{0,16},{16,32},{32,48},{48,64},{64,80},{80,96},{96,112},{112,128},... | collective-permute-start | bytes 393224 | tf_op jit(solution)/shard_map/while/body/eval_jaxpr/ppermute | solution.py:15
  347.8 7.5 %collective-permute-start = (f32[2,128,128]{2,1,0:T(8,128)S(1)}, f32[2,128,128]{2,1,0:T(8,128)S(1)}, u32[]{:S(2)}, u32[]{:S(2)}) collective-permute-start(f32[2,128,128]{2,1,0:T(8,128)S(1)} %convolution_add_fusion.9), channel_id=1, source_target_pairs={{0,16},{16,32},{32,48},{48,64},{64,80},{80,96},{96,112},{112,128},... | collective-permute-start | bytes 393224 | tf_op jit(solution)/shard_map/while/body/eval_jaxpr/ppermute | solution.py:15
  355.6 7.5 %collective-permute-start = (f32[2,128,128]{2,1,0:T(8,128)S(1)}, f32[2,128,128]{2,1,0:T(8,128)S(1)}, u32[]{:S(2)}, u32[]{:S(2)}) collective-permute-start(f32[2,128,128]{2,1,0:T(8,128)S(1)} %convolution_add_fusion.9), channel_id=1, source_target_pairs={{0,16},{16,32},{32,48},{48,64},{64,80},{80,96},{96,112},{112,128},... | collective-permute-start | bytes 393224 | tf_op jit(solution)/shard_map/while/body/eval_jaxpr/ppermute | solution.py:15
  363.4 7.5 %collective-permute-start = (f32[2,128,128]{2,1,0:T(8,128)S(1)}, f32[2,128,128]{2,1,0:T(8,128)S(1)}, u32[]{:S(2)}, u32[]{:S(2)}) collective-permute-start(f32[2,128,128]{2,1,0:T(8,128)S(1)} %convolution_add_fusion.9), channel_id=1, source_target_pairs={{0,16},{16,32},{32,48},{48,64},{64,80},{80,96},{96,112},{112,128},... | collective-permute-start | bytes 393224 | tf_op jit(solution)/shard_map/while/body/eval_jaxpr/ppermute | solution.py:15
  370.9 3.5 copy-start.4
  370.9 5.3 copy-start.5
  371.7 57.5 %copy-start.2 = (bf16[1,512,1024]{2,1,0:T(8,128)(2,1)S(1)}, bf16[1,512,1024]{2,1,0:T(8,128)(2,1)}, u32[]{:S(2)}) copy-start(bf16[1,512,1024]{2,1,0:T(8,128)(2,1)} %param.18) | copy-start | bytes 3145732
  372.9 98.9 %all-gather.7.cloned.1.call-start = ((), (), s32[]{:S(2)}) async-start(), calls=%async_computation.4 | async-start | bytes 2621440 | tf_op jit(solution)/shard_map/all_gather | solution.py:77
  373.7 138.9 %all-gather.9.cloned.1.call-start = ((), (), s32[]{:S(2)}) async-start(), calls=%async_computation.5 | async-start | bytes 2621440 | tf_op jit(solution)/shard_map/all_gather | solution.py:78
  435.1 19.7 %copy-start.7 = (bf16[1024]{0:T(1024)(128)(2,1)S(1)}, bf16[1024]{0:T(1024)(128)(2,1)}, u32[]{:S(2)}) copy-start(bf16[1024]{0:T(1024)(128)(2,1)} %param.28) | copy-start | bytes 6148
  436.7 77.3 %all-to-all-start = ((bf16[128,2,1024]{2,1,0:T(2,128)(2,1)}), bf16[128,2,1024]{2,1,0:T(2,128)(2,1)S(1)}, u32[]{:S(2)}, u32[]{:S(2)}) async-start(bf16[128,2,1024]{2,1,0:T(2,128)(2,1)} %broadcast_select_fusion), calls=%async_computation | async-start | bytes 1048576 | tf_op jit(solution)/shard_map/all_to_all | solution.py:205
  454.2 93.1 %all-gather.11.cloned.1.call-start = ((), (), s32[]{:S(2)}) async-start(), calls=%async_computation.6 | async-start | bytes 1310720 | tf_op jit(solution)/shard_map/all_gather | solution.py:79
  549.7 18.6 %copy-start.6 = (f32[1,32,8]{1,2,0:T(8,128)S(1)}, f32[1,32,8]{1,2,0:T(8,128)}, u32[]{:S(2)}) copy-start(f32[1,32,8]{1,2,0:T(8,128)} %param.27) | copy-start | bytes 3076
  550.7 51.0 %all-to-all-start.1 = ((bf16[128,2,1024]{2,1,0:T(2,128)(2,1)}), bf16[128,2,1024]{2,1,0:T(2,128)(2,1)S(1)}, u32[]{:S(2)}, u32[]{:S(2)}) async-start(bf16[128,2,1024]{2,1,0:T(2,128)(2,1)} %reshape.363), calls=%async_computation.1 | async-start | bytes 1048576 | tf_op jit(solution)/shard_map/all_to_all | solution.py:216
  604.3 9.0 %all-to-all-start.2 = ((f32[32,4,256]{2,0,1:T(8,128)}), f32[32,4,256]{2,0,1:T(8,128)S(1)}, u32[]{:S(2)}, u32[]{:S(2)}) async-start(f32[32,4,256]{2,0,1:T(8,128)} %bitcast.191), calls=%async_computation.2 | async-start | bytes 262144 | tf_op jit(solution)/shard_map/all_to_all | solution.py:230
  613.3 3.4 collective-permute-start.1
Sparse Core Ops, SparseCore 0:
  373.0 56.1 all-gather.4
  431.3 40.4 all-gather.6
  473.9 38.6 all-gather.8
  514.5 32.7 all-gather.10
where the time goes:
time: 629 us; the launch traced here: 627 us
  waiting for transfers between devices  236 us (38%)
  starting transfers between devices  194 us (31%)
  other arithmetic  96.7 us (15%)
  matrix products  62.5 us (10%)
  local copies, waits for them, and re-layouts  21.8 us (3%)
  between operations  14.8 us (2%)
    ppermute x32, starting transfers between devices, passed_along(): return lax.ppermute(x, axis, pairs)  155 us
    another operation x4, other arithmetic, lower_solve(): lax.linalg.triangular_solve(unit_lower, right_side, left_side=True, lower...  79.4 us
    ppermute x32, waiting for transfers between devices, passed_along(): return lax.ppermute(x, axis, pairs)  62.4 us
    all_gather x1, waiting for transfers between devices, shards(): gathered = lax.all_gather(head_rows, 'coarse', axis=1, tiled=True)  46.6 us
    all_gather x1, waiting for transfers between devices, shards(): lax.all_gather(expert_up, 'coarse', axis=1, tiled=True)  39.3 us
    all_to_all x1, waiting for transfers between devices, shards(): lax.all_to_all(expert_value, ('seq', 'exp'), split_axis=0, concat_axis=0,...  33.3 us
    all_gather x1, waiting for transfers between devices, shards(): lax.all_gather(expert_down, 'coarse', axis=2, tiled=True)  31.4 us
    all_to_all x1, starting transfers between devices, shards(): lax.all_to_all(expert_value, ('seq', 'exp'), split_axis=0, concat_axis=0,...  17.5 us
  transfers between devices with their start and end apart: 39, of which 38 were waited for; matrix products, arithmetic and copies ran while one was open for 3% of the time, Pallas kernels for 0%

commit v1 on v0

v1 whole, which is shorter than its diff:
```python
import functools

import jax
import jax.numpy as jnp
from jax import lax
from jax.experimental import pallas as pl
from jax.experimental.pallas import tpu as pltpu
from jax.sharding import PartitionSpec as P

f32 = jnp.float32
bf16 = jnp.bfloat16
HALF = 256
GROUP = 4
VMEM_LIMIT = 48 * 1024 * 1024


def params():
    return pltpu.CompilerParams(vmem_limit_bytes=VMEM_LIMIT)


def whole(count):
    return [pl.BlockSpec(memory_space=pltpu.VMEM)] * count


def mm(a, b, dims=((1,), (0,))):
    return lax.dot_general(a, b, (dims, ((), ())), preferred_element_type=f32)


def split(x):
    high = x.astype(bf16)
    return high, (x - high.astype(f32)).astype(bf16)


def mm3(a, b, dims=((1,), (0,))):
    (ah, al), (bh, bl) = a, b
    return mm(ah, bh, dims) + (mm(ah, bl, dims) + mm(al, bh, dims))


def iota(shape, dim):
    return lax.broadcasted_iota(jnp.int32, shape, dim)


def as_row(column):
    size = column.shape[0]
    eye = iota((size, size), 0) == iota((size, size), 1)
    return jnp.sum(jnp.where(eye, column, 0.0), axis=0, keepdims=True)


def delta_kernel(
    x_ref, gain_ref, w_ref, gw_ref, rate_ref, bias_ref, ab_ref, q_ref, k_ref, sol_ref, cum_ref, low_h, low_l, inv
):
    rows = x_ref.shape[0]
    dim = HALF // 2
    x = x_ref[...].astype(f32)
    normed = (x * lax.rsqrt(jnp.mean(x * x, -1, keepdims=True) + 1e-05) * gain_ref[...]).astype(bf16)
    decay_in = mm(normed, gw_ref[0])
    write_in = mm(normed, gw_ref[1])
    write = jax.nn.sigmoid(write_in + bias_ref[...])
    soft = jnp.maximum(decay_in, 0.0) + jnp.log1p(jnp.exp(-jnp.abs(decay_in)))
    log_decay = -rate_ref[...] * soft
    tri = jnp.where(iota((rows, rows), 0) >= iota((rows, rows), 1), 1.0, 0.0).astype(bf16)
    part_h, rest = log_decay.astype(bf16), None
    rest = log_decay - part_h.astype(f32)
    part_m = rest.astype(bf16)
    part_l = (rest - part_m.astype(f32)).astype(bf16)
    cum = mm(tri, part_h) + (mm(tri, part_m) + mm(tri, part_l))
    cum_ref[...] = cum

    def act(index):
        value = mm(normed, w_ref[index])
        return value / (1.0 + jnp.exp(-value))

    q_all, k_all, v_all = act(0), act(1), act(2)
    strict = iota((HALF, HALF), 0) > iota((HALF, HALF), 1)
    keep = []
    for head in range(2):
        cols = slice(head * dim, (head + 1) * dim)
        q, k, v = q_all[:, cols], k_all[:, cols], v_all[:, cols]
        q = q * lax.rsqrt(jnp.sum(q * q, -1, keepdims=True) + 1e-06)
        k = k * lax.rsqrt(jnp.sum(k * k, -1, keepdims=True) + 1e-06)
        q_ref[:, cols] = q
        k_ref[:, cols] = k
        cum_col = cum[:, head : head + 1]
        cum_row = as_row(cum_col)
        beta = write[:, head : head + 1]
        kh, kl = split(k)
        cross = None
        for i, j in ((0, 0), (1, 1), (1, 0)):
            ri, rj = slice(i * HALF, (i + 1) * HALF), slice(j * HALF, (j + 1) * HALF)
            gram = mm3((kh[ri], kl[ri]), (kh[rj], kl[rj]), ((1,), (1,)))
            decay = jnp.exp(jnp.minimum(cum_col[ri] - cum_row[:, rj], 0.0))
            low = beta[ri] * decay * gram
            if i == j:
                low = jnp.where(strict, low, 0.0)
                low_h[2 * head + i], low_l[2 * head + i] = split(low)
                first = (iota((HALF, HALF), 0) >> 1) == (iota((HALF, HALF), 1) >> 1)
                eye = jnp.where(iota((HALF, HALF), 0) == iota((HALF, HALF), 1), 1.0, 0.0)
                inv[2 * head + i] = eye - jnp.where(first, low, 0.0)
            else:
                cross = split(low)
        right = jnp.concatenate([(beta * jnp.exp(cum_col)) * k, beta * v], axis=1)
        last = cum_col[rows - 1 : rows]
        keep.append((cross, right, k * jnp.exp(last - cum_col), jnp.exp(last)))

    def level(step, carry):
        r, c = iota((HALF, HALF), 0), iota((HALF, HALF), 1)
        above = ((r >> (step + 1)) == (c >> (step + 1))) & ((r >> step) > (c >> step))
        for m in range(4):
            t = inv[m]
            parts = split(t)
            zero = jnp.zeros((HALF, HALF), bf16)
            off = (jnp.where(above, low_h[m], zero), jnp.where(above, low_l[m], zero))
            inner = mm3(off, parts)
            inv[m] = t - mm3(parts, split(inner))
        return carry

    lax.fori_loop(1, 8, level, 0)
    for head in range(2):
        cross, right, k_end, scale = keep[head]
        first = mm3(split(inv[2 * head]), split(right[:HALF]))
        second = right[HALF:] - mm3(cross, split(first))
        second = mm3(split(inv[2 * head + 1]), split(second))
        solved = jnp.concatenate([first, second], axis=0)
        sol_ref[head] = solved
        ends = mm3(split(k_end), split(solved), ((0,), (0,)))
        eye = jnp.where(iota((dim, dim), 0) == iota((dim, dim), 1), 1.0, 0.0)
        ab_ref[head] = jnp.concatenate([scale * eye - ends[:, :dim], ends[:, dim:]], axis=1)


def local_kernel(q_ref, k_ref, sol_ref, cum_ref, map_ref, out_ref):
    dim = HALF // 2
    causal = iota((HALF, HALF), 0) >= iota((HALF, HALF), 1)
    for head in range(2):
        cols = slice(head * dim, (head + 1) * dim)
        q, k = q_ref[:, cols], k_ref[:, cols]
        cum_col = cum_ref[:, head : head + 1]
        cum_row = as_row(cum_col)
        (qh, ql), (kh, kl) = split(q), split(k)
        sh, sl = split(sol_ref[head])
        grown = jnp.exp(cum_col) * q
        for i in range(2):
            ri = slice(i * HALF, (i + 1) * HALF)
            total = None
            for j in range(i + 1):
                rj = slice(j * HALF, (j + 1) * HALF)
                attend = mm3((qh[ri], ql[ri]), (kh[rj], kl[rj]), ((1,), (1,)))
                attend = attend * jnp.exp(jnp.minimum(cum_col[ri] - cum_row[:, rj], 0.0))
                if i == j:
                    attend = jnp.where(causal, attend, 0.0)
                term = mm3(split(attend), (sh[rj], sl[rj]))
                total = term if total is None else total + term
            map_ref[head, ri] = grown[ri] - total[:, :dim]
            out_ref[head, ri] = total[:, dim:]


def compose(late, early):
    dim = late.shape[0]
    both = mm3(split(late[:, :dim]), split(early))
    return jnp.concatenate([both[:, :dim], both[:, dim:] + late[:, dim:]], axis=1)


def pair_kernel(core_ref, own_ref, got_ref, msg_ref, first_ref):
    dim = HALF // 2
    lead = core_ref[0] == 0
    own, got = own_ref[...], got_ref[...]
    early, late = jnp.where(lead, own, got), jnp.where(lead, got, own)
    first_ref[...] = early
    both = compose(late, early)
    eye = jnp.where(iota((dim, HALF), 0) == iota((dim, HALF), 1), 1.0, 0.0)
    msg_ref[...] = (both - eye).astype(bf16)


def group_kernel(place_ref, got_ref, before_ref, total_ref):
    dim = HALF // 2
    eye = jnp.where(iota((dim, HALF), 0) == iota((dim, HALF), 1), 1.0, 0.0)
    place = place_ref[0]
    running = eye
    before = eye
    for chip in range(GROUP):
        item = got_ref[chip].astype(f32) + eye
        running = item if chip == 0 else compose(item, running)
        if chip + 1 < GROUP:
            before = jnp.where(place == chip + 1, running, before)
    before_ref[...] = before
    total_ref[...] = running


def hop_kernel(total_ref, state_ref, out_ref):
    dim = HALF // 2
    moved = mm3(split(total_ref[:, :dim]), split(state_ref[...].astype(f32)))
    out_ref[...] = (moved + total_ref[:, dim:]).astype(bf16)


def enter_kernel(core_ref, before_ref, first_ref, state_ref, keep_ref, send_ref):
    dim = HALF // 2
    state = mm3(split(before_ref[:, :dim]), split(state_ref[...].astype(f32))) + before_ref[:, dim:]
    after = mm3(split(first_ref[:, :dim]), split(state)) + first_ref[:, dim:]
    lead = core_ref[0] == 0
    keep_ref[...] = jnp.where(lead, state, after)
    send_ref[...] = jnp.where(lead, after, state)


def finish_kernel(
    where_ref, map_ref, out_ref, keep_ref, got_ref, x_ref, gain_ref, mask_ref, rank_ref, hidden_ref, picked_ref
):
    dim = HALF // 2
    lead = where_ref[1] == 0
    keep, got = keep_ref[...], got_ref[...]
    states = (jnp.where(lead, keep, got), jnp.where(lead, got, keep))
    parts = []
    for head in range(2):
        out = out_ref[head] + mm3(split(map_ref[head]), split(states[head]))
        norm = out * lax.rsqrt(jnp.mean(out * out, -1, keepdims=True) + 1e-06)
        parts.append((norm * gain_ref[:, head * dim : (head + 1) * dim]).astype(bf16))
    normed = jnp.concatenate(parts, axis=1)
    hidden = (x_ref[...].astype(f32) + normed.astype(f32)).astype(bf16)
    hidden_ref[...] = hidden
    slots, rows = picked_ref.shape[0], hidden.shape[0]
    chosen = (iota((slots, rows), 0) == rank_ref[...]) & (mask_ref[...] == 1)
    picked_ref[...] = mm(jnp.where(chosen, 1.0, 0.0).astype(bf16), hidden).astype(bf16)


def route_kernel(where_ref, mask_ref, pick_ref, gate_ref, rank_ref, take_ref, weigh_ref):
    rows = mask_ref.shape[1]
    slots, top = pick_ref.shape
    total = take_ref.shape[1]
    mask = mask_ref[...]
    tri = jnp.where(iota((rows, rows), 0) <= iota((rows, rows), 1), 1.0, 0.0).astype(bf16)
    wide = jnp.broadcast_to(mask.astype(f32), (16, rows)).astype(bf16)
    rank_ref[...] = mm(wide, tri)[:1].astype(jnp.int32) - 1
    live = where_ref[0] * slots + iota((slots, total), 0) < jnp.sum(mask)
    column = iota((slots, total), 1)
    hit = jnp.zeros((slots, total), f32)
    weight = jnp.zeros((slots, total), f32)
    for pick in range(top):
        same = ((column >> 1) == pick_ref[:, pick : pick + 1]) & live
        hit = hit + jnp.where(same, 1.0, 0.0)
        weight = weight + jnp.where(same, gate_ref[:, pick : pick + 1], 0.0)
    earlier = jnp.where(iota((slots, slots), 0) > iota((slots, slots), 1), 1.0, 0.0).astype(bf16)
    arrival = mm(earlier, hit.astype(bf16)).astype(jnp.int32)
    here = (hit > 0.0) & (arrival == (column & 1))
    take_ref[...] = jnp.where(here, 1.0, 0.0).astype(bf16)
    weigh_ref[...] = jnp.where(here, weight, 0.0)


def dispatch_kernel(take_ref, got_ref, out_ref):
    take = take_ref[...]
    width = got_ref.shape[2]
    for part in range(got_ref.shape[0]):
        out_ref[:, part * width : (part + 1) * width] = mm(take, got_ref[part], ((0,), (0,))).astype(bf16)


def expert_kernel(rows_ref, weight_ref, ext_ref, out_ref):
    rows = rows_ref[...]
    depth = rows.shape[1]
    ext = jnp.broadcast_to(ext_ref[...].astype(f32), (16, depth)).astype(bf16)
    hidden = weight_ref.shape[0] // GROUP

    def part(start):
        cols = slice(start, start + hidden)
        offset = mm(ext, weight_ref[depth:, cols])[:1]
        return mm(rows, weight_ref[:depth, cols]) + offset

    gate, up = part(0), part(hidden)
    act = (gate / (1.0 + jnp.exp(-gate)) * up).astype(bf16)
    for c in range(GROUP):
        down = weight_ref[c * hidden : (c + 1) * hidden, 2 * hidden :]
        width = down.shape[1]
        out_ref[:, c * width : (c + 1) * width] = mm(act, down).astype(bf16)


def combine_kernel(weigh_ref, back_ref, out_ref):
    wh, wl = split(weigh_ref[...])
    width = out_ref.shape[2]
    for part in range(out_ref.shape[0]):
        back = back_ref[:, part * width : (part + 1) * width]
        out_ref[part] = mm(wh, back) + mm(wl, back)


def spread_kernel(hidden_ref, rank_ref, stretch_ref, prev_ref, out_ref):
    rows, slots = hidden_ref.shape[0], stretch_ref.shape[0]
    rank = rank_ref[...]
    chosen = jnp.where(iota((slots, rows), 0) == rank, 1.0, 0.0).astype(bf16)
    before = jnp.where(rank < 0, 1.0, 0.0)
    sh, sl = split(stretch_ref[...])
    spread = mm(chosen, sh, ((0,), (0,))) + mm(chosen, sl, ((0,), (0,)))
    size = rows
    eye = iota((size, size), 0) == iota((size, size), 1)
    before_col = jnp.sum(jnp.where(eye, before, 0.0), axis=1, keepdims=True)
    spread = jnp.where(before_col > 0.0, prev_ref[...], spread)
    out_ref[...] = (hidden_ref[...].astype(f32) + spread).astype(bf16)


def sds(shape, dtype):
    return jax.ShapeDtypeStruct(shape, dtype)


def call(kernel, outs, args, scalars=0, scratch=(), flops=10**8):
    smem = [pl.BlockSpec(memory_space=pltpu.SMEM)] * scalars
    return pl.pallas_call(
        kernel,
        out_shape=outs,
        in_specs=smem + whole(len(args) - scalars),
        out_specs=jax.tree.map(lambda _: pl.BlockSpec(memory_space=pltpu.VMEM), outs),
        scratch_shapes=list(scratch),
        compiler_params=params(),
        cost_estimate=pl.CostEstimate(flops=flops, bytes_accessed=10**6, transcendentals=0),
    )(*args)


def shards(
    bytes_in,
    norm_gain,
    qkv_weight,
    gate_weight_enc,
    decay_rate,
    write_bias,
    head_gain,
    boundaries,
    picks,
    pick_gates,
    extension,
    expert_gate,
    expert_up,
    expert_down,
):
    x = bytes_in[0]
    rows, width = x.shape
    dim = HALF // 2
    seq = lax.axis_index("seq")
    coarse = lax.axis_index("coarse")
    seq_total = lax.axis_size("seq")
    core = (seq % 2).astype(jnp.int32)
    place = ((seq // 2) % GROUP).astype(jnp.int32)
    local_slots = picks.shape[1]
    slot_total = local_slots * GROUP
    pair_total = local_slots * picks.shape[2]

    weights = jnp.concatenate([expert_gate[0], expert_up[0], expert_down[0]], axis=1)
    weights = lax.all_gather(weights, "coarse", axis=0, tiled=True)

    ab, q, k, solved, cum = call(
        delta_kernel,
        (
            sds((2, dim, HALF), f32),
            sds((rows, HALF), f32),
            sds((rows, HALF), f32),
            sds((2, rows, HALF), f32),
            sds((rows, 2), f32),
        ),
        (x, norm_gain[None], qkv_weight, gate_weight_enc, decay_rate[None], write_bias[None]),
        scratch=(
            pltpu.VMEM((4, HALF, HALF), bf16),
            pltpu.VMEM((4, HALF, HALF), bf16),
            pltpu.VMEM((4, HALF, HALF), f32),
        ),
        flops=2 * 10**9,
    )

    swap = [(i, i ^ 1) for i in range(seq_total)]
    own = lax.dynamic_index_in_dim(ab, core, 0, keepdims=False)
    give = lax.dynamic_index_in_dim(ab, 1 - core, 0, keepdims=False)
    got = lax.ppermute(give, "seq", swap)
    query_map, local_out = call(
        local_kernel,
        (sds((2, rows, dim), f32), sds((2, rows, dim), f32)),
        (q, k, solved, cum),
        flops=2 * 10**9,
    )
    spots = jnp.stack([coarse.astype(jnp.int32), core])
    rank, take, weigh = call(
        route_kernel,
        (sds((1, rows), jnp.int32), sds((local_slots, pair_total), bf16), sds((local_slots, pair_total), f32)),
        (spots, boundaries, picks[0], pick_gates[0]),
        scalars=1,
    )
    message, first = call(
        pair_kernel, (sds((dim, HALF), bf16), sds((dim, HALF), f32)), (core[None], own, got), scalars=1
    )
    stride = 2 * GROUP
    groups = [
        [stride * g + 2 * i + c for i in range(GROUP)] for g in range(seq_total // stride) for c in range(2)
    ]
    sent = jnp.broadcast_to(message[None], (GROUP, dim, HALF))
    chips = lax.all_to_all(sent, "seq", split_axis=0, concat_axis=0, tiled=True, axis_index_groups=groups)
    before, total = call(
        group_kernel, (sds((dim, HALF), f32), sds((dim, HALF), f32)), (place[None], chips), scalars=1
    )
    state = jnp.zeros((dim, dim), bf16)
    for hop in range(seq_total // stride - 1):
        if hop == 0:
            outgoing = total[:, dim:].astype(bf16)
        else:
            outgoing = call(hop_kernel, sds((dim, dim), bf16), (total, state))
        pairs = [(stride * hop + i, stride * (hop + 1) + i) for i in range(stride)]
        state = state + lax.ppermute(outgoing, "seq", pairs)
    keep, send = call(
        enter_kernel,
        (sds((dim, dim), f32), sds((dim, dim), f32)),
        (core[None], before, first, state),
        scalars=1,
    )
    other = lax.ppermute(send, "seq", swap)

    x_share = lax.dynamic_slice_in_dim(x, coarse * HALF, HALF, 1)
    hidden, picked = call(
        finish_kernel,
        (sds((rows, HALF), bf16), sds((slot_total, HALF), bf16)),
        (spots, query_map, local_out, keep, other, x_share, head_gain[None], boundaries, rank),
        scalars=1,
    )
    picked = lax.all_to_all(
        picked.reshape(GROUP, local_slots, HALF), "coarse", split_axis=0, concat_axis=0, tiled=True
    )
    outgoing = call(dispatch_kernel, sds((pair_total, width), bf16), (take, picked))
    experts = lax.axis_size(("seq", "exp"))
    capacity = pair_total // experts
    received = lax.all_to_all(
        outgoing.reshape(experts, capacity, width), ("seq", "exp"), split_axis=0, concat_axis=0, tiled=True
    )
    value = call(
        expert_kernel,
        sds((pair_total, width), bf16),
        (received.reshape(pair_total, width), weights, extension[None]),
    )
    returned = lax.all_to_all(
        value.reshape(experts, capacity, width), ("seq", "exp"), split_axis=0, concat_axis=0, tiled=True
    )
    stretch = call(
        combine_kernel,
        sds((GROUP, local_slots, HALF), f32),
        (weigh, returned.reshape(pair_total, width)),
    )
    stretch = lax.all_to_all(stretch, "coarse", split_axis=0, concat_axis=0, tiled=True)
    stretch = stretch.reshape(slot_total, HALF)
    last = lax.dynamic_slice_in_dim(stretch, rank[0, rows - 1], 1, 0)
    previous = lax.ppermute(last, "seq", [(i, i + 1) for i in range(seq_total - 1)])
    mixed = call(spread_kernel, sds((rows, HALF), bf16), (hidden, rank, stretch, previous))
    return mixed[None]


def solution(mesh):
    placed = (
        P("exp", "seq", None),
        P(),
        P(None, None, "coarse"),
        P(None, None, "coarse"),
        P("coarse"),
        P("coarse"),
        P("coarse"),
        P("exp", "seq"),
        P("exp", ("seq", "coarse"), None),
        P("exp", ("seq", "coarse"), None),
        P(),
        P(("seq", "exp"), "coarse", None),
        P(("seq", "exp"), "coarse", None),
        P(("seq", "exp"), None, "coarse"),
    )
    return jax.shard_map(
        shards, mesh=mesh, in_specs=placed, out_specs=P("exp", "seq", "coarse"), check_vma=False
    )
```

time: 629 us -> 197 us (0.31)
  waiting for transfers between devices: 236 us -> 47.1 us
  starting transfers between devices: 194 us -> 48.1 us
  other arithmetic: 96.7 us -> 2.62 us
  matrix products: 62.5 us -> 0 us
  blocking collectives: 0 us -> 48.9 us
  Pallas kernels: 0 us -> 26 us
  local copies, waits for them, and re-layouts: 21.8 us -> 8.19 us
    all_gather x4 -> x1, waiting for transfers between devices: 134 us -> 0.02 us  [shards(): weights = lax.all_gather(weights, 'coarse', axis=0, tiled=True)]
    ppermute x32 -> x6, starting transfers between devices: 155 us -> 23.1 us  [the longest x1 8.79 us: shards(): got = lax.ppermute(give, 'seq', swap)]
    another operation x9 -> x1, other arithmetic: 80.6 us -> 0.08 us  [shards(): spots = jnp.stack([coarse.astype(jnp.int32), core])]
    ppermute x32 -> x6, waiting for transfers between devices: 62.4 us -> 3.51 us  [the longest x3 1.01 us: shards(): state = state + lax.ppermute(outgoing, 'seq', pairs)]
    dot_general x72 -> x0, matrix products: 58.1 us -> none  [the longest x8 10.1 us: advance(): jnp.einsum('hsd,hse->hde', decayed_b, update, precision=precise)]
    all_to_all x0 -> x2, blocking collectives: none -> 48.9 us  [the longest x1 39.7 us: shards(): lax.all_to_all(value.reshape(experts, capacity, width), ('seq', 'exp'), s...]
    pallas_call x0 -> x13, Pallas kernels: none -> 26 us  [call(): pl.pallas_call(kernel, out_shape=outs, in_specs=smem + whole(len(args) -...]
    all_to_all x3, starting transfers between devices: 38.7 us -> 24.9 us  [the longest x1 18.2 us: shards(): lax.all_to_all(outgoing.reshape(experts, capacity, width), ('seq', 'exp')...]
  transfers between devices with their start and end apart: 39 -> 10, of which waited for: 38 -> 7; matrix products, arithmetic and copies ran while one was open for 3% -> 2% of each run, Pallas kernels for 0% -> 10%
where the time goes in v1:
time: 197 us
  blocking collectives  48.9 us (25%)
  starting transfers between devices  48.1 us (24%)
  waiting for transfers between devices  47.1 us (24%)
  Pallas kernels  26 us (13%)
  between operations  15.8 us (8%)
  local copies, waits for them, and re-layouts  8.19 us (4%)
  other arithmetic  2.62 us (1%)
    all_to_all x1, blocking collectives, shards(): lax.all_to_all(value.reshape(experts, capacity, width), ('seq', 'exp'), s...  39.7 us
    all_to_all x1, waiting for transfers between devices, shards(): lax.all_to_all(outgoing.reshape(experts, capacity, width), ('seq', 'exp')...  33.5 us
    pallas_call x13, Pallas kernels, call(): pl.pallas_call(kernel, out_shape=outs, in_specs=smem + whole(len(args) -...  26 us
    all_to_all x1, starting transfers between devices, shards(): lax.all_to_all(outgoing.reshape(experts, capacity, width), ('seq', 'exp')...  18.2 us
    all_to_all x1, blocking collectives, shards(): lax.all_to_all(picked.reshape(GROUP, local_slots, HALF), 'coarse', split_...  9.16 us
    ppermute x1, starting transfers between devices, shards(): got = lax.ppermute(give, 'seq', swap)  8.79 us
    all_to_all x1, waiting for transfers between devices, shards(): lax.all_to_all(sent, 'seq', split_axis=0, concat_axis=0, tiled=True, axis...  7.77 us
    ppermute x3, starting transfers between devices, shards(): state = state + lax.ppermute(outgoing, 'seq', pairs)  6.99 us
  transfers between devices with their start and end apart: 10, of which 7 were waited for; matrix products, arithmetic and copies ran while one was open for 2% of the time, Pallas kernels for 10%

profile of v1, /device:TPU:1, one launch (start us, length us, event | category | flops | bytes accessed | tf_op | source)
XLA Modules:
  0.0 196.6 jit_solution(1953367943939278793)
XLA Ops:
  6.5 0.0 all-gather.2.cloned.1.call-start
  6.6 2.5 %pad_maximum_fusion = bf16[512,1280]{1,0:T(8,128)(2,1)} fusion(bf16[512,256]{1,0:T(8,128)(2,1)} %bitcast.35, bf16[512,512]{1,0:T(8,128)(2,1)} %bitcast.33, bf16[512,512]{1,0:T(8,128)(2,1)} %bitcast.34), kind=kLoop, calls=%fused_computation | loop fusion | flops 3932160 | bytes 2621440 | tf_op jit(solution)/shard_map/concatenate | solution.py:339
  9.1 0.0 all-gather.2.cloned.1.call-update
  9.2 0.0 copy-done.11
  9.2 0.3 copy.15.gw_ref
  9.5 0.0 copy-done
  9.5 0.0 copy-done.4
  9.5 0.0 copy-done.5
  9.5 0.0 copy-done.6
  9.5 0.0 copy-start.3
  9.5 1.4 copy-done.3
  10.9 14.5 %shard_map.136 = (f32[2,128,256]{2,1,0:T(8,128)S(1)}, f32[512,256]{1,0:T(8,128)S(1)}, f32[512,256]{1,0:T(8,128)S(1)}, f32[2,512,256]{2,1,0:T(8,128)S(1)}, f32[512,2]{1,0:T(8,128)S(1)}) custom-call(bf16[512,1024]{1,0:T(8,128)(2,1)S(1)} %bitcast.25, f32[1,1024]{1,0:T(1,128)S(1)} %bitcast.30, bf16[3,1024,256]{2,1,0:T(8,128)(2,1)S(1)} %copy-done.3, ...), custom_call_target="tpu_custom_call" | custom-call | flops 2000000000 | bytes 1000000 | tf_op jit(solution)/shard_map/pallas_call | solution.py:300
  25.5 1.0 copy-done.7
  26.5 8.8 %collective-permute-start = (f32[128,256]{1,0:T(8,128)S(1)}, f32[128,256]{1,0:T(8,128)S(1)}, u32[]{:S(2)}, u32[]{:S(2)}) collective-permute-start(f32[128,256]{1,0:T(8,128)S(1)} %get-tuple-element.41), channel_id=1, source_target_pairs={{0,16},{16,0},{32,48},{48,32},{64,80},{80,64},{96,112},{112,96},{1... | collective-permute-start | bytes 393224 | tf_op jit(solution)/shard_map/ppermute | solution.py:363
  35.3 1.0 collective-permute-done.got_ref
  36.2 0.2 shard_map.138
  36.4 0.0 copy-done.9
  36.5 0.7 broadcast_in_dim.33
  37.2 3.4 %all-to-all-start = ((bf16[4,128,256]{2,1,0:T(8,128)(2,1)}), bf16[4,128,256]{2,1,0:T(8,128)(2,1)S(1)}, u32[]{:S(2)}, u32[]{:S(2)}) async-start(bf16[4,128,256]{2,1,0:T(8,128)(2,1)} %broadcast_in_dim.33), calls=%async_computation | async-start | bytes 524288 | tf_op jit(solution)/shard_map/all_to_all | solution.py:385
  40.6 7.8 %all-to-all-done.got_ref = bf16[4,128,256]{2,1,0:T(8,128)(2,1)S(1)} async-done(((bf16[4,128,256]{2,1,0:T(8,128)(2,1)}), bf16[4,128,256]{2,1,0:T(8,128)(2,1)S(1)}, u32[]{:S(2)}, u32[]{:S(2)}) %all-to-all-start) | async-done | bytes 262176 | tf_op jit(solution)/shard_map/all_to_all | solution.py:385
  48.4 0.6 shard_map.139
  49.1 5.7 %collective-permute-start.1 = (bf16[128,128]{1,0:T(8,128)(2,1)S(1)}, bf16[128,128]{1,0:T(8,128)(2,1)S(1)}, u32[]{:S(2)}, u32[]{:S(2)}) collective-permute-start(bf16[128,128]{1,0:T(8,128)(2,1)S(1)} %slice.11), channel_id=1, source_target_pairs={{0,128},{16,144},{32,160},{48,176},{64,192},{80,208},{96,224},{112... | collective-permute-start | bytes 98312 | tf_op jit(solution)/shard_map/ppermute | solution.py:396
  54.7 1.0 collective-permute-done.1.state_ref
  55.7 0.2 shard_map.140
  55.9 0.7 collective-permute-start.2
  56.6 0.0 copy-start.8
  56.6 1.2 copy-done.8
  57.8 1.0 copy-done.10
  58.9 1.7 shard_map.137
  60.5 0.0 collective-permute-done.2
  60.6 0.2 shard_map.141
  60.8 0.7 collective-permute-start.3
  61.4 0.1 pad_add_fusion.where_ref
  61.5 0.0 copy-done.12
  61.5 0.1 copy.16
  61.6 0.0 copy-done.13
  61.6 0.1 copy.17
  61.7 0.0 copy-done.1
  61.7 0.9 shard_map.143
  62.5 0.0 collective-permute-done.3
  62.6 0.0 copy-start.14
  62.6 0.4 shard_map.142
  62.9 4.8 %collective-permute-start.4 = (f32[128,128]{1,0:T(8,128)S(1)}, f32[128,128]{1,0:T(8,128)S(1)}, u32[]{:S(2)}, u32[]{:S(2)}) collective-permute-start(f32[128,128]{1,0:T(8,128)S(1)} %get-tuple-element.35), channel_id=1, source_target_pairs={{0,16},{16,0},{32,48},{48,32},{64,80},{80,64},{96,112},{112,96},{1... | collective-permute-start | bytes 196616 | tf_op jit(solution)/shard_map/ppermute | solution.py:403
  67.8 0.8 collective-permute-done.4.got_ref
  68.7 1.2 shard_map.144
  69.9 9.2 %all_to_all.25.got_ref = bf16[4,32,256]{2,1,0:T(8,128)(2,1)S(1)} all-to-all(bf16[4,32,256]{2,1,0:T(8,128)(2,1)S(1)} %bitcast.26), channel_id=1, replica_groups=mesh['seq'=32,'coarse'=4,'exp'=4] {'coarse'}, dimensions={0} | all-to-all | bytes 131072 | tf_op jit(solution)/shard_map/all_to_all | solution.py:412
  79.1 0.3 shard_map.145
  79.4 1.0 reshape.21
  80.4 18.2 %all-to-all-start.2 = ((bf16[128,2,1024]{2,1,0:T(2,128)(2,1)}), bf16[128,2,1024]{2,1,0:T(2,128)(2,1)S(1)}, u32[]{:S(2)}, u32[]{:S(2)}) async-start(bf16[128,2,1024]{2,1,0:T(2,128)(2,1)} %reshape.21), calls=%async_computation.2 | async-start | bytes 1048576 | tf_op jit(solution)/shard_map/all_to_all | solution.py:418
  98.6 0.0 copy-done.14
  98.6 33.5 %all-to-all-done.2 = bf16[128,2,1024]{2,1,0:T(2,128)(2,1)S(1)} async-done(((bf16[128,2,1024]{2,1,0:T(2,128)(2,1)}), bf16[128,2,1024]{2,1,0:T(2,128)(2,1)S(1)}, u32[]{:S(2)}, u32[]{:S(2)}) %all-to-all-start.2) | async-done | bytes 524320 | tf_op jit(solution)/shard_map/all_to_all | solution.py:418
  132.2 0.2 reshape.22.rows_ref
  132.4 0.0 all-gather.2.cloned.1.call-done.weight_ref
  132.4 3.8 %shard_map.146 = bf16[256,1024]{1,0:T(8,128)(2,1)S(1)} custom-call(bf16[256,1024]{1,0:T(8,128)(2,1)S(1)} %reshape.22.rows_ref, bf16[2048,1280]{1,0:T(8,128)(2,1)} %all-gather.2.cloned.1.call-done.weight_ref, bf16[1,1024]{1,0:T(2,128)(2,1)S(1)} %broadcast_in_dim.35.ext_ref), custom_call_target="tpu_custom_call" | custom-call | flops 100000000 | bytes 1000000 | tf_op jit(solution)/shard_map/pallas_call | solution.py:300
  136.2 0.2 reshape.23
  136.4 39.7 %all_to_all.26 = bf16[128,2,1024]{2,1,0:T(2,128)(2,1)S(1)} all-to-all(bf16[128,2,1024]{2,1,0:T(2,128)(2,1)S(1)} %reshape.23), channel_id=1, replica_groups=mesh['seq'=32,'coarse'=4,'exp'=4] {'seq','exp'}, dimensions={0} | all-to-all | bytes 1048576 | tf_op jit(solution)/shard_map/all_to_all | solution.py:426
  176.1 0.2 reshape.24.back_ref
  176.3 0.9 shard_map.147
  177.3 3.3 %all-to-all-start.4 = ((f32[4,32,256]{2,1,0:T(8,128)}), f32[4,32,256]{2,1,0:T(8,128)S(1)}, u32[]{:S(2)}, u32[]{:S(2)}) async-start(f32[4,32,256]{2,1,0:T(8,128)} %shard_map.147), calls=%async_computation.4 | async-start | bytes 262144 | tf_op jit(solution)/shard_map/all_to_all | solution.py:434
  180.6 0.6 slice.8
  183.3 2.3 %all-to-all-done.4 = f32[4,32,256]{2,1,0:T(8,128)S(1)} async-done(((f32[4,32,256]{2,1,0:T(8,128)}), f32[4,32,256]{2,1,0:T(8,128)S(1)}, u32[]{:S(2)}, u32[]{:S(2)}) %all-to-all-start.4) | async-done | bytes 131104 | tf_op jit(solution)/shard_map/all_to_all | solution.py:434
  185.6 2.5 %collective-permute-start.5 = (f32[1,256]{1,0:T(1,128)S(1)}, f32[1,256]{1,0:T(1,128)S(1)}, u32[]{:S(2)}, u32[]{:S(2)}) collective-permute-start(f32[1,256]{1,0:T(1,128)S(1)} %constant_dynamic-slice_fusion), channel_id=1, source_target_pairs={{0,16},{16,32},{32,48},{48,64},{64,80},{80,96},{96,112},{112,128},... | collective-permute-start | bytes 3080 | tf_op jit(solution)/shard_map/ppermute | solution.py:437
  188.0 0.7 collective-permute-done.5.prev_ref
  188.7 1.0 shard_map.148
  (20 shorter events, 0.1 us)
Async XLA Ops:
  6.5 2.6 %copy-start.11 = (bf16[2,1024,2]{1,2,0:T(2,128)(2,1)S(1)}, bf16[2,1024,2]{1,2,0:T(2,128)(2,1)}, u32[]{:S(2)}) copy-start(bf16[2,1024,2]{1,2,0:T(2,128)(2,1)} %param.17) | copy-start | bytes 24580
  6.5 3.0 %copy-start = (bf16[1,512,1024]{2,1,0:T(8,128)(2,1)S(1)}, bf16[1,512,1024]{2,1,0:T(8,128)(2,1)}, u32[]{:S(2)}) copy-start(bf16[1,512,1024]{2,1,0:T(8,128)(2,1)} %param.14) | copy-start | bytes 3145732
  6.5 3.0 %copy-start.4 = (f32[1024]{0:T(1024)S(1)}, f32[1024]{0:T(1024)}, u32[]{:S(2)}) copy-start(f32[1024]{0:T(1024)} %param.15) | copy-start | bytes 12292
  6.5 3.0 %copy-start.5 = (f32[2]{0:T(128)S(1)}, f32[2]{0:T(128)}, u32[]{:S(2)}) copy-start(f32[2]{0:T(128)} %param.18) | copy-start | bytes 28
  6.5 3.0 %copy-start.6 = (f32[2]{0:T(128)S(1)}, f32[2]{0:T(128)}, u32[]{:S(2)}) copy-start(f32[2]{0:T(128)} %param.19) | copy-start | bytes 28
  6.5 125.8 %all-gather.2.cloned.1.call-start = ((), (), s32[]{:S(2)}) async-start(), calls=%async_computation.5 | async-start | bytes 6553600 | tf_op jit(solution)/shard_map/all_gather | solution.py:340
  9.5 1.4 copy-start.3
  25.5 1.0 copy-start.7
  26.4 10.0 %copy-start.9 = (f32[512,256]{1,0:T(8,128)}, f32[512,256]{1,0:T(8,128)S(1)}, u32[]{:S(2)}) copy-start(f32[512,256]{1,0:T(8,128)S(1)} %get-tuple-element.24.k_ref) | copy-start | bytes 1572868
  26.5 9.8 %collective-permute-start = (f32[128,256]{1,0:T(8,128)S(1)}, f32[128,256]{1,0:T(8,128)S(1)}, u32[]{:S(2)}, u32[]{:S(2)}) collective-permute-start(f32[128,256]{1,0:T(8,128)S(1)} %get-tuple-element.41), channel_id=1, source_target_pairs={{0,16},{16,0},{32,48},{48,32},{64,80},{80,64},{96,112},{112,96},{1... | collective-permute-start | bytes 393224 | tf_op jit(solution)/shard_map/ppermute | solution.py:363
  37.2 11.2 %all-to-all-start = ((bf16[4,128,256]{2,1,0:T(8,128)(2,1)}), bf16[4,128,256]{2,1,0:T(8,128)(2,1)S(1)}, u32[]{:S(2)}, u32[]{:S(2)}) async-start(bf16[4,128,256]{2,1,0:T(8,128)(2,1)} %broadcast_in_dim.33), calls=%async_computation | async-start | bytes 524288 | tf_op jit(solution)/shard_map/all_to_all | solution.py:385
  49.1 6.7 %collective-permute-start.1 = (bf16[128,128]{1,0:T(8,128)(2,1)S(1)}, bf16[128,128]{1,0:T(8,128)(2,1)S(1)}, u32[]{:S(2)}, u32[]{:S(2)}) collective-permute-start(bf16[128,128]{1,0:T(8,128)(2,1)S(1)} %slice.11), channel_id=1, source_target_pairs={{0,128},{16,144},{32,160},{48,176},{64,192},{80,208},{96,224},{112... | collective-permute-start | bytes 98312 | tf_op jit(solution)/shard_map/ppermute | solution.py:396
  55.9 4.6 %collective-permute-start.2 = (bf16[128,128]{1,0:T(8,128)(2,1)S(1)}, bf16[128,128]{1,0:T(8,128)(2,1)S(1)}, u32[]{:S(2)}, u32[]{:S(2)}) collective-permute-start(bf16[128,128]{1,0:T(8,128)(2,1)S(1)} %shard_map.140), channel_id=1, source_target_pairs={{128,256},{144,272},{160,288},{176,304},{192,320},{208,336},{224,3... | collective-permute-start | bytes 98312 | tf_op jit(solution)/shard_map/ppermute | solution.py:396
  56.6 1.2 copy-start.8
  57.8 1.0 copy-start.10
  58.9 2.7 %copy-start.12 = (s32[1,32,8]{1,2,0:T(8,128)S(1)}, s32[1,32,8]{1,2,0:T(8,128)}, u32[]{:S(2)}) copy-start(s32[1,32,8]{1,2,0:T(8,128)} %param.22) | copy-start | bytes 3076
  58.9 2.7 %copy-start.13 = (f32[1,32,8]{1,2,0:T(8,128)S(1)}, f32[1,32,8]{1,2,0:T(8,128)}, u32[]{:S(2)}) copy-start(f32[1,32,8]{1,2,0:T(8,128)} %param.23) | copy-start | bytes 3076
  58.9 2.8 %copy-start.1 = (s32[1,512]{1,0:T(1,128)S(1)}, s32[1,512]{1,0:T(1,128)}, u32[]{:S(2)}) copy-start(s32[1,512]{1,0:T(1,128)} %mask_ref.3) | copy-start | bytes 6148
  58.9 9.8 %copy-start.2 = (f32[256]{0:T(256)S(1)}, f32[256]{0:T(256)}, u32[]{:S(2)}) copy-start(f32[256]{0:T(256)} %param.20) | copy-start | bytes 3076
  60.8 1.8 collective-permute-start.3
  62.6 36.0 %copy-start.14 = (bf16[1024]{0:T(1024)(128)(2,1)S(1)}, bf16[1024]{0:T(1024)(128)(2,1)}, u32[]{:S(2)}) copy-start(bf16[1024]{0:T(1024)(128)(2,1)} %param.24) | copy-start | bytes 6148
  62.9 5.7 %collective-permute-start.4 = (f32[128,128]{1,0:T(8,128)S(1)}, f32[128,128]{1,0:T(8,128)S(1)}, u32[]{:S(2)}, u32[]{:S(2)}) collective-permute-start(f32[128,128]{1,0:T(8,128)S(1)} %get-tuple-element.35), channel_id=1, source_target_pairs={{0,16},{16,0},{32,48},{48,32},{64,80},{80,64},{96,112},{112,96},{1... | collective-permute-start | bytes 196616 | tf_op jit(solution)/shard_map/ppermute | solution.py:403
  80.4 51.8 %all-to-all-start.2 = ((bf16[128,2,1024]{2,1,0:T(2,128)(2,1)}), bf16[128,2,1024]{2,1,0:T(2,128)(2,1)S(1)}, u32[]{:S(2)}, u32[]{:S(2)}) async-start(bf16[128,2,1024]{2,1,0:T(2,128)(2,1)} %reshape.21), calls=%async_computation.2 | async-start | bytes 1048576 | tf_op jit(solution)/shard_map/all_to_all | solution.py:418
  177.3 8.3 %all-to-all-start.4 = ((f32[4,32,256]{2,1,0:T(8,128)}), f32[4,32,256]{2,1,0:T(8,128)S(1)}, u32[]{:S(2)}, u32[]{:S(2)}) async-start(f32[4,32,256]{2,1,0:T(8,128)} %shard_map.147), calls=%async_computation.4 | async-start | bytes 262144 | tf_op jit(solution)/shard_map/all_to_all | solution.py:434
  185.6 3.2 %collective-permute-start.5 = (f32[1,256]{1,0:T(1,128)S(1)}, f32[1,256]{1,0:T(1,128)S(1)}, u32[]{:S(2)}, u32[]{:S(2)}) collective-permute-start(f32[1,256]{1,0:T(1,128)S(1)} %constant_dynamic-slice_fusion), channel_id=1, source_target_pairs={{0,16},{16,32},{32,48},{48,64},{64,80},{80,96},{96,112},{112,128},... | collective-permute-start | bytes 3080 | tf_op jit(solution)/shard_map/ppermute | solution.py:437
Sparse Core Ops, SparseCore 0:
  9.5 70.5 all-gather.1

commit v2 on v1

v2 whole, which is shorter than its diff:
```python
import jax
import jax.numpy as jnp
from jax import lax
from jax.experimental import pallas as pl
from jax.experimental.pallas import tpu as pltpu
from jax.sharding import PartitionSpec as P

f32 = jnp.float32
bf16 = jnp.bfloat16
HALF = 256
GROUP = 4


def mm(a, b, dims=((1,), (0,))):
    return lax.dot_general(a, b, (dims, ((), ())), preferred_element_type=f32)


def split(x):
    high = x.astype(bf16)
    return high, (x - high.astype(f32)).astype(bf16)


def mm3(a, b, dims=((1,), (0,))):
    (ah, al), (bh, bl) = a, b
    return mm(ah, bh, dims) + (mm(ah, bl, dims) + mm(al, bh, dims))


def iota(shape, dim):
    return lax.broadcasted_iota(jnp.int32, shape, dim)


def as_row(column):
    size = column.shape[0]
    eye = iota((size, size), 0) == iota((size, size), 1)
    return jnp.sum(jnp.where(eye, column, 0.0), axis=0, keepdims=True)


def delta_kernel(
    spots_ref,
    x_far,
    gain_far,
    w_far,
    gw_far,
    rate_far,
    bias_far,
    egate_far,
    eup_far,
    edown_far,
    own_ref,
    give_ref,
    q_ref,
    k_ref,
    sol_ref,
    cum_ref,
    share_ref,
    weights_ref,
    x_ref,
    gain_ref,
    w_ref,
    gw_ref,
    rate_ref,
    bias_ref,
    low,
    inv,
    sems,
):
    rows = x_ref.shape[0]
    dim = HALF // 2
    pairs = [(x_far, x_ref), (gain_far, gain_ref), (gw_far, gw_ref), (rate_far, rate_ref), (bias_far, bias_ref)]
    pairs.append((w_far, w_ref))
    start = 0
    for far in (egate_far, eup_far, edown_far):
        size = far.shape[2]
        pairs.append((far.at[0], weights_ref.at[:, pl.ds(start, size)]))
        start += size
    moves = [pltpu.make_async_copy(a, b, sems.at[n]) for n, (a, b) in enumerate(pairs)]
    for move in moves:
        move.start()
    for move in moves[:5]:
        move.wait()
    first = pl.multiple_of(spots_ref[1] * HALF, HALF)
    moves.append(pltpu.make_async_copy(x_ref.at[:, pl.ds(first, HALF)], share_ref, sems.at[9]))
    moves[9].start()

    x = x_ref[...].astype(f32)
    normed = (x * lax.rsqrt(jnp.mean(x * x, -1, keepdims=True) + 1e-05) * gain_ref[...]).astype(bf16)
    linear = mm(normed, jnp.concatenate([gw_ref[0], gw_ref[1]], axis=0), ((1,), (1,)))
    decay_in, write_in = linear[:, :2], linear[:, 2:]
    write = jax.nn.sigmoid(write_in + bias_ref[...])
    soft = jnp.maximum(decay_in, 0.0) + jnp.log1p(jnp.exp(-jnp.abs(decay_in)))
    log_decay = -rate_ref[...] * soft
    tri = jnp.where(iota((rows, rows), 0) >= iota((rows, rows), 1), 1.0, 0.0).astype(bf16)
    part_h = log_decay.astype(bf16)
    rest = log_decay - part_h.astype(f32)
    part_m = rest.astype(bf16)
    part_l = (rest - part_m.astype(f32)).astype(bf16)
    sums = mm(tri, jnp.concatenate([part_h, part_m, part_l], axis=1))
    cum = sums[:, 0:2] + (sums[:, 2:4] + sums[:, 4:6])
    cum_ref[...] = cum

    moves[5].wait()

    def act(index):
        value = mm(normed, w_ref[index])
        return value / (1.0 + jnp.exp(-value))

    q_all, k_all, v_all = act(0), act(1), act(2)
    strict = iota((HALF, HALF), 0) > iota((HALF, HALF), 1)
    pair = (iota((dim, dim), 0) >> 1) == (iota((dim, dim), 1) >> 1)
    eye = jnp.where(iota((dim, dim), 0) == iota((dim, dim), 1), 1.0, 0.0)
    keep = []
    for head in range(2):
        cols = slice(head * dim, (head + 1) * dim)
        q, k, v = q_all[:, cols], k_all[:, cols], v_all[:, cols]
        q = q * lax.rsqrt(jnp.sum(q * q, -1, keepdims=True) + 1e-06)
        k = k * lax.rsqrt(jnp.sum(k * k, -1, keepdims=True) + 1e-06)
        q_ref[:, cols] = q
        k_ref[:, cols] = k
        cum_col = cum[:, head : head + 1]
        cum_row = as_row(cum_col)
        beta = write[:, head : head + 1]
        kh, kl = split(k)
        deep = jnp.concatenate([kh, kl], axis=1)
        twice = jnp.concatenate([kh, kh], axis=1)
        cross = None
        inner = []
        for i, j in ((0, 0), (1, 1), (1, 0)):
            ri, rj = slice(i * HALF, (i + 1) * HALF), slice(j * HALF, (j + 1) * HALF)
            gram = mm(deep[ri], twice[rj], ((1,), (1,))) + mm(kh[ri], kl[rj], ((1,), (1,)))
            lower = beta[ri] * jnp.exp(jnp.minimum(cum_col[ri] - cum_row[:, rj], 0.0)) * gram
            if i == j:
                lower = jnp.where(strict, lower, 0.0)
                for sub in range(2):
                    rs = slice(sub * dim, (sub + 1) * dim)
                    block = 4 * head + 2 * i + sub
                    part = lower[rs, rs]
                    low[block] = jnp.concatenate(split(part), axis=1)
                    inv[block] = eye - jnp.where(pair, part, 0.0)
                inner.append(jnp.concatenate(split(lower[dim:, :dim]), axis=1))
            else:
                cross = split(lower)
        right = jnp.concatenate([(beta * jnp.exp(cum_col)) * k, beta * v], axis=1)
        last = cum_col[rows - 1 : rows]
        keep.append((cross, inner, right, k * jnp.exp(last - cum_col), jnp.exp(last)))

    def packed(left, block):
        wide = jnp.concatenate(split(block), axis=1)
        out = mm(left, jnp.concatenate([wide, wide], axis=0))
        return out[:, :dim] + out[:, dim:]

    def level(step, carry):
        r, c = iota((dim, HALF), 0), iota((dim, HALF), 1) & (dim - 1)
        above = ((r >> (step + 1)) == (c >> (step + 1))) & ((r >> step) > (c >> step))
        zero = jnp.zeros((dim, HALF), bf16)
        blocks = [inv[m] for m in range(8)]
        inside = [packed(jnp.where(above, low[m], zero), blocks[m]) for m in range(8)]
        for m in range(8):
            inv[m] = blocks[m] - packed(jnp.concatenate(split(blocks[m]), axis=1), inside[m])
        return carry

    lax.fori_loop(1, 7, level, 0)
    for head in range(2):
        cross, inner, right, k_end, scale = keep[head]
        full = []
        for i in range(2):
            top, bottom = inv[4 * head + 2 * i], inv[4 * head + 2 * i + 1]
            corner = packed(jnp.concatenate(split(bottom), axis=1), packed(inner[i], top))
            upper = jnp.concatenate([top, jnp.zeros_like(top)], axis=1)
            full.append(split(jnp.concatenate([upper, jnp.concatenate([-corner, bottom], axis=1)], axis=0)))
        first = mm3(full[0], split(right[:HALF]))
        second = right[HALF:] - mm3(cross, split(first))
        second = mm3(full[1], split(second))
        solved = jnp.concatenate([first, second], axis=0)
        sol_ref[head] = solved
        ends = mm3(split(k_end), split(solved), ((0,), (0,)))
        keep[head] = jnp.concatenate([scale * eye - ends[:, :dim], ends[:, dim:]], axis=1)
    lead = spots_ref[0] == 0
    own_ref[...] = jnp.where(lead, keep[0], keep[1])
    give_ref[...] = jnp.where(lead, keep[1], keep[0])
    for move in moves[6:]:
        move.wait()


def local_kernel(q_ref, k_ref, sol_ref, cum_ref, both_ref, token_ref):
    token_ref[...] = jnp.zeros_like(token_ref)
    dim = HALF // 2
    causal = iota((HALF, HALF), 0) >= iota((HALF, HALF), 1)
    for head in range(2):
        cols = slice(head * dim, (head + 1) * dim)
        q, k = q_ref[:, cols], k_ref[:, cols]
        cum_col = cum_ref[:, head : head + 1]
        cum_row = as_row(cum_col)
        (qh, ql), (kh, kl) = split(q), split(k)
        sh, sl = split(sol_ref[head])
        grown = jnp.exp(cum_col) * q
        for i in range(2):
            ri = slice(i * HALF, (i + 1) * HALF)
            total = None
            for j in range(i + 1):
                rj = slice(j * HALF, (j + 1) * HALF)
                attend = mm3((qh[ri], ql[ri]), (kh[rj], kl[rj]), ((1,), (1,)))
                attend = attend * jnp.exp(jnp.minimum(cum_col[ri] - cum_row[:, rj], 0.0))
                if i == j:
                    attend = jnp.where(causal, attend, 0.0)
                term = mm3(split(attend), (sh[rj], sl[rj]))
                total = term if total is None else total + term
            both_ref[head, ri] = jnp.concatenate([grown[ri] - total[:, :dim], total[:, dim:]], axis=1)


def compose(late, early):
    dim = late.shape[0]
    both = mm3(split(late[:, :dim]), split(early))
    return jnp.concatenate([both[:, :dim], both[:, dim:] + late[:, dim:]], axis=1)


def pair_kernel(core_ref, own_ref, got_ref, msg_ref, first_ref):
    dim = HALF // 2
    lead = core_ref[0] == 0
    own, got = own_ref[...], got_ref[...]
    early, late = jnp.where(lead, own, got), jnp.where(lead, got, own)
    first_ref[...] = early
    eye = jnp.where(iota((dim, HALF), 0) == iota((dim, HALF), 1), 1.0, 0.0)
    message = (compose(late, early) - eye).astype(bf16)
    for chip in range(GROUP):
        msg_ref[chip] = message


def group_kernel(place_ref, got_ref, token_ref, before_ref, total_ref):
    del token_ref
    dim = HALF // 2
    eye = jnp.where(iota((dim, HALF), 0) == iota((dim, HALF), 1), 1.0, 0.0)
    place = place_ref[0]
    running = eye
    before = eye
    for chip in range(GROUP):
        item = got_ref[chip].astype(f32) + eye
        running = item if chip == 0 else compose(item, running)
        if chip + 1 < GROUP:
            before = jnp.where(place == chip + 1, running, before)
    before_ref[...] = before
    total_ref[...] = running


def hop_kernel(total_ref, state_ref, token_ref, out_ref):
    del token_ref
    dim = HALF // 2
    moved = mm3(split(total_ref[:, :dim]), split(state_ref[...].astype(f32)))
    out_ref[...] = (moved + total_ref[:, dim:]).astype(bf16)


def enter_kernel(core_ref, before_ref, first_ref, state_ref, pair_ref):
    dim = HALF // 2
    state = mm3(split(before_ref[:, :dim]), split(state_ref[...].astype(f32))) + before_ref[:, dim:]
    after = mm3(split(first_ref[:, :dim]), split(state)) + first_ref[:, dim:]
    lead = core_ref[0] == 0
    pair_ref[0] = jnp.where(lead, state, after)
    pair_ref[1] = jnp.where(lead, after, state)


def finish_kernel(
    core_ref,
    local_ref,
    own_ref,
    got_ref,
    x_ref,
    gain_ref,
    mask_ref,
    rank_ref,
    take_ref,
    left_far,
    right_far,
    hidden_ref,
    send_ref,
):
    del left_far, right_far
    dim = HALF // 2
    lead = core_ref[0] == 0
    keep, got = own_ref[0], got_ref[1]
    states = (jnp.where(lead, keep, got), jnp.where(lead, got, keep))
    parts = []
    for head in range(2):
        out = local_ref[head, :, dim:] + mm3(split(local_ref[head, :, :dim]), split(states[head]))
        norm = out * lax.rsqrt(jnp.mean(out * out, -1, keepdims=True) + 1e-06)
        parts.append((norm * gain_ref[:, head * dim : (head + 1) * dim]).astype(bf16))
    normed = jnp.concatenate(parts, axis=1)
    hidden = (x_ref[...].astype(f32) + normed.astype(f32)).astype(bf16)
    hidden_ref[...] = hidden
    quarters, _, slots = take_ref.shape
    count = send_ref.shape[0] // quarters
    chosen = (iota((quarters * slots, hidden.shape[0]), 0) == rank_ref[...]) & (mask_ref[...] == 1)
    picked = mm(jnp.where(chosen, 1.0, 0.0).astype(bf16), hidden).astype(bf16)
    for quarter in range(quarters):
        rows = picked[quarter * slots : (quarter + 1) * slots]
        taken = mm(take_ref[quarter], rows).astype(bf16)
        send_ref[quarter * count : (quarter + 1) * count] = taken.reshape(count, *send_ref.shape[1:])


def rank_kernel(mask_ref, rank_ref):
    rows = mask_ref.shape[1]
    tri = jnp.where(iota((rows, rows), 0) <= iota((rows, rows), 1), 1.0, 0.0).astype(bf16)
    wide = jnp.broadcast_to(mask_ref[...].astype(f32), (16, rows)).astype(bf16)
    rank_ref[...] = mm(wide, tri)[:1].astype(jnp.int32) - 1


def route_kernel(mask_ref, choice_ref, take_ref, weigh_ref, token_ref):
    token_ref[...] = jnp.zeros_like(token_ref)
    quarters, total, slots = take_ref.shape
    top = choice_ref.shape[1] // 2
    count = jnp.sum(mask_ref[...])
    line = iota((total, slots), 0)
    expert = (line >> 1).astype(f32)
    earlier = jnp.where(iota((slots, slots), 0) < iota((slots, slots), 1), 1.0, 0.0).astype(bf16)
    for quarter in range(quarters):
        live = quarter * slots + iota((total, slots), 1) < count
        hit = jnp.zeros((total, slots), f32)
        weight = jnp.zeros((total, slots), f32)
        for pick in range(top):
            same = (expert == choice_ref[quarter, pick : pick + 1, :slots]) & live
            hit = hit + jnp.where(same, 1.0, 0.0)
            weight = weight + jnp.where(same, choice_ref[quarter, top + pick : top + pick + 1, :slots], 0.0)
        arrival = mm(hit.astype(bf16), earlier).astype(jnp.int32)
        here = (hit > 0.0) & (arrival == (line & 1))
        take_ref[quarter] = jnp.where(here, 1.0, 0.0).astype(bf16)
        weigh_ref[quarter] = jnp.where(here, weight, 0.0)


def expert_part(coarse_ref, rows_ref, ext_ref, pieces, total, offset):
    width = rows_ref.shape[2]
    count = rows_ref.shape[0] // GROUP
    inner = total.shape[1]
    for ref, step, parts in pieces:
        c = lax.rem(coarse_ref[0] + step, GROUP)

        @pl.when(2 * c < GROUP)
        def _():
            for n, part in enumerate(parts):
                rows = rows_ref[pl.ds((2 * c + part) * count, count)].reshape(total.shape[0], width)
                total[...] += mm(rows, ref[n * width : (n + 1) * width, :inner])

        @pl.when(2 * c >= GROUP)
        def _():
            for n, part in enumerate(parts):
                ext = jnp.broadcast_to(ext_ref[2 * c + part - GROUP].astype(f32), (16, width)).astype(bf16)
                offset[...] += mm(ext, ref[n * width : (n + 1) * width, :inner])


def near_kernel(coarse_ref, rows_ref, ext_ref, own_ref, left_ref, right_ref, total_ref, offset_ref):
    total_ref[...] = jnp.zeros_like(total_ref)
    offset_ref[...] = jnp.zeros_like(offset_ref)
    pieces = ((own_ref, 0, (0, 1)), (left_ref, GROUP - 1, (0, 1)), (right_ref, 1, (0, 1)))
    expert_part(coarse_ref, rows_ref, ext_ref, pieces, total_ref, offset_ref)


def expert_kernel(
    coarse_ref,
    rows_ref,
    ext_ref,
    near_ref,
    near_offset_ref,
    own_ref,
    left_ref,
    right_ref,
    upper_ref,
    lower_ref,
    out_ref,
    total,
    offset,
):
    width = rows_ref.shape[2]
    count = rows_ref.shape[0] // GROUP
    inner = total.shape[1]
    hidden = inner // 2
    total[...] = near_ref[...]
    offset[...] = near_offset_ref[...]
    pieces = ((upper_ref, 2, (0,)), (lower_ref, 2, (1,)))
    expert_part(coarse_ref, rows_ref, ext_ref, pieces, total, offset)
    gate = total[:, :hidden] + offset[:1, :hidden]
    up = total[:, hidden:] + offset[:1, hidden:]
    act = (gate / (1.0 + jnp.exp(-gate)) * up).astype(bf16)

    def put(step, value):
        c = lax.rem(coarse_ref[0] + step, GROUP)
        out_ref[pl.ds(c * count, count)] = value.astype(bf16).reshape(count, *out_ref.shape[1:])

    for ref, step in ((own_ref, 0), (left_ref, GROUP - 1), (right_ref, 1)):
        put(step, mm(act, ref[:, inner:]))
    put(2, mm(act[:, :width], upper_ref[:, inner:]) + mm(act[:, width:], lower_ref[:, inner:]))


def combine_kernel(mask_ref, weigh_ref, back_ref, out_ref, last_ref):
    quarters, _, slots = weigh_ref.shape
    count, width = back_ref.shape[0] // quarters, back_ref.shape[2]
    bounds = jnp.sum(mask_ref[...])
    last = jnp.zeros(last_ref.shape, f32)
    for c in range(quarters):
        wh, wl = split(weigh_ref[c])
        back = back_ref[c * count : (c + 1) * count].reshape(weigh_ref.shape[1], width)
        part = mm(wh, back, ((0,), (0,))) + mm(wl, back, ((0,), (0,)))
        out_ref[c * slots : (c + 1) * slots] = part
        here = c * slots + iota((slots, 1), 0) == bounds - 1
        last = last + jnp.sum(jnp.where(here, part, 0.0), axis=0, keepdims=True)
    last_ref[...] = last


def spread_kernel(hidden_ref, rank_ref, stretch_ref, out_ref, before_ref):
    rows, slots = hidden_ref.shape[0], stretch_ref.shape[0]
    rank = rank_ref[...]
    chosen = jnp.where(iota((slots, rows), 0) == rank, 1.0, 0.0).astype(bf16)
    sh, sl = split(stretch_ref[...])
    spread = mm(chosen, sh, ((0,), (0,))) + mm(chosen, sl, ((0,), (0,)))
    eye = iota((rows, rows), 0) == iota((rows, rows), 1)
    before = jnp.sum(jnp.where(eye & (rank < 0), 1.0, 0.0), axis=1, keepdims=True)
    before_ref[...] = jnp.broadcast_to(before, before_ref.shape)
    out_ref[...] = (hidden_ref[...].astype(f32) + spread).astype(bf16)


def entry_kernel(hidden_ref, mixed_ref, before_ref, prev_ref, out_ref):
    entry = (hidden_ref[...].astype(f32) + prev_ref[...]).astype(bf16)
    out_ref[...] = jnp.where(before_ref[:, :1] > 0.0, entry, mixed_ref[...])


def sds(shape, dtype):
    return jax.ShapeDtypeStruct(shape, dtype)


def call(kernel, outs, args, scalars=0, scratch=(), flops=10**5, megabytes=16, far_in=(), far_out=()):
    def spec(far, index):
        space = pltpu.SMEM if index < 0 else pltpu.HBM if index in far else pltpu.VMEM
        return pl.BlockSpec(memory_space=space)

    many = isinstance(outs, tuple)
    places = tuple(spec(far_out, i) for i in range(len(outs))) if many else spec((), 0)
    return pl.pallas_call(
        kernel,
        out_shape=outs,
        in_specs=[spec(far_in, i - scalars) for i in range(len(args))],
        out_specs=places,
        scratch_shapes=list(scratch),
        compiler_params=pltpu.CompilerParams(vmem_limit_bytes=megabytes * 2**20),
        cost_estimate=pl.CostEstimate(flops=flops, bytes_accessed=flops // 100, transcendentals=0),
    )(*args)


def shards(
    bytes_in,
    norm_gain,
    qkv_weight,
    gate_weight_enc,
    decay_rate,
    write_bias,
    head_gain,
    boundaries,
    picks,
    pick_gates,
    extension,
    expert_gate,
    expert_up,
    expert_down,
):
    x = bytes_in[0]
    rows, width = x.shape
    dim = HALF // 2
    seq = lax.axis_index("seq")
    spot = lax.axis_index("coarse").astype(jnp.int32)[None]
    seq_total = lax.axis_size("seq")
    core = (seq % 2).astype(jnp.int32)[None]
    place = ((seq // 2) % GROUP).astype(jnp.int32)[None]
    local_slots = picks.shape[1]
    slot_total = local_slots * GROUP
    pair_total = local_slots * picks.shape[2]
    everywhere = ("coarse", "seq", "exp")

    def exchange(array, axes, **kwargs):
        return lax.all_to_all(array, axes, split_axis=0, concat_axis=0, tiled=True, **kwargs)

    choice = jnp.concatenate([picks[0].T.astype(f32), pick_gates[0].T], axis=0)
    choice = jnp.pad(choice, ((0, 0), (0, dim - local_slots)))
    choice = exchange(jnp.broadcast_to(choice[None], (GROUP, *choice.shape)), "coarse")

    depth, hidden_units = expert_gate.shape[1:]
    columns = 2 * hidden_units + expert_down.shape[2]
    gate_rows = gate_weight_enc.transpose(0, 2, 1)
    own, give, q, k, solved, cum, x_share, weights = call(
        delta_kernel,
        (
            sds((dim, HALF), f32),
            sds((dim, HALF), f32),
            sds((rows, HALF), f32),
            sds((rows, HALF), f32),
            sds((2, rows, HALF), f32),
            sds((rows, 2), f32),
            sds((rows, HALF), bf16),
            sds((depth, columns), bf16),
        ),
        (
            jnp.concatenate([core, spot]),
            x,
            norm_gain[None],
            qkv_weight,
            gate_rows,
            decay_rate[None],
            write_bias[None],
            expert_gate,
            expert_up,
            expert_down,
        ),
        scalars=1,
        scratch=(
            pltpu.VMEM((rows, width), bf16),
            pltpu.VMEM((1, width), f32),
            pltpu.VMEM(qkv_weight.shape, bf16),
            pltpu.VMEM(gate_rows.shape, bf16),
            pltpu.VMEM((1, 2), f32),
            pltpu.VMEM((1, 2), f32),
            pltpu.VMEM((8, dim, HALF), bf16),
            pltpu.VMEM((8, dim, dim), f32),
            pltpu.SemaphoreType.DMA((10,)),
        ),
        flops=2 * 10**9,
        megabytes=60,
        far_in=range(9),
    )

    swap = [(i, i ^ 1) for i in range(seq_total)]
    got = lax.ppermute(give, "seq", swap)
    local, ready = call(local_kernel, (sds((2, rows, HALF), f32), sds((8, dim), f32)), (q, k, solved, cum))
    rank = call(rank_kernel, sds((1, rows), jnp.int32), (boundaries,))
    take, weigh, routed = call(
        route_kernel,
        (
            sds((GROUP, pair_total, local_slots), bf16),
            sds((GROUP, pair_total, local_slots), f32),
            sds((8, dim), f32),
        ),
        (boundaries, choice),
    )
    message, first = call(
        pair_kernel, (sds((GROUP, dim, HALF), bf16), sds((dim, HALF), f32)), (core, own, got), scalars=1
    )
    half = depth // 2
    ring = [(i, (i + 1) % GROUP) for i in range(GROUP)]
    back = [(b, a) for a, b in ring]
    left = lax.ppermute(weights, "coarse", ring)
    right = lax.ppermute(weights, "coarse", back)
    facing = (lax.ppermute(left[:half], "coarse", ring), lax.ppermute(right[half:], "coarse", back))
    stride = 2 * GROUP
    groups = [
        [stride * g + 2 * i + c for i in range(GROUP)] for g in range(seq_total // stride) for c in range(2)
    ]
    chips = exchange(message, "seq", axis_index_groups=groups)
    before, total = call(
        group_kernel, (sds((dim, HALF), f32), sds((dim, HALF), f32)), (place, chips, ready), scalars=1
    )
    state = jnp.zeros((dim, dim), bf16)
    for hop in range(seq_total // stride - 1):
        if hop == 0:
            outgoing = total[:, dim:].astype(bf16)
        else:
            token = choice if hop == 1 else routed
            outgoing = call(hop_kernel, sds((dim, dim), bf16), (total, state, token))
        pairs = [(stride * hop + i, stride * (hop + 1) + i) for i in range(stride)]
        state = state + lax.ppermute(outgoing, "seq", pairs)
    states = call(enter_kernel, sds((2, dim, dim), f32), (core, before, first, state), scalars=1)
    others = lax.ppermute(states, "seq", swap)

    devices = lax.axis_size(everywhere)
    capacity = GROUP * pair_total // devices
    hidden, outgoing = call(
        finish_kernel,
        (sds((rows, HALF), bf16), sds((devices, capacity, HALF), bf16)),
        (core, local, states, others, x_share, head_gain[None], boundaries, rank, take, left, right),
        scalars=1,
        far_in=(8, 9),
    )
    received = exchange(outgoing, everywhere)
    parts = (sds((pair_total, 2 * hidden_units), f32), sds((16, 2 * hidden_units), f32))
    extra_rows = extension.reshape(width // HALF, 1, HALF)
    near = call(near_kernel, parts, (spot, received, extra_rows, weights, left, right), scalars=1)
    value = call(
        expert_kernel,
        sds((devices, capacity, HALF), bf16),
        (spot, received, extra_rows, *near, weights, left, right, *facing),
        scalars=1,
        scratch=tuple(pltpu.VMEM(part.shape, part.dtype) for part in parts),
    )
    returned = exchange(value, everywhere)
    stretch, last = call(
        combine_kernel,
        (sds((slot_total, HALF), f32), sds((1, HALF), f32)),
        (boundaries, weigh, returned),
    )
    previous = lax.ppermute(last, "seq", [(i, i + 1) for i in range(seq_total - 1)])
    mixed, early = call(
        spread_kernel, (sds((rows, HALF), bf16), sds((rows, dim), f32)), (hidden, rank, stretch), flops=10**9
    )
    mixed = call(entry_kernel, sds((rows, HALF), bf16), (hidden, mixed, early, previous))
    return mixed[None]


def solution(mesh):
    placed = (
        P("exp", "seq", None),
        P(),
        P(None, None, "coarse"),
        P(None, None, "coarse"),
        P("coarse"),
        P("coarse"),
        P("coarse"),
        P("exp", "seq"),
        P("exp", ("seq", "coarse"), None),
        P("exp", ("seq", "coarse"), None),
        P(),
        P(("seq", "exp"), "coarse", None),
        P(("seq", "exp"), "coarse", None),
        P(("seq", "exp"), None, "coarse"),
    )
    return jax.shard_map(
        shards, mesh=mesh, in_specs=placed, out_specs=P("exp", "seq", "coarse"), check_vma=False
    )
```

time: 197 us -> 185 us (0.939)
  waiting for transfers between devices: 47.1 us -> 31.4 us
  between operations: 15.8 us -> 0.36 us
  starting transfers between devices: 48.1 us -> 62.6 us
  blocking collectives: 48.9 us -> 53.6 us
  local copies, waits for them, and re-layouts: 8.19 us -> 10.8 us
    all_to_all x3 -> x2, waiting for transfers between devices: 43.6 us -> 28.6 us  [exchange(): lax.all_to_all(array, axes, split_axis=0, concat_axis=0, tiled=True, **kw...]
    ppermute x1 -> x5, starting transfers between devices: 4.84 us -> 19.6 us  [the longest x1 5.78 us: shards(): others = lax.ppermute(states, 'seq', swap)]
    all_to_all x2, blocking collectives: 48.9 us -> 53.6 us  [exchange(): lax.all_to_all(array, axes, split_axis=0, concat_axis=0, tiled=True, **kw...]
    unnamed x33 -> x34, local copies, waits for them, and re-layouts: 5.15 us -> 9.04 us
    pallas_call x13 -> x15, Pallas kernels: 26 us -> 24.7 us  [call(): pl.pallas_call(kernel, out_shape=outs, in_specs=[spec(far_in, i - scalars...]
    all_to_all x3 -> x2, starting transfers between devices: 24.9 us -> 25.9 us  [exchange(): lax.all_to_all(array, axes, split_axis=0, concat_axis=0, tiled=True, **kw...]
  transfers between devices with their start and end apart: 10 -> 12, of which waited for: 7 -> 5; matrix products, arithmetic and copies ran while one was open for 2% -> 1% of each run, Pallas kernels for 10% -> 4%
where the time goes in v2:
time: 185 us; the launch traced here: 184 us
  starting transfers between devices  62.6 us (34%)
  blocking collectives  53.6 us (29%)
  waiting for transfers between devices  31.4 us (17%)
  Pallas kernels  24.7 us (13%)
  local copies, waits for them, and re-layouts  10.8 us (6%)
    all_to_all x2, blocking collectives, exchange(): lax.all_to_all(array, axes, split_axis=0, concat_axis=0, tiled=True, **kw...  53.6 us
    all_to_all x2, waiting for transfers between devices, exchange(): lax.all_to_all(array, axes, split_axis=0, concat_axis=0, tiled=True, **kw...  28.6 us
    all_to_all x2, starting transfers between devices, exchange(): lax.all_to_all(array, axes, split_axis=0, concat_axis=0, tiled=True, **kw...  25.9 us
    pallas_call x15, Pallas kernels, call(): pl.pallas_call(kernel, out_shape=outs, in_specs=[spec(far_in, i - scalars...  24.7 us
    unnamed x34, local copies, waits for them, and re-layouts  9.04 us
    ppermute x3, starting transfers between devices, shards(): state = state + lax.ppermute(outgoing, 'seq', pairs)  8 us
    ppermute x1, starting transfers between devices, shards(): got = lax.ppermute(give, 'seq', swap)  7.23 us
    ppermute x1, starting transfers between devices, shards(): others = lax.ppermute(states, 'seq', swap)  5.78 us
  transfers between devices with their start and end apart: 12, of which 5 were waited for; matrix products, arithmetic and copies ran while one was open for 1% of the time, Pallas kernels for 4%

profile of v2, /device:TPU:1, one launch (start us, length us, event | category | flops | bytes accessed | tf_op | source)
XLA Modules:
  0.0 184.2 jit_solution(12375378711127641559)
XLA Ops:
  0.0 0.7 pad_add_fusion.spots_ref
  0.7 13.3 %shard_map.136 = (f32[128,256]{1,0:T(8,128)}, f32[128,256]{1,0:T(8,128)}, f32[512,256]{1,0:T(8,128)}, f32[512,256]{1,0:T(8,128)}, f32[2,512,256]{2,1,0:T(8,128)}...) custom-call(s32[2]{0:T(128)} %pad_add_fusion.spots_ref, bf16[512,1024]{1,0:T(8,128)(2,1)} %bitcast.19, ...), custom_call_target="tpu_custom_call" | custom-call | flops 2000000000 | bytes 20000000 | tf_op jit(solution)/shard_map/pallas_call | solution.py:433
  14.0 5.5 %collective-permute-start.6 = (bf16[512,1280]{1,0:T(8,128)(2,1)}, bf16[512,1280]{1,0:T(8,128)(2,1)S(1)}, u32[]{:S(2)}, u32[]{:S(2)}) collective-permute-start(bf16[512,1280]{1,0:T(8,128)(2,1)} %get-tuple-element.45.own_ref), channel_id=1, source_target_pairs={{4,0},{8,4},{12,8},{0,12},{5,1},{9,5},{13,9},{1,13},{6,2},{10,6},{... | collective-permute-start | bytes 3932168 | tf_op jit(solution)/shard_map/ppermute | solution.py:544
  19.5 1.9 %collective-permute-start.5 = (bf16[512,1280]{1,0:T(8,128)(2,1)}, bf16[512,1280]{1,0:T(8,128)(2,1)S(1)}, u32[]{:S(2)}, u32[]{:S(2)}) collective-permute-start(bf16[512,1280]{1,0:T(8,128)(2,1)} %get-tuple-element.45.own_ref), channel_id=1, source_target_pairs={{0,4},{4,8},{8,12},{12,0},{1,5},{5,9},{9,13},{13,1},{2,6},{6,10},{... | collective-permute-start | bytes 3932168 | tf_op jit(solution)/shard_map/ppermute | solution.py:543
  21.4 7.2 %collective-permute-start = (f32[128,256]{1,0:T(8,128)}, f32[128,256]{1,0:T(8,128)S(1)}, u32[]{:S(2)}, u32[]{:S(2)}) collective-permute-start(f32[128,256]{1,0:T(8,128)} %get-tuple-element.36), channel_id=1, source_target_pairs={{0,16},{16,0},{32,48},{48,32},{64,80},{80,64},{96,112},{112,96},{1... | collective-permute-start | bytes 393224 | tf_op jit(solution)/shard_map/ppermute | solution.py:525
  28.6 1.2 collective-permute-done.got_ref
  29.8 0.9 copy-done.11
  30.7 0.9 shard_map.138
  31.6 3.4 %all-to-all-start = ((bf16[4,128,256]{2,1,0:T(8,128)(2,1)}), bf16[4,128,256]{2,1,0:T(8,128)(2,1)S(1)}, u32[]{:S(2)}, u32[]{:S(2)}) async-start(bf16[4,128,256]{2,1,0:T(8,128)(2,1)} %get-tuple-element.37), calls=%async_computation | async-start | bytes 524288 | tf_op jit(solution)/shard_map/all_to_all | solution.py:474
  35.0 0.0 copy-start.14
  35.1 0.0 copy-start.3
  35.1 1.2 copy-done.3
  36.3 1.0 copy-done.7
  37.3 1.0 copy-done.8
  38.4 0.9 copy-done.10
  39.3 1.6 shard_map.137
  41.0 0.0 copy-start.1
  41.0 1.0 copy-done.1
  42.0 0.0 copy-done.14
  42.0 0.8 all-to-all-done.got_ref
  42.7 0.6 shard_map.139
  43.4 6.7 %collective-permute-start.1 = (bf16[128,128]{1,0:T(8,128)(2,1)S(1)}, bf16[128,128]{1,0:T(8,128)(2,1)S(1)}, u32[]{:S(2)}, u32[]{:S(2)}) collective-permute-start(bf16[128,128]{1,0:T(8,128)(2,1)S(1)} %slice.17), channel_id=1, source_target_pairs={{0,128},{16,144},{32,160},{48,176},{64,192},{80,208},{96,224},{112... | collective-permute-start | bytes 98312 | tf_op jit(solution)/shard_map/ppermute | solution.py:562
  50.1 0.0 copy-done.15
  50.1 8.3 %all_to_all.20.token_ref.choice_ref = f32[4,16,128]{2,1,0:T(8,128)S(1)} all-to-all(f32[4,16,128]{2,1,0:T(8,128)S(1)} %broadcast_in_dim.36), channel_id=1, replica_groups=mesh['seq'=32,'coarse'=4,'exp'=4] {'coarse'}, dimensions={0} | all-to-all | bytes 65536 | tf_op jit(solution)/shard_map/all_to_all | solution.py:474
  58.4 0.0 collective-permute-done.1.state_ref
  58.4 0.2 shard_map.140
  58.6 0.7 collective-permute-start.2
  59.3 0.0 copy-done.12
  59.3 1.4 shard_map.141
  60.7 0.0 copy-start.4
  60.7 0.8 copy-done.4
  61.5 0.0 collective-permute-done.2
  61.5 0.2 shard_map.142
  61.7 0.7 collective-permute-start.3
  62.4 0.0 collective-permute-done.3
  62.4 0.4 shard_map.143.own_ref
  62.7 5.8 %collective-permute-start.4 = (f32[2,128,128]{2,1,0:T(8,128)S(1)}, f32[2,128,128]{2,1,0:T(8,128)S(1)}, u32[]{:S(2)}, u32[]{:S(2)}) collective-permute-start(f32[2,128,128]{2,1,0:T(8,128)S(1)} %shard_map.143.own_ref), channel_id=1, source_target_pairs={{0,16},{16,0},{32,48},{48,32},{64,80},{80,64},{96,112},{112,96},{1... | collective-permute-start | bytes 393224 | tf_op jit(solution)/shard_map/ppermute | solution.py:564
  68.5 0.2 shard_map.144.rank_ref
  68.7 0.8 collective-permute-done.4.got_ref
  69.5 0.0 collective-permute-done.6.right_far.right_ref
  69.5 0.0 collective-permute-done.5.left_far.left_ref
  69.5 0.0 copy-done.9
  69.5 0.0 copy-done.13
  69.5 0.0 copy-done.2
  69.5 1.0 shard_map.145
  70.5 0.8 copy-done.6
  71.3 22.5 %all-to-all-start.2 = ((bf16[512,2,256]{2,1,0:T(2,128)(2,1)}), bf16[512,2,256]{2,1,0:T(2,128)(2,1)S(1)}, u32[]{:S(2)}, u32[]{:S(2)}) async-start(bf16[512,2,256]{2,1,0:T(2,128)(2,1)} %copy-done.6), calls=%async_computation.2 | async-start | bytes 1048576 | tf_op jit(solution)/shard_map/all_to_all | solution.py:474
  93.7 0.0 copy-start.16
  93.8 0.9 slice.15
  94.6 4.5 %collective-permute-start.8 = (bf16[256,1280]{1,0:T(8,128)(2,1)}, bf16[256,1280]{1,0:T(8,128)(2,1)}, u32[]{:S(2)}, u32[]{:S(2)}) collective-permute-start(bf16[256,1280]{1,0:T(8,128)(2,1)} %slice.15), channel_id=1, source_target_pairs={{4,0},{8,4},{12,8},{0,12},{5,1},{9,5},{13,9},{1,13},{6,2},{10,6},{... | collective-permute-start | bytes 1966088 | tf_op jit(solution)/shard_map/ppermute | solution.py:545
  99.2 0.9 slice.14
  100.1 1.9 %collective-permute-start.7 = (bf16[256,1280]{1,0:T(8,128)(2,1)}, bf16[256,1280]{1,0:T(8,128)(2,1)}, u32[]{:S(2)}, u32[]{:S(2)}) collective-permute-start(bf16[256,1280]{1,0:T(8,128)(2,1)} %slice.14), channel_id=1, source_target_pairs={{0,4},{4,8},{8,12},{12,0},{1,5},{5,9},{9,13},{13,1},{2,6},{6,10},{... | collective-permute-start | bytes 1966088 | tf_op jit(solution)/shard_map/ppermute | solution.py:545
  102.0 27.9 %all-to-all-done.2.rows_ref = bf16[512,2,256]{2,1,0:T(2,128)(2,1)S(1)} async-done(((bf16[512,2,256]{2,1,0:T(2,128)(2,1)}), bf16[512,2,256]{2,1,0:T(2,128)(2,1)S(1)}, u32[]{:S(2)}, u32[]{:S(2)}) %all-to-all-start.2) | async-done | bytes 524320 | tf_op jit(solution)/shard_map/all_to_all | solution.py:474
  129.9 1.3 copy-done
  131.2 1.2 shard_map.146
  132.4 0.0 collective-permute-done.8.lower_ref
  132.4 0.0 collective-permute-done.7.upper_ref
  132.4 2.3 %shard_map.147 = bf16[512,2,256]{2,1,0:T(2,128)(2,1)S(1)} custom-call(s32[1]{0:T(128)} %bitcast.1.coarse_ref, bf16[512,2,256]{2,1,0:T(2,128)(2,1)S(1)} %all-to-all-done.2.rows_ref, bf16[4,1,256]{2,1,0:T(2,128)(2,1)S(1)} %reshape.6.ext_ref, f32[256,1024]{1,0:T(8,128)S(1)} %get-tuple-element.49.near_ref, f32[16,1024]{1,0:T(8,128)S(1)} %get-tuple-element.50.near_offset_ref, ...), custom_call_target="tpu_custom_call" | custom-call | flops 100000 | bytes 1000 | tf_op jit(solution)/shard_map/pallas_call | solution.py:433
  134.7 45.3 %all_to_all.21.back_ref = bf16[512,2,256]{2,1,0:T(2,128)(2,1)S(1)} all-to-all(bf16[512,2,256]{2,1,0:T(2,128)(2,1)S(1)} %shard_map.147), channel_id=1, replica_groups=mesh['seq'=32,'coarse'=4,'exp'=4] {'coarse','seq','exp'}, dimensions={0} | all-to-all | bytes 1048576 | tf_op jit(solution)/shard_map/all_to_all | solution.py:474
  179.9 0.4 shard_map.148
  180.3 1.9 %collective-permute-start.9 = (f32[1,256]{1,0:T(1,128)S(1)}, f32[1,256]{1,0:T(1,128)S(1)}, u32[]{:S(2)}, u32[]{:S(2)}) collective-permute-start(f32[1,256]{1,0:T(1,128)S(1)} %get-tuple-element.54), channel_id=1, source_target_pairs={{0,16},{16,32},{32,48},{48,64},{64,80},{80,96},{96,112},{112,128},... | collective-permute-start | bytes 3080 | tf_op jit(solution)/shard_map/ppermute | solution.py:592
  182.3 0.3 shard_map.149
  182.6 0.8 collective-permute-done.9.prev_ref
  183.4 0.8 shard_map.150
  (21 shorter events, 0.1 us)
Async XLA Ops:
  14.0 55.5 %collective-permute-start.6 = (bf16[512,1280]{1,0:T(8,128)(2,1)}, bf16[512,1280]{1,0:T(8,128)(2,1)S(1)}, u32[]{:S(2)}, u32[]{:S(2)}) collective-permute-start(bf16[512,1280]{1,0:T(8,128)(2,1)} %get-tuple-element.45.own_ref), channel_id=1, source_target_pairs={{4,0},{8,4},{12,8},{0,12},{5,1},{9,5},{13,9},{1,13},{6,2},{10,6},{... | collective-permute-start | bytes 3932168 | tf_op jit(solution)/shard_map/ppermute | solution.py:544
  19.5 50.0 %collective-permute-start.5 = (bf16[512,1280]{1,0:T(8,128)(2,1)}, bf16[512,1280]{1,0:T(8,128)(2,1)S(1)}, u32[]{:S(2)}, u32[]{:S(2)}) collective-permute-start(bf16[512,1280]{1,0:T(8,128)(2,1)} %get-tuple-element.45.own_ref), channel_id=1, source_target_pairs={{0,4},{4,8},{8,12},{12,0},{1,5},{5,9},{9,13},{13,1},{2,6},{6,10},{... | collective-permute-start | bytes 3932168 | tf_op jit(solution)/shard_map/ppermute | solution.py:543
  21.4 8.4 %collective-permute-start = (f32[128,256]{1,0:T(8,128)}, f32[128,256]{1,0:T(8,128)S(1)}, u32[]{:S(2)}, u32[]{:S(2)}) collective-permute-start(f32[128,256]{1,0:T(8,128)} %get-tuple-element.36), channel_id=1, source_target_pairs={{0,16},{16,0},{32,48},{48,32},{64,80},{80,64},{96,112},{112,96},{1... | collective-permute-start | bytes 393224 | tf_op jit(solution)/shard_map/ppermute | solution.py:525
  29.8 0.9 copy-start.11
  31.6 11.1 %all-to-all-start = ((bf16[4,128,256]{2,1,0:T(8,128)(2,1)}), bf16[4,128,256]{2,1,0:T(8,128)(2,1)S(1)}, u32[]{:S(2)}, u32[]{:S(2)}) async-start(bf16[4,128,256]{2,1,0:T(8,128)(2,1)} %get-tuple-element.37), calls=%async_computation | async-start | bytes 524288 | tf_op jit(solution)/shard_map/all_to_all | solution.py:474
  35.0 6.9 %copy-start.14 = (s32[1,32,8]{1,2,0:T(8,128)S(1)}, s32[1,32,8]{1,2,0:T(8,128)}, u32[]{:S(2)}) copy-start(s32[1,32,8]{1,2,0:T(8,128)} %param.22) | copy-start | bytes 3076
  35.1 1.2 copy-start.3
  36.3 1.0 copy-start.7
  37.3 1.0 copy-start.8
  38.4 0.9 copy-start.10
  39.3 10.8 %copy-start.15 = (f32[1,32,8]{1,2,0:T(8,128)S(1)}, f32[1,32,8]{1,2,0:T(8,128)}, u32[]{:S(2)}) copy-start(f32[1,32,8]{1,2,0:T(8,128)} %param.23) | copy-start | bytes 3076
  39.3 20.0 %copy-start.12 = (s32[1,512]{1,0:T(1,128)S(1)}, s32[1,512]{1,0:T(1,128)}, u32[]{:S(2)}) copy-start(s32[1,512]{1,0:T(1,128)} %mask_ref.7) | copy-start | bytes 6148
  41.0 1.0 copy-start.1
  42.0 27.6 %copy-start.9 = (bf16[512,256]{1,0:T(8,128)(2,1)S(1)}, bf16[512,256]{1,0:T(8,128)(2,1)}, u32[]{:S(2)}) copy-start(bf16[512,256]{1,0:T(8,128)(2,1)} %get-tuple-element.43.x_ref) | copy-start | bytes 786436
  42.0 27.6 %copy-start.13 = (f32[256]{0:T(256)S(1)}, f32[256]{0:T(256)}, u32[]{:S(2)}) copy-start(f32[256]{0:T(256)} %param.20) | copy-start | bytes 3076
  42.7 26.8 %copy-start.2 = (f32[2,512,256]{2,1,0:T(8,128)S(1)}, f32[2,512,256]{2,1,0:T(8,128)}, u32[]{:S(2)}) copy-start(f32[2,512,256]{2,1,0:T(8,128)} %copy-done.1) | copy-start | bytes 3145732
  43.4 15.0 %collective-permute-start.1 = (bf16[128,128]{1,0:T(8,128)(2,1)S(1)}, bf16[128,128]{1,0:T(8,128)(2,1)S(1)}, u32[]{:S(2)}, u32[]{:S(2)}) collective-permute-start(bf16[128,128]{1,0:T(8,128)(2,1)S(1)} %slice.17), channel_id=1, source_target_pairs={{0,128},{16,144},{32,160},{48,176},{64,192},{80,208},{96,224},{112... | collective-permute-start | bytes 98312 | tf_op jit(solution)/shard_map/ppermute | solution.py:562
  58.6 2.9 %collective-permute-start.2 = (bf16[128,128]{1,0:T(8,128)(2,1)S(1)}, bf16[128,128]{1,0:T(8,128)(2,1)S(1)}, u32[]{:S(2)}, u32[]{:S(2)}) collective-permute-start(bf16[128,128]{1,0:T(8,128)(2,1)S(1)} %shard_map.140), channel_id=1, source_target_pairs={{128,256},{144,272},{160,288},{176,304},{192,320},{208,336},{224,3... | collective-permute-start | bytes 98312 | tf_op jit(solution)/shard_map/ppermute | solution.py:562
  60.7 0.8 copy-start.4
  61.7 0.7 collective-permute-start.3
  62.7 6.7 %collective-permute-start.4 = (f32[2,128,128]{2,1,0:T(8,128)S(1)}, f32[2,128,128]{2,1,0:T(8,128)S(1)}, u32[]{:S(2)}, u32[]{:S(2)}) collective-permute-start(f32[2,128,128]{2,1,0:T(8,128)S(1)} %shard_map.143.own_ref), channel_id=1, source_target_pairs={{0,16},{16,0},{32,48},{48,32},{64,80},{80,64},{96,112},{112,96},{1... | collective-permute-start | bytes 393224 | tf_op jit(solution)/shard_map/ppermute | solution.py:564
  70.5 0.8 copy-start.6
  71.3 58.6 %all-to-all-start.2 = ((bf16[512,2,256]{2,1,0:T(2,128)(2,1)}), bf16[512,2,256]{2,1,0:T(2,128)(2,1)S(1)}, u32[]{:S(2)}, u32[]{:S(2)}) async-start(bf16[512,2,256]{2,1,0:T(2,128)(2,1)} %copy-done.6), calls=%async_computation.2 | async-start | bytes 1048576 | tf_op jit(solution)/shard_map/all_to_all | solution.py:474
  93.7 8.2 %copy-start.16 = (bf16[1024]{0:T(1024)(128)(2,1)S(1)}, bf16[1024]{0:T(1024)(128)(2,1)}, u32[]{:S(2)}) copy-start(bf16[1024]{0:T(1024)(128)(2,1)} %param.24) | copy-start | bytes 6148
  94.6 37.8 %collective-permute-start.8 = (bf16[256,1280]{1,0:T(8,128)(2,1)}, bf16[256,1280]{1,0:T(8,128)(2,1)}, u32[]{:S(2)}, u32[]{:S(2)}) collective-permute-start(bf16[256,1280]{1,0:T(8,128)(2,1)} %slice.15), channel_id=1, source_target_pairs={{4,0},{8,4},{12,8},{0,12},{5,1},{9,5},{13,9},{1,13},{6,2},{10,6},{... | collective-permute-start | bytes 1966088 | tf_op jit(solution)/shard_map/ppermute | solution.py:545
  100.1 32.3 %collective-permute-start.7 = (bf16[256,1280]{1,0:T(8,128)(2,1)}, bf16[256,1280]{1,0:T(8,128)(2,1)}, u32[]{:S(2)}, u32[]{:S(2)}) collective-permute-start(bf16[256,1280]{1,0:T(8,128)(2,1)} %slice.14), channel_id=1, source_target_pairs={{0,4},{4,8},{8,12},{12,0},{1,5},{5,9},{9,13},{13,1},{2,6},{6,10},{... | collective-permute-start | bytes 1966088 | tf_op jit(solution)/shard_map/ppermute | solution.py:545
  129.9 1.3 copy-start
  134.7 45.3 %copy-start.5 = (f32[4,256,32]{2,1,0:T(8,128)S(1)}, f32[4,256,32]{2,1,0:T(8,128)}, u32[]{:S(2)}) copy-start(f32[4,256,32]{2,1,0:T(8,128)} %copy-done.4) | copy-start | bytes 393220
  180.3 3.0 %collective-permute-start.9 = (f32[1,256]{1,0:T(1,128)S(1)}, f32[1,256]{1,0:T(1,128)S(1)}, u32[]{:S(2)}, u32[]{:S(2)}) collective-permute-start(f32[1,256]{1,0:T(1,128)S(1)} %get-tuple-element.54), channel_id=1, source_target_pairs={{0,16},{16,32},{32,48},{48,64},{64,80},{80,96},{96,112},{112,128},... | collective-permute-start | bytes 3080 | tf_op jit(solution)/shard_map/ppermute | solution.py:592

commit v3 on v2

--- a/solution.py
+++ b/solution.py
@@ -36,7 +36,6 @@
 
 
 def delta_kernel(
-    spots_ref,
     x_far,
     gain_far,
     w_far,
@@ -48,10 +47,7 @@
     edown_far,
     own_ref,
     give_ref,
-    q_ref,
-    k_ref,
-    sol_ref,
-    cum_ref,
+    local_ref,
     share_ref,
     weights_ref,
     x_ref,
@@ -78,7 +74,7 @@
         move.start()
     for move in moves[:5]:
         move.wait()
-    first = pl.multiple_of(spots_ref[1] * HALF, HALF)
+    first = pl.multiple_of(lax.axis_index("coarse") * HALF, HALF)
     moves.append(pltpu.make_async_copy(x_ref.at[:, pl.ds(first, HALF)], share_ref, sems.at[9]))
     moves[9].start()
 
@@ -96,7 +92,6 @@
     part_l = (rest - part_m.astype(f32)).astype(bf16)
     sums = mm(tri, jnp.concatenate([part_h, part_m, part_l], axis=1))
     cum = sums[:, 0:2] + (sums[:, 2:4] + sums[:, 4:6])
-    cum_ref[...] = cum
 
     moves[5].wait()
 
@@ -106,6 +101,7 @@
 
     q_all, k_all, v_all = act(0), act(1), act(2)
     strict = iota((HALF, HALF), 0) > iota((HALF, HALF), 1)
+    causal = iota((HALF, HALF), 0) >= iota((HALF, HALF), 1)
     pair = (iota((dim, dim), 0) >> 1) == (iota((dim, dim), 1) >> 1)
     eye = jnp.where(iota((dim, dim), 0) == iota((dim, dim), 1), 1.0, 0.0)
     keep = []
@@ -114,8 +110,6 @@
         q, k, v = q_all[:, cols], k_all[:, cols], v_all[:, cols]
         q = q * lax.rsqrt(jnp.sum(q * q, -1, keepdims=True) + 1e-06)
         k = k * lax.rsqrt(jnp.sum(k * k, -1, keepdims=True) + 1e-06)
-        q_ref[:, cols] = q
-        k_ref[:, cols] = k
         cum_col = cum[:, head : head + 1]
         cum_row = as_row(cum_col)
         beta = write[:, head : head + 1]
@@ -141,7 +135,16 @@
                 cross = split(lower)
         right = jnp.concatenate([(beta * jnp.exp(cum_col)) * k, beta * v], axis=1)
         last = cum_col[rows - 1 : rows]
-        keep.append((cross, inner, right, k * jnp.exp(last - cum_col), jnp.exp(last)))
+        (qh, ql) = split(q)
+        broad = jnp.concatenate([qh, ql], axis=1)
+        attend = {}
+        for i, j in ((0, 0), (1, 1), (1, 0)):
+            ri, rj = slice(i * HALF, (i + 1) * HALF), slice(j * HALF, (j + 1) * HALF)
+            gram = mm(broad[ri], twice[rj], ((1,), (1,))) + mm(qh[ri], kl[rj], ((1,), (1,)))
+            gram = gram * jnp.exp(jnp.minimum(cum_col[ri] - cum_row[:, rj], 0.0))
+            attend[i, j] = split(jnp.where(causal, gram, 0.0) if i == j else gram)
+        grown = jnp.exp(cum_col) * q
+        keep.append((cross, inner, right, k * jnp.exp(last - cum_col), jnp.exp(last), attend, grown))
 
     def packed(left, block):
         wide = jnp.concatenate(split(block), axis=1)
@@ -160,7 +163,7 @@
 
     lax.fori_loop(1, 7, level, 0)
     for head in range(2):
-        cross, inner, right, k_end, scale = keep[head]
+        cross, inner, right, k_end, scale, attend, grown = keep[head]
         full = []
         for i in range(2):
             top, bottom = inv[4 * head + 2 * i], inv[4 * head + 2 * i + 1]
@@ -171,40 +174,20 @@
         second = right[HALF:] - mm3(cross, split(first))
         second = mm3(full[1], split(second))
         solved = jnp.concatenate([first, second], axis=0)
-        sol_ref[head] = solved
+        halves = (split(first), split(second))
+        for i in range(2):
+            ri = slice(i * HALF, (i + 1) * HALF)
+            out = mm3(attend[i, i], halves[i])
+            if i > 0:
+                out = out + mm3(attend[1, 0], halves[0])
+            local_ref[head, ri] = jnp.concatenate([grown[ri] - out[:, :dim], out[:, dim:]], axis=1)
         ends = mm3(split(k_end), split(solved), ((0,), (0,)))
         keep[head] = jnp.concatenate([scale * eye - ends[:, :dim], ends[:, dim:]], axis=1)
-    lead = spots_ref[0] == 0
+    lead = lax.rem(lax.axis_index("seq"), 2) == 0
     own_ref[...] = jnp.where(lead, keep[0], keep[1])
     give_ref[...] = jnp.where(lead, keep[1], keep[0])
     for move in moves[6:]:
         move.wait()
-
-
-def local_kernel(q_ref, k_ref, sol_ref, cum_ref, both_ref, token_ref):
-    token_ref[...] = jnp.zeros_like(token_ref)
-    dim = HALF // 2
-    causal = iota((HALF, HALF), 0) >= iota((HALF, HALF), 1)
-    for head in range(2):
-        cols = slice(head * dim, (head + 1) * dim)
-        q, k = q_ref[:, cols], k_ref[:, cols]
-        cum_col = cum_ref[:, head : head + 1]
-        cum_row = as_row(cum_col)
-        (qh, ql), (kh, kl) = split(q), split(k)
-        sh, sl = split(sol_ref[head])
-        grown = jnp.exp(cum_col) * q
-        for i in range(2):
-            ri = slice(i * HALF, (i + 1) * HALF)
-            total = None
-            for j in range(i + 1):
-                rj = slice(j * HALF, (j + 1) * HALF)
-                attend = mm3((qh[ri], ql[ri]), (kh[rj], kl[rj]), ((1,), (1,)))
-                attend = attend * jnp.exp(jnp.minimum(cum_col[ri] - cum_row[:, rj], 0.0))
-                if i == j:
-                    attend = jnp.where(causal, attend, 0.0)
-                term = mm3(split(attend), (sh[rj], sl[rj]))
-                total = term if total is None else total + term
-            both_ref[head, ri] = jnp.concatenate([grown[ri] - total[:, :dim], total[:, dim:]], axis=1)
 
 
 def compose(late, early):
@@ -302,7 +285,13 @@
     rank_ref[...] = mm(wide, tri)[:1].astype(jnp.int32) - 1
 
 
-def route_kernel(mask_ref, choice_ref, take_ref, weigh_ref, token_ref):
+def route_kernel(coarse_ref, mask_ref, near_ref, far_ref, take_ref, weigh_ref, token_ref, choice_ref):
+    here = coarse_ref[0]
+    beside, facing = here + 1 - 2 * lax.rem(here, 2), GROUP - 1 - here
+    choice_ref[here] = near_ref[0]
+    choice_ref[beside] = near_ref[1]
+    choice_ref[facing] = far_ref[0]
+    choice_ref[GROUP - 1 - beside] = far_ref[1]
     token_ref[...] = jnp.zeros_like(token_ref)
     quarters, total, slots = take_ref.shape
     top = choice_ref.shape[1] // 2
@@ -319,9 +308,9 @@
             hit = hit + jnp.where(same, 1.0, 0.0)
             weight = weight + jnp.where(same, choice_ref[quarter, top + pick : top + pick + 1, :slots], 0.0)
         arrival = mm(hit.astype(bf16), earlier).astype(jnp.int32)
-        here = (hit > 0.0) & (arrival == (line & 1))
-        take_ref[quarter] = jnp.where(here, 1.0, 0.0).astype(bf16)
-        weigh_ref[quarter] = jnp.where(here, weight, 0.0)
+        found = (hit > 0.0) & (arrival == (line & 1))
+        take_ref[quarter] = jnp.where(found, 1.0, 0.0).astype(bf16)
+        weigh_ref[quarter] = jnp.where(found, weight, 0.0)
 
 
 def expert_part(coarse_ref, rows_ref, ext_ref, pieces, total, offset):
@@ -342,6 +331,11 @@
             for n, part in enumerate(parts):
                 ext = jnp.broadcast_to(ext_ref[2 * c + part - GROUP].astype(f32), (16, width)).astype(bf16)
                 offset[...] += mm(ext, ref[n * width : (n + 1) * width, :inner])
+
+
+def stage_kernel(weights_ref, hidden_far, out_ref):
+    del hidden_far
+    out_ref[...] = weights_ref[...]
 
 
 def near_kernel(coarse_ref, rows_ref, ext_ref, own_ref, left_ref, right_ref, total_ref, offset_ref):
@@ -475,25 +469,24 @@
 
     choice = jnp.concatenate([picks[0].T.astype(f32), pick_gates[0].T], axis=0)
     choice = jnp.pad(choice, ((0, 0), (0, dim - local_slots)))
-    choice = exchange(jnp.broadcast_to(choice[None], (GROUP, *choice.shape)), "coarse")
+    choice = choice[None]
+    paired = lax.ppermute(choice, "coarse", [(i, i ^ 1) for i in range(GROUP)])
+    choice = jnp.concatenate([choice, paired])
+    facing_choice = lax.ppermute(choice, "coarse", [(i, GROUP - 1 - i) for i in range(GROUP)])
 
     depth, hidden_units = expert_gate.shape[1:]
     columns = 2 * hidden_units + expert_down.shape[2]
     gate_rows = gate_weight_enc.transpose(0, 2, 1)
-    own, give, q, k, solved, cum, x_share, weights = call(
+    own, give, local, x_share, weights = call(
         delta_kernel,
         (
             sds((dim, HALF), f32),
             sds((dim, HALF), f32),
-            sds((rows, HALF), f32),
-            sds((rows, HALF), f32),
             sds((2, rows, HALF), f32),
-            sds((rows, 2), f32),
             sds((rows, HALF), bf16),
             sds((depth, columns), bf16),
         ),
         (
-            jnp.concatenate([core, spot]),
             x,
             norm_gain[None],
             qkv_weight,
@@ -504,7 +497,6 @@
             expert_up,
             expert_down,
         ),
-        scalars=1,
         scratch=(
             pltpu.VMEM((rows, width), bf16),
             pltpu.VMEM((1, width), f32),
@@ -523,7 +515,6 @@
 
     swap = [(i, i ^ 1) for i in range(seq_total)]
     got = lax.ppermute(give, "seq", swap)
-    local, ready = call(local_kernel, (sds((2, rows, HALF), f32), sds((8, dim), f32)), (q, k, solved, cum))
     rank = call(rank_kernel, sds((1, rows), jnp.int32), (boundaries,))
     take, weigh, routed = call(
         route_kernel,
@@ -532,7 +523,9 @@
             sds((GROUP, pair_total, local_slots), f32),
             sds((8, dim), f32),
         ),
-        (boundaries, choice),
+        (spot, boundaries, choice, facing_choice),
+        scalars=1,
+        scratch=(pltpu.VMEM((GROUP, 2 * picks.shape[2], dim), f32),),
     )
     message, first = call(
         pair_kernel, (sds((GROUP, dim, HALF), bf16), sds((dim, HALF), f32)), (core, own, got), scalars=1
@@ -549,15 +542,14 @@
     ]
     chips = exchange(message, "seq", axis_index_groups=groups)
     before, total = call(
-        group_kernel, (sds((dim, HALF), f32), sds((dim, HALF), f32)), (place, chips, ready), scalars=1
+        group_kernel, (sds((dim, HALF), f32), sds((dim, HALF), f32)), (place, chips, facing_choice), scalars=1
     )
     state = jnp.zeros((dim, dim), bf16)
     for hop in range(seq_total // stride - 1):
         if hop == 0:
             outgoing = total[:, dim:].astype(bf16)
         else:
-            token = choice if hop == 1 else routed
-            outgoing = call(hop_kernel, sds((dim, dim), bf16), (total, state, token))
+            outgoing = call(hop_kernel, sds((dim, dim), bf16), (total, state, routed))
         pairs = [(stride * hop + i, stride * (hop + 1) + i) for i in range(stride)]
         state = state + lax.ppermute(outgoing, "seq", pairs)
     states = call(enter_kernel, sds((2, dim, dim), f32), (core, before, first, state), scalars=1)
@@ -575,11 +567,12 @@
     received = exchange(outgoing, everywhere)
     parts = (sds((pair_total, 2 * hidden_units), f32), sds((16, 2 * hidden_units), f32))
     extra_rows = extension.reshape(width // HALF, 1, HALF)
-    near = call(near_kernel, parts, (spot, received, extra_rows, weights, left, right), scalars=1)
+    staged = call(stage_kernel, sds(weights.shape, bf16), (weights, hidden), far_in=(1,))
+    near = call(near_kernel, parts, (spot, received, extra_rows, staged, left, right), scalars=1)
     value = call(
         expert_kernel,
         sds((devices, capacity, HALF), bf16),
-        (spot, received, extra_rows, *near, weights, left, right, *facing),
+        (spot, received, extra_rows, *near, staged, left, right, *facing),
         scalars=1,
         scratch=tuple(pltpu.VMEM(part.shape, part.dtype) for part in parts),
     )

time: 185 us -> 196 us (1.059)
  starting transfers between devices: 62.6 us -> 79 us
  blocking collectives: 53.6 us -> 45.2 us
  waiting for transfers between devices: 31.4 us -> 37 us
    ppermute x0 -> x2, starting transfers between devices: none -> 10.6 us  [the longest x1 8.67 us: shards(): lax.ppermute(choice, 'coarse', [(i, GROUP - 1 - i) for i in range(GROUP)])]
    ppermute x0 -> x2, waiting for transfers between devices: none -> 8.82 us  [the longest x1 7.74 us: shards(): paired = lax.ppermute(choice, 'coarse', [(i, i ^ 1) for i in range(GROUP)])]
    all_to_all x2 -> x1, blocking collectives: 53.6 us -> 45.2 us  [exchange(): lax.all_to_all(array, axes, split_axis=0, concat_axis=0, tiled=True, **kw...]
    all_to_all x2, starting transfers between devices: 25.9 us -> 29.9 us  [exchange(): lax.all_to_all(array, axes, split_axis=0, concat_axis=0, tiled=True, **kw...]
    all_to_all x2, waiting for transfers between devices: 28.6 us -> 25.4 us  [exchange(): lax.all_to_all(array, axes, split_axis=0, concat_axis=0, tiled=True, **kw...]
    ppermute x3, starting transfers between devices: 8 us -> 10.5 us  [shards(): state = state + lax.ppermute(outgoing, 'seq', pairs)]
  transfers between devices with their start and end apart: 12 -> 14, of which waited for: 5 -> 6; matrix products, arithmetic and copies ran while one was open for 1% -> 1% of each run, Pallas kernels for 4% -> 3%
where the time goes in v3:
time: 196 us; the launch traced here: 195 us
  starting transfers between devices  79 us (40%)
  blocking collectives  45.2 us (23%)
  waiting for transfers between devices  37 us (19%)
  Pallas kernels  23.3 us (12%)
  local copies, waits for them, and re-layouts  10.2 us (5%)
    all_to_all x1, blocking collectives, exchange(): lax.all_to_all(array, axes, split_axis=0, concat_axis=0, tiled=True, **kw...  45.2 us
    all_to_all x2, starting transfers between devices, exchange(): lax.all_to_all(array, axes, split_axis=0, concat_axis=0, tiled=True, **kw...  29.9 us
    all_to_all x2, waiting for transfers between devices, exchange(): lax.all_to_all(array, axes, split_axis=0, concat_axis=0, tiled=True, **kw...  25.4 us
    pallas_call x15, Pallas kernels, call(): pl.pallas_call(kernel, out_shape=outs, in_specs=[spec(far_in, i - scalars...  23.3 us
    ppermute x3, starting transfers between devices, shards(): state = state + lax.ppermute(outgoing, 'seq', pairs)  10.5 us
    ppermute x1, starting transfers between devices, shards(): lax.ppermute(choice, 'coarse', [(i, GROUP - 1 - i) for i in range(GROUP)])  8.67 us
    unnamed x34, local copies, waits for them, and re-layouts  8.39 us
    ppermute x1, waiting for transfers between devices, shards(): paired = lax.ppermute(choice, 'coarse', [(i, i ^ 1) for i in range(GROUP)])  7.74 us
  transfers between devices with their start and end apart: 14, of which 6 were waited for; matrix products, arithmetic and copies ran while one was open for 1% of the time, Pallas kernels for 3%

profile of v3, /device:TPU:1, one launch (start us, length us, event | category | flops | bytes accessed | tf_op | source)
XLA Modules:
  0.0 195.2 jit_solution(8641079405271804362)
XLA Ops:
  0.0 13.4 %shard_map.136 = (f32[128,256]{1,0:T(8,128)}, f32[128,256]{1,0:T(8,128)}, f32[2,512,256]{2,1,0:T(8,128)}, bf16[512,256]{1,0:T(8,128)(2,1)}, bf16[512,1280]{1,0:T(8,128)(2,1)}) custom-call(bf16[512,1024]{1,0:T(8,128)(2,1)} %bitcast.21, f32[1,1024]{1,0:T(1,128)} %bitcast.23, bf16[3,1024,256]{2,1,0:T(8,128)(2,1)} %w_far.1, bf16[2,2,1024]{2,1,0:T(2,128)(2,1)} %bitcast.22, ...), custom_call_target="tpu_custom_call" | custom-call | flops 2000000000 | bytes 20000000 | tf_op jit(solution)/shard_map/pallas_call | solution.py:427
  13.4 0.0 copy-start.7
  13.4 5.6 %collective-permute-start.8 = (bf16[512,1280]{1,0:T(8,128)(2,1)}, bf16[512,1280]{1,0:T(8,128)(2,1)S(1)}, u32[]{:S(2)}, u32[]{:S(2)}) collective-permute-start(bf16[512,1280]{1,0:T(8,128)(2,1)} %get-tuple-element.35.weights_ref), channel_id=1, source_target_pairs={{4,0},{8,4},{12,8},{0,12},{5,1},{9,5},{13,9},{1,13},{6,2},{10,6},{... | collective-permute-start | bytes 3932168 | tf_op jit(solution)/shard_map/ppermute | solution.py:537
  19.0 1.9 collective-permute-start.7
  20.9 7.2 %collective-permute-start = (f32[128,256]{1,0:T(8,128)}, f32[128,256]{1,0:T(8,128)S(1)}, u32[]{:S(2)}, u32[]{:S(2)}) collective-permute-start(f32[128,256]{1,0:T(8,128)} %get-tuple-element.27), channel_id=1, source_target_pairs={{0,16},{16,0},{32,48},{48,32},{64,80},{80,64},{96,112},{112,96},{1... | collective-permute-start | bytes 393224 | tf_op jit(solution)/shard_map/ppermute | solution.py:517
  28.2 1.2 collective-permute-done.got_ref
  29.3 0.9 copy-done.8
  30.2 0.9 shard_map.137
  31.2 3.4 %all-to-all-start = ((bf16[4,128,256]{2,1,0:T(8,128)(2,1)}), bf16[4,128,256]{2,1,0:T(8,128)(2,1)S(1)}, u32[]{:S(2)}, u32[]{:S(2)}) async-start(bf16[4,128,256]{2,1,0:T(8,128)(2,1)} %get-tuple-element.28), calls=%async_computation | async-start | bytes 524288 | tf_op jit(solution)/shard_map/all_to_all | solution.py:468
  34.6 0.0 copy-done.14
  34.6 1.9 collective-permute-start.1
  36.5 7.7 %collective-permute-done.1 = f32[1,16,128]{2,1,0:T(8,128)S(1)} collective-permute-done((f32[1,16,128]{2,1,0:T(8,128)S(1)}, f32[1,16,128]{2,1,0:T(8,128)S(1)}, u32[]{:S(2)}, u32[]{:S(2)}) %collective-permute-start.1) | collective-permute-done | bytes 8224 | tf_op jit(solution)/shard_map/ppermute | solution.py:473
  44.3 8.7 %collective-permute-start.2 = (f32[2,16,128]{2,1,0:T(8,128)S(1)}, f32[2,16,128]{2,1,0:T(8,128)S(1)}, u32[]{:S(2)}, u32[]{:S(2)}) collective-permute-start(f32[2,16,128]{2,1,0:T(8,128)S(1)} %pad_maximum_fusion.near_ref), channel_id=1, source_target_pairs={{0,12},{4,8},{8,4},{12,0},{1,13},{5,9},{9,5},{13,1},{2,14},{6,10},... | collective-permute-start | bytes 49160 | tf_op jit(solution)/shard_map/ppermute | solution.py:475
  53.0 1.1 collective-permute-done.2.token_ref.far_ref
  54.1 0.0 all-to-all-done.got_ref
  54.1 0.6 shard_map.138
  54.8 9.1 %collective-permute-start.3 = (bf16[128,128]{1,0:T(8,128)(2,1)S(1)}, bf16[128,128]{1,0:T(8,128)(2,1)S(1)}, u32[]{:S(2)}, u32[]{:S(2)}) collective-permute-start(bf16[128,128]{1,0:T(8,128)(2,1)S(1)} %slice.17), channel_id=1, source_target_pairs={{0,128},{16,144},{32,160},{48,176},{64,192},{80,208},{96,224},{112... | collective-permute-start | bytes 98312 | tf_op jit(solution)/shard_map/ppermute | solution.py:554
  63.9 0.0 copy-start.3
  63.9 0.0 copy-start.10
  63.9 0.8 copy-done.10
  64.7 0.7 copy-done.11
  65.4 1.5 shard_map.139
  66.9 0.8 copy-done.4
  67.7 0.0 collective-permute-done.3.state_ref
  67.7 0.2 shard_map.140
  67.9 0.7 collective-permute-start.4
  68.5 0.0 collective-permute-done.4
  68.6 0.2 shard_map.141
  68.8 0.7 collective-permute-start.5
  69.4 0.0 collective-permute-done.5
  69.5 0.4 shard_map.142.own_ref
  69.8 4.9 %collective-permute-start.6 = (f32[2,128,128]{2,1,0:T(8,128)S(1)}, f32[2,128,128]{2,1,0:T(8,128)S(1)}, u32[]{:S(2)}, u32[]{:S(2)}) collective-permute-start(f32[2,128,128]{2,1,0:T(8,128)S(1)} %shard_map.142.own_ref), channel_id=1, source_target_pairs={{0,16},{16,0},{32,48},{48,32},{64,80},{80,64},{96,112},{112,96},{1... | collective-permute-start | bytes 393224 | tf_op jit(solution)/shard_map/ppermute | solution.py:556
  74.7 0.2 shard_map.143.rank_ref
  74.9 0.8 collective-permute-done.6.got_ref
  75.7 0.0 collective-permute-done.8.right_far.right_ref
  75.7 0.0 collective-permute-done.7.left_far.left_ref
  75.7 0.0 copy-done.3
  75.7 0.0 copy-start.13
  75.7 0.7 copy-done.13
  76.4 1.0 shard_map.144
  77.4 0.8 copy-done.6
  78.2 26.5 %all-to-all-start.1 = ((bf16[512,2,256]{2,1,0:T(2,128)(2,1)}), bf16[512,2,256]{2,1,0:T(2,128)(2,1)S(1)}, u32[]{:S(2)}, u32[]{:S(2)}) async-start(bf16[512,2,256]{2,1,0:T(2,128)(2,1)} %copy-done.6), calls=%async_computation.1 | async-start | bytes 1048576 | tf_op jit(solution)/shard_map/all_to_all | solution.py:468
  104.7 0.0 copy-start.16
  104.7 0.9 slice.15
  105.6 4.5 %collective-permute-start.10 = (bf16[256,1280]{1,0:T(8,128)(2,1)}, bf16[256,1280]{1,0:T(8,128)(2,1)}, u32[]{:S(2)}, u32[]{:S(2)}) collective-permute-start(bf16[256,1280]{1,0:T(8,128)(2,1)} %slice.15), channel_id=1, source_target_pairs={{4,0},{8,4},{12,8},{0,12},{5,1},{9,5},{13,9},{1,13},{6,2},{10,6},{... | collective-permute-start | bytes 1966088 | tf_op jit(solution)/shard_map/ppermute | solution.py:538
  110.2 0.9 slice.14
  111.0 1.9 collective-permute-start.9
  113.0 1.3 copy-done.2
  114.3 0.1 shard_map.145.own_ref
  114.4 0.0 copy-start
  114.4 1.1 copy-done
  115.5 25.4 %all-to-all-done.1.rows_ref = bf16[512,2,256]{2,1,0:T(2,128)(2,1)S(1)} async-done(((bf16[512,2,256]{2,1,0:T(2,128)(2,1)}), bf16[512,2,256]{2,1,0:T(2,128)(2,1)S(1)}, u32[]{:S(2)}, u32[]{:S(2)}) %all-to-all-start.1) | async-done | bytes 524320 | tf_op jit(solution)/shard_map/all_to_all | solution.py:468
  140.9 1.3 copy-done.1
  142.2 1.2 shard_map.146
  143.4 0.0 collective-permute-done.10.lower_ref
  143.4 0.0 collective-permute-done.9.upper_ref
  143.4 0.0 copy-start.12
  143.4 2.2 %shard_map.147 = bf16[512,2,256]{2,1,0:T(2,128)(2,1)S(1)} custom-call(s32[1]{0:T(128)} %bitcast.12.coarse_ref, bf16[512,2,256]{2,1,0:T(2,128)(2,1)S(1)} %all-to-all-done.1.rows_ref, bf16[4,1,256]{2,1,0:T(2,128)(2,1)S(1)} %reshape.5.ext_ref, f32[256,1024]{1,0:T(8,128)S(1)} %get-tuple-element.39.near_ref, f32[16,1024]{1,0:T(8,128)S(1)} %get-tuple-element.40.near_offset_ref, ...), custom_call_target="tpu_custom_call" | custom-call | flops 100000 | bytes 1000 | tf_op jit(solution)/shard_map/pallas_call | solution.py:427
  145.7 45.2 %all_to_all.15.back_ref = bf16[512,2,256]{2,1,0:T(2,128)(2,1)S(1)} all-to-all(bf16[512,2,256]{2,1,0:T(2,128)(2,1)S(1)} %shard_map.147), channel_id=1, replica_groups=mesh['seq'=32,'coarse'=4,'exp'=4] {'coarse','seq','exp'}, dimensions={0} | all-to-all | bytes 1048576 | tf_op jit(solution)/shard_map/all_to_all | solution.py:468
  190.9 0.4 shard_map.148
  191.3 1.9 collective-permute-start.11
  193.2 0.3 shard_map.149
  193.6 0.8 collective-permute-done.11.prev_ref
  194.3 0.8 shard_map.150
  (23 shorter events, 0.1 us)
Async XLA Ops:
  0.0 34.6 %copy-start.14 = (s32[1,32,8]{1,2,0:T(8,128)S(1)}, s32[1,32,8]{1,2,0:T(8,128)}, u32[]{:S(2)}) copy-start(s32[1,32,8]{1,2,0:T(8,128)} %param.22) | copy-start | bytes 3076
  0.0 34.6 %copy-start.15 = (f32[1,32,8]{1,2,0:T(8,128)S(1)}, f32[1,32,8]{1,2,0:T(8,128)}, u32[]{:S(2)}) copy-start(f32[1,32,8]{1,2,0:T(8,128)} %param.23) | copy-start | bytes 3076
  13.4 62.3 %copy-start.7 = (bf16[512,256]{1,0:T(8,128)(2,1)S(1)}, bf16[512,256]{1,0:T(8,128)(2,1)}, u32[]{:S(2)}) copy-start(bf16[512,256]{1,0:T(8,128)(2,1)} %get-tuple-element.33.x_ref) | copy-start | bytes 786436
  13.4 62.3 %collective-permute-start.8 = (bf16[512,1280]{1,0:T(8,128)(2,1)}, bf16[512,1280]{1,0:T(8,128)(2,1)S(1)}, u32[]{:S(2)}, u32[]{:S(2)}) collective-permute-start(bf16[512,1280]{1,0:T(8,128)(2,1)} %get-tuple-element.35.weights_ref), channel_id=1, source_target_pairs={{4,0},{8,4},{12,8},{0,12},{5,1},{9,5},{13,9},{1,13},{6,2},{10,6},{... | collective-permute-start | bytes 3932168 | tf_op jit(solution)/shard_map/ppermute | solution.py:537
  19.0 56.7 %collective-permute-start.7 = (bf16[512,1280]{1,0:T(8,128)(2,1)}, bf16[512,1280]{1,0:T(8,128)(2,1)S(1)}, u32[]{:S(2)}, u32[]{:S(2)}) collective-permute-start(bf16[512,1280]{1,0:T(8,128)(2,1)} %get-tuple-element.35.weights_ref), channel_id=1, source_target_pairs={{0,4},{4,8},{8,12},{12,0},{1,5},{5,9},{9,13},{13,1},{2,6},{6,10},{... | collective-permute-start | bytes 3932168 | tf_op jit(solution)/shard_map/ppermute | solution.py:536
  20.9 8.4 %collective-permute-start = (f32[128,256]{1,0:T(8,128)}, f32[128,256]{1,0:T(8,128)S(1)}, u32[]{:S(2)}, u32[]{:S(2)}) collective-permute-start(f32[128,256]{1,0:T(8,128)} %get-tuple-element.27), channel_id=1, source_target_pairs={{0,16},{16,0},{32,48},{48,32},{64,80},{80,64},{96,112},{112,96},{1... | collective-permute-start | bytes 393224 | tf_op jit(solution)/shard_map/ppermute | solution.py:517
  29.3 0.9 copy-start.8
  31.2 22.9 %all-to-all-start = ((bf16[4,128,256]{2,1,0:T(8,128)(2,1)}), bf16[4,128,256]{2,1,0:T(8,128)(2,1)S(1)}, u32[]{:S(2)}, u32[]{:S(2)}) async-start(bf16[4,128,256]{2,1,0:T(8,128)(2,1)} %get-tuple-element.28), calls=%async_computation | async-start | bytes 524288 | tf_op jit(solution)/shard_map/all_to_all | solution.py:468
  34.6 9.7 %collective-permute-start.1 = (f32[1,16,128]{2,1,0:T(8,128)S(1)}, f32[1,16,128]{2,1,0:T(8,128)S(1)}, u32[]{:S(2)}, u32[]{:S(2)}) collective-permute-start(f32[1,16,128]{2,1,0:T(8,128)S(1)} %fusion), channel_id=1, source_target_pairs={{0,4},{4,0},{8,12},{12,8},{1,5},{5,1},{9,13},{13,9},{2,6},{6,2},{1... | collective-permute-start | bytes 24584 | tf_op jit(solution)/shard_map/ppermute | solution.py:473
  44.3 9.8 %copy-start.9 = (f32[2,16,128]{2,1,0:T(8,128)}, f32[2,16,128]{2,1,0:T(8,128)S(1)}, u32[]{:S(2)}) copy-start(f32[2,16,128]{2,1,0:T(8,128)S(1)} %pad_maximum_fusion.near_ref) | copy-start | bytes 49156
  44.3 9.8 %collective-permute-start.2 = (f32[2,16,128]{2,1,0:T(8,128)S(1)}, f32[2,16,128]{2,1,0:T(8,128)S(1)}, u32[]{:S(2)}, u32[]{:S(2)}) collective-permute-start(f32[2,16,128]{2,1,0:T(8,128)S(1)} %pad_maximum_fusion.near_ref), channel_id=1, source_target_pairs={{0,12},{4,8},{8,4},{12,0},{1,13},{5,9},{9,5},{13,1},{2,14},{6,10},... | collective-permute-start | bytes 49160 | tf_op jit(solution)/shard_map/ppermute | solution.py:475
  54.8 12.9 %collective-permute-start.3 = (bf16[128,128]{1,0:T(8,128)(2,1)S(1)}, bf16[128,128]{1,0:T(8,128)(2,1)S(1)}, u32[]{:S(2)}, u32[]{:S(2)}) collective-permute-start(bf16[128,128]{1,0:T(8,128)(2,1)S(1)} %slice.17), channel_id=1, source_target_pairs={{0,128},{16,144},{32,160},{48,176},{64,192},{80,208},{96,224},{112... | collective-permute-start | bytes 98312 | tf_op jit(solution)/shard_map/ppermute | solution.py:554
  63.9 11.8 %copy-start.3 = (f32[2,512,256]{2,1,0:T(8,128)S(1)}, f32[2,512,256]{2,1,0:T(8,128)}, u32[]{:S(2)}) copy-start(f32[2,512,256]{2,1,0:T(8,128)} %get-tuple-element.25.local_ref) | copy-start | bytes 3145732
  63.9 0.8 copy-start.10
  64.7 0.7 copy-start.11
  66.9 0.8 copy-start.4
  67.9 0.7 collective-permute-start.4
  68.8 0.7 collective-permute-start.5
  69.8 5.9 %collective-permute-start.6 = (f32[2,128,128]{2,1,0:T(8,128)S(1)}, f32[2,128,128]{2,1,0:T(8,128)S(1)}, u32[]{:S(2)}, u32[]{:S(2)}) collective-permute-start(f32[2,128,128]{2,1,0:T(8,128)S(1)} %shard_map.142.own_ref), channel_id=1, source_target_pairs={{0,16},{16,0},{32,48},{48,32},{64,80},{80,64},{96,112},{112,96},{1... | collective-permute-start | bytes 393224 | tf_op jit(solution)/shard_map/ppermute | solution.py:556
  75.7 0.7 copy-start.13
  77.4 0.8 copy-start.6
  78.2 62.7 %all-to-all-start.1 = ((bf16[512,2,256]{2,1,0:T(2,128)(2,1)}), bf16[512,2,256]{2,1,0:T(2,128)(2,1)S(1)}, u32[]{:S(2)}, u32[]{:S(2)}) async-start(bf16[512,2,256]{2,1,0:T(2,128)(2,1)} %copy-done.6), calls=%async_computation.1 | async-start | bytes 1048576 | tf_op jit(solution)/shard_map/all_to_all | solution.py:468
  104.7 8.2 %copy-start.16 = (bf16[1024]{0:T(1024)(128)(2,1)S(1)}, bf16[1024]{0:T(1024)(128)(2,1)}, u32[]{:S(2)}) copy-start(bf16[1024]{0:T(1024)(128)(2,1)} %param.24) | copy-start | bytes 6148
  105.6 37.8 %collective-permute-start.10 = (bf16[256,1280]{1,0:T(8,128)(2,1)}, bf16[256,1280]{1,0:T(8,128)(2,1)}, u32[]{:S(2)}, u32[]{:S(2)}) collective-permute-start(bf16[256,1280]{1,0:T(8,128)(2,1)} %slice.15), channel_id=1, source_target_pairs={{4,0},{8,4},{12,8},{0,12},{5,1},{9,5},{13,9},{1,13},{6,2},{10,6},{... | collective-permute-start | bytes 1966088 | tf_op jit(solution)/shard_map/ppermute | solution.py:538
  111.0 32.3 %collective-permute-start.9 = (bf16[256,1280]{1,0:T(8,128)(2,1)}, bf16[256,1280]{1,0:T(8,128)(2,1)}, u32[]{:S(2)}, u32[]{:S(2)}) collective-permute-start(bf16[256,1280]{1,0:T(8,128)(2,1)} %slice.14), channel_id=1, source_target_pairs={{0,4},{4,8},{8,12},{12,0},{1,5},{5,9},{9,13},{13,1},{2,6},{6,10},{... | collective-permute-start | bytes 1966088 | tf_op jit(solution)/shard_map/ppermute | solution.py:538
  113.0 1.3 copy-start.2
  114.4 1.1 copy-start
  140.9 1.3 copy-start.1
  143.4 47.5 %copy-start.12 = (s32[1,512]{1,0:T(1,128)S(1)}, s32[1,512]{1,0:T(1,128)}, u32[]{:S(2)}) copy-start(s32[1,512]{1,0:T(1,128)} %mask_ref.7) | copy-start | bytes 6148
  145.7 45.3 %copy-start.5 = (f32[4,256,32]{2,1,0:T(8,128)S(1)}, f32[4,256,32]{2,1,0:T(8,128)}, u32[]{:S(2)}) copy-start(f32[4,256,32]{2,1,0:T(8,128)} %copy-done.4) | copy-start | bytes 393220
  191.3 3.0 %collective-permute-start.11 = (f32[1,256]{1,0:T(1,128)S(1)}, f32[1,256]{1,0:T(1,128)S(1)}, u32[]{:S(2)}, u32[]{:S(2)}) collective-permute-start(f32[1,256]{1,0:T(1,128)S(1)} %get-tuple-element.44), channel_id=1, source_target_pairs={{0,16},{16,32},{32,48},{48,64},{64,80},{80,96},{96,112},{112,128},... | collective-permute-start | bytes 3080 | tf_op jit(solution)/shard_map/ppermute | solution.py:585

commit v4 on v3

--- a/solution.py
+++ b/solution.py
@@ -33,6 +33,18 @@
     size = column.shape[0]
     eye = iota((size, size), 0) == iota((size, size), 1)
     return jnp.sum(jnp.where(eye, column, 0.0), axis=0, keepdims=True)
+
+
+def choice_kernel(picks_ref, gates_ref, out_ref):
+    top, slots = picks_ref.shape
+    out_ref[...] = jnp.zeros_like(out_ref)
+    for quarter in range(out_ref.shape[0]):
+        out_ref[quarter, :top, :slots] = picks_ref[...].astype(f32)
+        out_ref[quarter, top:, :slots] = gates_ref[...]
+
+
+def after_kernel(choice_far, give_far, same_far):
+    del choice_far, give_far, same_far
 
 
 def delta_kernel(
@@ -49,6 +61,7 @@
     give_ref,
     local_ref,
     share_ref,
+    weights_far,
     weights_ref,
     x_ref,
     gain_ref,
@@ -100,6 +113,10 @@
         return value / (1.0 + jnp.exp(-value))
 
     q_all, k_all, v_all = act(0), act(1), act(2)
+    for move in moves[6:9]:
+        move.wait()
+    leave = pltpu.make_async_copy(weights_ref, weights_far, sems.at[10])
+    leave.start()
     strict = iota((HALF, HALF), 0) > iota((HALF, HALF), 1)
     causal = iota((HALF, HALF), 0) >= iota((HALF, HALF), 1)
     pair = (iota((dim, dim), 0) >> 1) == (iota((dim, dim), 1) >> 1)
@@ -186,8 +203,8 @@
     lead = lax.rem(lax.axis_index("seq"), 2) == 0
     own_ref[...] = jnp.where(lead, keep[0], keep[1])
     give_ref[...] = jnp.where(lead, keep[1], keep[0])
-    for move in moves[6:]:
-        move.wait()
+    moves[9].wait()
+    leave.wait()
 
 
 def compose(late, early):
@@ -224,8 +241,7 @@
     total_ref[...] = running
 
 
-def hop_kernel(total_ref, state_ref, token_ref, out_ref):
-    del token_ref
+def hop_kernel(total_ref, state_ref, out_ref):
     dim = HALF // 2
     moved = mm3(split(total_ref[:, :dim]), split(state_ref[...].astype(f32)))
     out_ref[...] = (moved + total_ref[:, dim:]).astype(bf16)
@@ -285,14 +301,7 @@
     rank_ref[...] = mm(wide, tri)[:1].astype(jnp.int32) - 1
 
 
-def route_kernel(coarse_ref, mask_ref, near_ref, far_ref, take_ref, weigh_ref, token_ref, choice_ref):
-    here = coarse_ref[0]
-    beside, facing = here + 1 - 2 * lax.rem(here, 2), GROUP - 1 - here
-    choice_ref[here] = near_ref[0]
-    choice_ref[beside] = near_ref[1]
-    choice_ref[facing] = far_ref[0]
-    choice_ref[GROUP - 1 - beside] = far_ref[1]
-    token_ref[...] = jnp.zeros_like(token_ref)
+def route_kernel(mask_ref, choice_ref, take_ref, weigh_ref, token_ref):
     quarters, total, slots = take_ref.shape
     top = choice_ref.shape[1] // 2
     count = jnp.sum(mask_ref[...])
@@ -331,11 +340,6 @@
             for n, part in enumerate(parts):
                 ext = jnp.broadcast_to(ext_ref[2 * c + part - GROUP].astype(f32), (16, width)).astype(bf16)
                 offset[...] += mm(ext, ref[n * width : (n + 1) * width, :inner])
-
-
-def stage_kernel(weights_ref, hidden_far, out_ref):
-    del hidden_far
-    out_ref[...] = weights_ref[...]
 
 
 def near_kernel(coarse_ref, rows_ref, ext_ref, own_ref, left_ref, right_ref, total_ref, offset_ref):
@@ -417,19 +421,20 @@
     return jax.ShapeDtypeStruct(shape, dtype)
 
 
-def call(kernel, outs, args, scalars=0, scratch=(), flops=10**5, megabytes=16, far_in=(), far_out=()):
+def call(kernel, outs, args, scalars=0, scratch=(), flops=10**5, megabytes=16, far_in=(), far_out=(), same=None):
     def spec(far, index):
         space = pltpu.SMEM if index < 0 else pltpu.HBM if index in far else pltpu.VMEM
         return pl.BlockSpec(memory_space=space)
 
     many = isinstance(outs, tuple)
-    places = tuple(spec(far_out, i) for i in range(len(outs))) if many else spec((), 0)
+    places = tuple(spec(far_out, i) for i in range(len(outs))) if many else spec(far_out, 0)
     return pl.pallas_call(
         kernel,
         out_shape=outs,
         in_specs=[spec(far_in, i - scalars) for i in range(len(args))],
         out_specs=places,
         scratch_shapes=list(scratch),
+        input_output_aliases=same or {},
         compiler_params=pltpu.CompilerParams(vmem_limit_bytes=megabytes * 2**20),
         cost_estimate=pl.CostEstimate(flops=flops, bytes_accessed=flops // 100, transcendentals=0),
     )(*args)
@@ -467,12 +472,9 @@
     def exchange(array, axes, **kwargs):
         return lax.all_to_all(array, axes, split_axis=0, concat_axis=0, tiled=True, **kwargs)
 
-    choice = jnp.concatenate([picks[0].T.astype(f32), pick_gates[0].T], axis=0)
-    choice = jnp.pad(choice, ((0, 0), (0, dim - local_slots)))
-    choice = choice[None]
-    paired = lax.ppermute(choice, "coarse", [(i, i ^ 1) for i in range(GROUP)])
-    choice = jnp.concatenate([choice, paired])
-    facing_choice = lax.ppermute(choice, "coarse", [(i, GROUP - 1 - i) for i in range(GROUP)])
+    top = picks.shape[2]
+    choice = call(choice_kernel, sds((GROUP, 2 * top, dim), f32), (picks[0].T, pick_gates[0].T), megabytes=63)
+    choice = exchange(choice, "coarse")
 
     depth, hidden_units = expert_gate.shape[1:]
     columns = 2 * hidden_units + expert_down.shape[2]
@@ -498,6 +500,7 @@
             expert_down,
         ),
         scratch=(
+            pltpu.VMEM((depth, columns), bf16),
             pltpu.VMEM((rows, width), bf16),
             pltpu.VMEM((1, width), f32),
             pltpu.VMEM(qkv_weight.shape, bf16),
@@ -506,12 +509,15 @@
             pltpu.VMEM((1, 2), f32),
             pltpu.VMEM((8, dim, HALF), bf16),
             pltpu.VMEM((8, dim, dim), f32),
-            pltpu.SemaphoreType.DMA((10,)),
+            pltpu.SemaphoreType.DMA((11,)),
         ),
         flops=2 * 10**9,
         megabytes=60,
         far_in=range(9),
-    )
+        far_out=(4,),
+    )
+
+    give = call(after_kernel, sds(give.shape, f32), (choice, give), far_in=(0, 1), far_out=(0,), same={1: 0})
 
     swap = [(i, i ^ 1) for i in range(seq_total)]
     got = lax.ppermute(give, "seq", swap)
@@ -523,9 +529,7 @@
             sds((GROUP, pair_total, local_slots), f32),
             sds((8, dim), f32),
         ),
-        (spot, boundaries, choice, facing_choice),
-        scalars=1,
-        scratch=(pltpu.VMEM((GROUP, 2 * picks.shape[2], dim), f32),),
+        (boundaries, choice),
     )
     message, first = call(
         pair_kernel, (sds((GROUP, dim, HALF), bf16), sds((dim, HALF), f32)), (core, own, got), scalars=1
@@ -542,17 +546,17 @@
     ]
     chips = exchange(message, "seq", axis_index_groups=groups)
     before, total = call(
-        group_kernel, (sds((dim, HALF), f32), sds((dim, HALF), f32)), (place, chips, facing_choice), scalars=1
+        group_kernel, (sds((dim, HALF), f32), sds((dim, HALF), f32)), (place, chips, routed), scalars=1, flops=10**9
     )
     state = jnp.zeros((dim, dim), bf16)
     for hop in range(seq_total // stride - 1):
         if hop == 0:
             outgoing = total[:, dim:].astype(bf16)
         else:
-            outgoing = call(hop_kernel, sds((dim, dim), bf16), (total, state, routed))
+            outgoing = call(hop_kernel, sds((dim, dim), bf16), (total, state), flops=10**9)
         pairs = [(stride * hop + i, stride * (hop + 1) + i) for i in range(stride)]
         state = state + lax.ppermute(outgoing, "seq", pairs)
-    states = call(enter_kernel, sds((2, dim, dim), f32), (core, before, first, state), scalars=1)
+    states = call(enter_kernel, sds((2, dim, dim), f32), (core, before, first, state), scalars=1, flops=10**9)
     others = lax.ppermute(states, "seq", swap)
 
     devices = lax.axis_size(everywhere)
@@ -567,12 +571,11 @@
     received = exchange(outgoing, everywhere)
     parts = (sds((pair_total, 2 * hidden_units), f32), sds((16, 2 * hidden_units), f32))
     extra_rows = extension.reshape(width // HALF, 1, HALF)
-    staged = call(stage_kernel, sds(weights.shape, bf16), (weights, hidden), far_in=(1,))
-    near = call(near_kernel, parts, (spot, received, extra_rows, staged, left, right), scalars=1)
+    near = call(near_kernel, parts, (spot, received, extra_rows, weights, left, right), scalars=1)
     value = call(
         expert_kernel,
         sds((devices, capacity, HALF), bf16),
-        (spot, received, extra_rows, *near, staged, left, right, *facing),
+        (spot, received, extra_rows, *near, weights, left, right, *facing),
         scalars=1,
         scratch=tuple(pltpu.VMEM(part.shape, part.dtype) for part in parts),
     )

time: 196 us -> 182 us (0.929)
  starting transfers between devices: 79 us -> 60.2 us
  waiting for transfers between devices: 37 us -> 45.1 us
  local copies, waits for them, and re-layouts: 10.2 us -> 5.62 us
    ppermute x2 -> x0, starting transfers between devices: 10.6 us -> none  [the longest x1 8.67 us: shards(): lax.ppermute(choice, 'coarse', [(i, GROUP - 1 - i) for i in range(GROUP)])]
    ppermute x2 -> x0, waiting for transfers between devices: 8.82 us -> none  [the longest x1 7.74 us: shards(): paired = lax.ppermute(choice, 'coarse', [(i, i ^ 1) for i in range(GROUP)])]
    ppermute x1, waiting for transfers between devices: 0.01 us -> 8.59 us  [shards(): right = lax.ppermute(weights, 'coarse', back)]
    ppermute x1, waiting for transfers between devices: 0.01 us -> 4.9 us  [shards(): left = lax.ppermute(weights, 'coarse', ring)]
    unnamed x34 -> x20, local copies, waits for them, and re-layouts: 8.39 us -> 3.84 us
    all_to_all x2 -> x3, starting transfers between devices: 29.9 us -> 26.2 us  [exchange(): lax.all_to_all(array, axes, split_axis=0, concat_axis=0, tiled=True, **kw...]
    all_to_all x2 -> x3, waiting for transfers between devices: 25.4 us -> 27.9 us  [exchange(): lax.all_to_all(array, axes, split_axis=0, concat_axis=0, tiled=True, **kw...]
    ppermute x3, starting transfers between devices: 10.5 us -> 8.18 us  [shards(): state = state + lax.ppermute(outgoing, 'seq', pairs)]
  transfers between devices with their start and end apart: 14 -> 13, of which waited for: 6 -> 7; matrix products, arithmetic and copies ran while one was open for 1% -> 1% of each run, Pallas kernels for 3% -> 10%
where the time goes in v4:
time: 182 us; the launch traced here: 181 us
  starting transfers between devices  60.2 us (33%)
  waiting for transfers between devices  45.1 us (25%)
  blocking collectives  45.1 us (25%)
  Pallas kernels  24.5 us (13%)
  local copies, waits for them, and re-layouts  5.62 us (3%)
    all_to_all x1, blocking collectives, exchange(): lax.all_to_all(array, axes, split_axis=0, concat_axis=0, tiled=True, **kw...  45.1 us
    all_to_all x3, waiting for transfers between devices, exchange(): lax.all_to_all(array, axes, split_axis=0, concat_axis=0, tiled=True, **kw...  27.9 us
    all_to_all x3, starting transfers between devices, exchange(): lax.all_to_all(array, axes, split_axis=0, concat_axis=0, tiled=True, **kw...  26.2 us
    pallas_call x16, Pallas kernels, call(): pl.pallas_call(kernel, out_shape=outs, in_specs=[spec(far_in, i - scalars...  24.5 us
    ppermute x1, waiting for transfers between devices, shards(): right = lax.ppermute(weights, 'coarse', back)  8.59 us
    ppermute x3, starting transfers between devices, shards(): state = state + lax.ppermute(outgoing, 'seq', pairs)  8.18 us
    ppermute x1, starting transfers between devices, shards(): got = lax.ppermute(give, 'seq', swap)  7.05 us
    ppermute x1, waiting for transfers between devices, shards(): left = lax.ppermute(weights, 'coarse', ring)  4.9 us
  transfers between devices with their start and end apart: 13, of which 7 were waited for; matrix products, arithmetic and copies ran while one was open for 1% of the time, Pallas kernels for 10%

profile of v4, /device:TPU:1, one launch (start us, length us, event | category | flops | bytes accessed | tf_op | source)
XLA Modules:
  0.0 180.9 jit_solution(16692566260647987540)
XLA Ops:
  0.0 1.3 shard_map.137
  1.3 5.0 %all-to-all-start = ((f32[4,16,128]{2,1,0:T(8,128)}), f32[4,16,128]{2,1,0:T(8,128)S(1)}, u32[]{:S(2)}, u32[]{:S(2)}) async-start(f32[4,16,128]{2,1,0:T(8,128)} %shard_map.137), calls=%async_computation | async-start | bytes 65536 | tf_op jit(solution)/shard_map/all_to_all | solution.py:473
  6.3 0.0 copy-start.7
  6.3 13.4 %shard_map.136 = (f32[128,256]{1,0:T(8,128)}, f32[128,256]{1,0:T(8,128)}, f32[2,512,256]{2,1,0:T(8,128)}, bf16[512,256]{1,0:T(8,128)(2,1)}, bf16[512,1280]{1,0:T(8,128)(2,1)}) custom-call(bf16[512,1024]{1,0:T(8,128)(2,1)} %bitcast.19, f32[1,1024]{1,0:T(1,128)} %bitcast.21, bf16[3,1024,256]{2,1,0:T(8,128)(2,1)} %w_far.1, bf16[2,2,1024]{2,1,0:T(2,128)(2,1)} %bitcast.20, ...), custom_call_target="tpu_custom_call" | custom-call | flops 2000000000 | bytes 20000000 | tf_op jit(solution)/shard_map/pallas_call | solution.py:431
  19.7 0.0 all-to-all-done.choice_far.choice_ref
  19.7 7.0 %collective-permute-start = (f32[128,256]{1,0:T(8,128)}, f32[128,256]{1,0:T(8,128)S(1)}, u32[]{:S(2)}, u32[]{:S(2)}) collective-permute-start(f32[128,256]{1,0:T(8,128)} %shard_map.138), channel_id=1, source_target_pairs={{0,16},{16,0},{32,48},{48,32},{64,80},{80,64},{96,112},{112,96},{1... | collective-permute-start | bytes 393224 | tf_op jit(solution)/shard_map/ppermute | solution.py:523
  26.8 1.2 collective-permute-done.got_ref
  27.9 0.0 copy-start.6
  27.9 0.9 copy-done.6
  28.9 0.9 shard_map.139
  29.8 3.4 %all-to-all-start.1 = ((bf16[4,128,256]{2,1,0:T(8,128)(2,1)}), bf16[4,128,256]{2,1,0:T(8,128)(2,1)S(1)}, u32[]{:S(2)}, u32[]{:S(2)}) async-start(bf16[4,128,256]{2,1,0:T(8,128)(2,1)} %get-tuple-element.28), calls=%async_computation.1 | async-start | bytes 524288 | tf_op jit(solution)/shard_map/all_to_all | solution.py:473
  33.2 4.8 %collective-permute-start.6 = (bf16[512,1280]{1,0:T(8,128)(2,1)}, bf16[512,1280]{1,0:T(8,128)(2,1)S(1)}, u32[]{:S(2)}, u32[]{:S(2)}) collective-permute-start(bf16[512,1280]{1,0:T(8,128)(2,1)} %get-tuple-element.35.own_ref), channel_id=1, source_target_pairs={{4,0},{8,4},{12,8},{0,12},{5,1},{9,5},{13,9},{1,13},{6,2},{10,6},{... | collective-permute-start | bytes 3932168 | tf_op jit(solution)/shard_map/ppermute | solution.py:541
  38.0 1.9 %collective-permute-start.5 = (bf16[512,1280]{1,0:T(8,128)(2,1)}, bf16[512,1280]{1,0:T(8,128)(2,1)S(1)}, u32[]{:S(2)}, u32[]{:S(2)}) collective-permute-start(bf16[512,1280]{1,0:T(8,128)(2,1)} %get-tuple-element.35.own_ref), channel_id=1, source_target_pairs={{0,4},{4,8},{8,12},{12,0},{1,5},{5,9},{9,13},{13,1},{2,6},{6,10},{... | collective-permute-start | bytes 3932168 | tf_op jit(solution)/shard_map/ppermute | solution.py:540
  40.0 0.0 copy-done.7
  40.0 1.4 shard_map.140
  41.4 0.0 copy-start.2
  41.4 0.8 copy-done.2
  42.2 0.0 all-to-all-done.1.got_ref
  42.2 0.6 shard_map.141
  42.9 6.9 %collective-permute-start.1 = (bf16[128,128]{1,0:T(8,128)(2,1)S(1)}, bf16[128,128]{1,0:T(8,128)(2,1)S(1)}, u32[]{:S(2)}, u32[]{:S(2)}) collective-permute-start(bf16[128,128]{1,0:T(8,128)(2,1)S(1)} %slice.17), channel_id=1, source_target_pairs={{0,128},{16,144},{32,160},{48,176},{64,192},{80,208},{96,224},{112... | collective-permute-start | bytes 98312 | tf_op jit(solution)/shard_map/ppermute | solution.py:558
  49.7 1.0 collective-permute-done.1.state_ref
  50.7 0.2 shard_map.142
  50.9 0.7 collective-permute-start.2
  51.6 0.0 collective-permute-done.2
  51.6 0.2 shard_map.143
  51.8 0.7 collective-permute-start.3
  52.4 0.0 collective-permute-done.3
  52.5 0.0 copy-start.1
  52.5 0.0 copy-start.5
  52.5 0.0 copy-start.8
  52.5 0.4 shard_map.144.own_ref
  52.9 3.7 %collective-permute-start.4 = (f32[2,128,128]{2,1,0:T(8,128)S(1)}, f32[2,128,128]{2,1,0:T(8,128)S(1)}, u32[]{:S(2)}, u32[]{:S(2)}) collective-permute-start(f32[2,128,128]{2,1,0:T(8,128)S(1)} %shard_map.144.own_ref), channel_id=1, source_target_pairs={{0,16},{16,0},{32,48},{48,32},{64,80},{80,64},{96,112},{112,96},{1... | collective-permute-start | bytes 393224 | tf_op jit(solution)/shard_map/ppermute | solution.py:560
  56.6 0.2 shard_map.145.rank_ref
  56.7 0.8 collective-permute-done.4.got_ref
  57.5 8.6 %collective-permute-done.6.right_far.right_ref = bf16[512,1280]{1,0:T(8,128)(2,1)S(1)} collective-permute-done((bf16[512,1280]{1,0:T(8,128)(2,1)}, bf16[512,1280]{1,0:T(8,128)(2,1)S(1)}, u32[]{:S(2)}, u32[]{:S(2)}) %collective-permute-start.6) | collective-permute-done | bytes 1310752 | tf_op jit(solution)/shard_map/ppermute | solution.py:541
  66.1 4.9 %collective-permute-done.5.left_far.left_ref = bf16[512,1280]{1,0:T(8,128)(2,1)S(1)} collective-permute-done((bf16[512,1280]{1,0:T(8,128)(2,1)}, bf16[512,1280]{1,0:T(8,128)(2,1)S(1)}, u32[]{:S(2)}, u32[]{:S(2)}) %collective-permute-start.5) | collective-permute-done | bytes 1310752 | tf_op jit(solution)/shard_map/ppermute | solution.py:540
  71.0 0.0 copy-done.1
  71.0 0.0 copy-done.5
  71.0 0.0 copy-done.8
  71.0 1.0 shard_map.146
  72.0 0.0 copy-start.4
  72.0 0.8 copy-done.4
  72.8 17.8 %all-to-all-start.2 = ((bf16[512,2,256]{2,1,0:T(2,128)(2,1)}), bf16[512,2,256]{2,1,0:T(2,128)(2,1)S(1)}, u32[]{:S(2)}, u32[]{:S(2)}) async-start(bf16[512,2,256]{2,1,0:T(2,128)(2,1)} %copy-done.4), calls=%async_computation.2 | async-start | bytes 1048576 | tf_op jit(solution)/shard_map/all_to_all | solution.py:473
  90.6 0.0 copy-start.9
  90.6 0.9 slice.15
  91.5 4.5 %collective-permute-start.8 = (bf16[256,1280]{1,0:T(8,128)(2,1)}, bf16[256,1280]{1,0:T(8,128)(2,1)}, u32[]{:S(2)}, u32[]{:S(2)}) collective-permute-start(bf16[256,1280]{1,0:T(8,128)(2,1)} %slice.15), channel_id=1, source_target_pairs={{4,0},{8,4},{12,8},{0,12},{5,1},{9,5},{13,9},{1,13},{6,2},{10,6},{... | collective-permute-start | bytes 1966088 | tf_op jit(solution)/shard_map/ppermute | solution.py:542
  96.1 0.9 slice.14
  96.9 1.9 %collective-permute-start.7 = (bf16[256,1280]{1,0:T(8,128)(2,1)}, bf16[256,1280]{1,0:T(8,128)(2,1)}, u32[]{:S(2)}, u32[]{:S(2)}) collective-permute-start(bf16[256,1280]{1,0:T(8,128)(2,1)} %slice.14), channel_id=1, source_target_pairs={{0,4},{4,8},{8,12},{12,0},{1,5},{5,9},{9,13},{13,1},{2,6},{6,10},{... | collective-permute-start | bytes 1966088 | tf_op jit(solution)/shard_map/ppermute | solution.py:542
  98.9 0.0 copy-done.9
  98.9 27.9 %all-to-all-done.2.rows_ref = bf16[512,2,256]{2,1,0:T(2,128)(2,1)S(1)} async-done(((bf16[512,2,256]{2,1,0:T(2,128)(2,1)}), bf16[512,2,256]{2,1,0:T(2,128)(2,1)S(1)}, u32[]{:S(2)}, u32[]{:S(2)}) %all-to-all-start.2) | async-done | bytes 524320 | tf_op jit(solution)/shard_map/all_to_all | solution.py:473
  126.7 0.0 copy-start
  126.7 1.3 copy-done
  128.1 1.2 shard_map.147
  129.3 0.0 collective-permute-done.8.lower_ref
  129.3 0.0 collective-permute-done.7.upper_ref
  129.3 2.3 %shard_map.148 = bf16[512,2,256]{2,1,0:T(2,128)(2,1)S(1)} custom-call(s32[1]{0:T(128)} %bitcast.12.coarse_ref, bf16[512,2,256]{2,1,0:T(2,128)(2,1)S(1)} %all-to-all-done.2.rows_ref, bf16[4,1,256]{2,1,0:T(2,128)(2,1)S(1)} %reshape.4.ext_ref, f32[256,1024]{1,0:T(8,128)S(1)} %get-tuple-element.39.near_ref, f32[16,1024]{1,0:T(8,128)S(1)} %get-tuple-element.40.near_offset_ref, ...), custom_call_target="tpu_custom_call" | custom-call | flops 100000 | bytes 1000 | tf_op jit(solution)/shard_map/pallas_call | solution.py:431
  131.6 0.0 copy-start.3
  131.6 45.1 %all_to_all.20.back_ref = bf16[512,2,256]{2,1,0:T(2,128)(2,1)S(1)} all-to-all(bf16[512,2,256]{2,1,0:T(2,128)(2,1)S(1)} %shard_map.148), channel_id=1, replica_groups=mesh['seq'=32,'coarse'=4,'exp'=4] {'coarse','seq','exp'}, dimensions={0} | all-to-all | bytes 1048576 | tf_op jit(solution)/shard_map/all_to_all | solution.py:473
  176.6 0.0 copy-done.3
  176.6 0.4 shard_map.149
  177.0 1.9 %collective-permute-start.9 = (f32[1,256]{1,0:T(1,128)S(1)}, f32[1,256]{1,0:T(1,128)S(1)}, u32[]{:S(2)}, u32[]{:S(2)}) collective-permute-start(f32[1,256]{1,0:T(1,128)S(1)} %get-tuple-element.44), channel_id=1, source_target_pairs={{0,16},{16,32},{32,48},{48,64},{64,80},{80,96},{96,112},{112,128},... | collective-permute-start | bytes 3080 | tf_op jit(solution)/shard_map/ppermute | solution.py:588
  179.0 0.3 shard_map.150
  179.3 0.8 collective-permute-done.9.prev_ref
  180.1 0.8 shard_map.151
  (5 shorter events, 0.0 us)
Async XLA Ops:
  1.3 18.4 %all-to-all-start = ((f32[4,16,128]{2,1,0:T(8,128)}), f32[4,16,128]{2,1,0:T(8,128)S(1)}, u32[]{:S(2)}, u32[]{:S(2)}) async-start(f32[4,16,128]{2,1,0:T(8,128)} %shard_map.137), calls=%async_computation | async-start | bytes 65536 | tf_op jit(solution)/shard_map/all_to_all | solution.py:473
  6.3 33.7 %copy-start.7 = (s32[1,512]{1,0:T(1,128)S(1)}, s32[1,512]{1,0:T(1,128)}, u32[]{:S(2)}) copy-start(s32[1,512]{1,0:T(1,128)} %mask_ref.7) | copy-start | bytes 6148
  19.7 8.2 %collective-permute-start = (f32[128,256]{1,0:T(8,128)}, f32[128,256]{1,0:T(8,128)S(1)}, u32[]{:S(2)}, u32[]{:S(2)}) collective-permute-start(f32[128,256]{1,0:T(8,128)} %shard_map.138), channel_id=1, source_target_pairs={{0,16},{16,0},{32,48},{48,32},{64,80},{80,64},{96,112},{112,96},{1... | collective-permute-start | bytes 393224 | tf_op jit(solution)/shard_map/ppermute | solution.py:523
  27.9 0.9 copy-start.6
  29.8 12.4 %all-to-all-start.1 = ((bf16[4,128,256]{2,1,0:T(8,128)(2,1)}), bf16[4,128,256]{2,1,0:T(8,128)(2,1)S(1)}, u32[]{:S(2)}, u32[]{:S(2)}) async-start(bf16[4,128,256]{2,1,0:T(8,128)(2,1)} %get-tuple-element.28), calls=%async_computation.1 | async-start | bytes 524288 | tf_op jit(solution)/shard_map/all_to_all | solution.py:473
  33.2 32.9 %collective-permute-start.6 = (bf16[512,1280]{1,0:T(8,128)(2,1)}, bf16[512,1280]{1,0:T(8,128)(2,1)S(1)}, u32[]{:S(2)}, u32[]{:S(2)}) collective-permute-start(bf16[512,1280]{1,0:T(8,128)(2,1)} %get-tuple-element.35.own_ref), channel_id=1, source_target_pairs={{4,0},{8,4},{12,8},{0,12},{5,1},{9,5},{13,9},{1,13},{6,2},{10,6},{... | collective-permute-start | bytes 3932168 | tf_op jit(solution)/shard_map/ppermute | solution.py:541
  38.0 33.0 %collective-permute-start.5 = (bf16[512,1280]{1,0:T(8,128)(2,1)}, bf16[512,1280]{1,0:T(8,128)(2,1)S(1)}, u32[]{:S(2)}, u32[]{:S(2)}) collective-permute-start(bf16[512,1280]{1,0:T(8,128)(2,1)} %get-tuple-element.35.own_ref), channel_id=1, source_target_pairs={{0,4},{4,8},{8,12},{12,0},{1,5},{5,9},{9,13},{13,1},{2,6},{6,10},{... | collective-permute-start | bytes 3932168 | tf_op jit(solution)/shard_map/ppermute | solution.py:540
  41.4 0.8 copy-start.2
  42.9 7.9 %collective-permute-start.1 = (bf16[128,128]{1,0:T(8,128)(2,1)S(1)}, bf16[128,128]{1,0:T(8,128)(2,1)S(1)}, u32[]{:S(2)}, u32[]{:S(2)}) collective-permute-start(bf16[128,128]{1,0:T(8,128)(2,1)S(1)} %slice.17), channel_id=1, source_target_pairs={{0,128},{16,144},{32,160},{48,176},{64,192},{80,208},{96,224},{112... | collective-permute-start | bytes 98312 | tf_op jit(solution)/shard_map/ppermute | solution.py:558
  50.9 0.7 collective-permute-start.2
  51.8 0.7 collective-permute-start.3
  52.5 18.6 %copy-start.1 = (f32[2,512,256]{2,1,0:T(8,128)S(1)}, f32[2,512,256]{2,1,0:T(8,128)}, u32[]{:S(2)}) copy-start(f32[2,512,256]{2,1,0:T(8,128)} %get-tuple-element.25.local_ref) | copy-start | bytes 3145732
  52.5 18.5 %copy-start.5 = (bf16[512,256]{1,0:T(8,128)(2,1)S(1)}, bf16[512,256]{1,0:T(8,128)(2,1)}, u32[]{:S(2)}) copy-start(bf16[512,256]{1,0:T(8,128)(2,1)} %get-tuple-element.33.x_ref) | copy-start | bytes 786436
  52.5 18.5 %copy-start.8 = (f32[256]{0:T(256)S(1)}, f32[256]{0:T(256)}, u32[]{:S(2)}) copy-start(f32[256]{0:T(256)} %param.20) | copy-start | bytes 3076
  52.9 4.7 %collective-permute-start.4 = (f32[2,128,128]{2,1,0:T(8,128)S(1)}, f32[2,128,128]{2,1,0:T(8,128)S(1)}, u32[]{:S(2)}, u32[]{:S(2)}) collective-permute-start(f32[2,128,128]{2,1,0:T(8,128)S(1)} %shard_map.144.own_ref), channel_id=1, source_target_pairs={{0,16},{16,0},{32,48},{48,32},{64,80},{80,64},{96,112},{112,96},{1... | collective-permute-start | bytes 393224 | tf_op jit(solution)/shard_map/ppermute | solution.py:560
  72.0 0.8 copy-start.4
  72.8 53.9 %all-to-all-start.2 = ((bf16[512,2,256]{2,1,0:T(2,128)(2,1)}), bf16[512,2,256]{2,1,0:T(2,128)(2,1)S(1)}, u32[]{:S(2)}, u32[]{:S(2)}) async-start(bf16[512,2,256]{2,1,0:T(2,128)(2,1)} %copy-done.4), calls=%async_computation.2 | async-start | bytes 1048576 | tf_op jit(solution)/shard_map/all_to_all | solution.py:473
  90.6 8.3 %copy-start.9 = (bf16[1024]{0:T(1024)(128)(2,1)S(1)}, bf16[1024]{0:T(1024)(128)(2,1)}, u32[]{:S(2)}) copy-start(bf16[1024]{0:T(1024)(128)(2,1)} %param.24) | copy-start | bytes 6148
  91.5 37.8 %collective-permute-start.8 = (bf16[256,1280]{1,0:T(8,128)(2,1)}, bf16[256,1280]{1,0:T(8,128)(2,1)}, u32[]{:S(2)}, u32[]{:S(2)}) collective-permute-start(bf16[256,1280]{1,0:T(8,128)(2,1)} %slice.15), channel_id=1, source_target_pairs={{4,0},{8,4},{12,8},{0,12},{5,1},{9,5},{13,9},{1,13},{6,2},{10,6},{... | collective-permute-start | bytes 1966088 | tf_op jit(solution)/shard_map/ppermute | solution.py:542
  96.9 32.3 %collective-permute-start.7 = (bf16[256,1280]{1,0:T(8,128)(2,1)}, bf16[256,1280]{1,0:T(8,128)(2,1)}, u32[]{:S(2)}, u32[]{:S(2)}) collective-permute-start(bf16[256,1280]{1,0:T(8,128)(2,1)} %slice.14), channel_id=1, source_target_pairs={{0,4},{4,8},{8,12},{12,0},{1,5},{5,9},{9,13},{13,1},{2,6},{6,10},{... | collective-permute-start | bytes 1966088 | tf_op jit(solution)/shard_map/ppermute | solution.py:542
  126.7 1.3 copy-start
  131.6 45.1 %copy-start.3 = (f32[4,256,32]{2,1,0:T(8,128)S(1)}, f32[4,256,32]{2,1,0:T(8,128)}, u32[]{:S(2)}) copy-start(f32[4,256,32]{2,1,0:T(8,128)} %copy-done.2) | copy-start | bytes 393220
  177.0 3.0 %collective-permute-start.9 = (f32[1,256]{1,0:T(1,128)S(1)}, f32[1,256]{1,0:T(1,128)S(1)}, u32[]{:S(2)}, u32[]{:S(2)}) collective-permute-start(f32[1,256]{1,0:T(1,128)S(1)} %get-tuple-element.44), channel_id=1, source_target_pairs={{0,16},{16,32},{32,48},{48,64},{64,80},{80,96},{96,112},{112,128},... | collective-permute-start | bytes 3080 | tf_op jit(solution)/shard_map/ppermute | solution.py:588

commit v5 on v4

--- a/solution.py
+++ b/solution.py
@@ -168,7 +168,7 @@
         out = mm(left, jnp.concatenate([wide, wide], axis=0))
         return out[:, :dim] + out[:, dim:]
 
-    def level(step, carry):
+    def level(step):
         r, c = iota((dim, HALF), 0), iota((dim, HALF), 1) & (dim - 1)
         above = ((r >> (step + 1)) == (c >> (step + 1))) & ((r >> step) > (c >> step))
         zero = jnp.zeros((dim, HALF), bf16)
@@ -176,9 +176,9 @@
         inside = [packed(jnp.where(above, low[m], zero), blocks[m]) for m in range(8)]
         for m in range(8):
             inv[m] = blocks[m] - packed(jnp.concatenate(split(blocks[m]), axis=1), inside[m])
-        return carry
-
-    lax.fori_loop(1, 7, level, 0)
+
+    for step in range(1, 7):
+        level(step)
     for head in range(2):
         cross, inner, right, k_end, scale, attend, grown = keep[head]
         full = []
@@ -225,8 +225,7 @@
         msg_ref[chip] = message
 
 
-def group_kernel(place_ref, got_ref, token_ref, before_ref, total_ref):
-    del token_ref
+def group_kernel(place_ref, got_ref, before_ref, total_ref):
     dim = HALF // 2
     eye = jnp.where(iota((dim, HALF), 0) == iota((dim, HALF), 1), 1.0, 0.0)
     place = place_ref[0]
@@ -241,7 +240,8 @@
     total_ref[...] = running
 
 
-def hop_kernel(total_ref, state_ref, out_ref):
+def hop_kernel(total_ref, state_ref, token_ref, out_ref):
+    del token_ref
     dim = HALF // 2
     moved = mm3(split(total_ref[:, :dim]), split(state_ref[...].astype(f32)))
     out_ref[...] = (moved + total_ref[:, dim:]).astype(bf16)
@@ -546,14 +546,14 @@
     ]
     chips = exchange(message, "seq", axis_index_groups=groups)
     before, total = call(
-        group_kernel, (sds((dim, HALF), f32), sds((dim, HALF), f32)), (place, chips, routed), scalars=1, flops=10**9
+        group_kernel, (sds((dim, HALF), f32), sds((dim, HALF), f32)), (place, chips), scalars=1, flops=10**9
     )
     state = jnp.zeros((dim, dim), bf16)
     for hop in range(seq_total // stride - 1):
         if hop == 0:
             outgoing = total[:, dim:].astype(bf16)
         else:
-            outgoing = call(hop_kernel, sds((dim, dim), bf16), (total, state), flops=10**9)
+            outgoing = call(hop_kernel, sds((dim, dim), bf16), (total, state, routed), flops=10**9)
         pairs = [(stride * hop + i, stride * (hop + 1) + i) for i in range(stride)]
         state = state + lax.ppermute(outgoing, "seq", pairs)
     states = call(enter_kernel, sds((2, dim, dim), f32), (core, before, first, state), scalars=1, flops=10**9)

time: 182 us -> 180 us (0.989)
  transfers between devices with their start and end apart: 13 -> 13, of which waited for: 7 -> 7; matrix products, arithmetic and copies ran while one was open for 1% -> 1% of each run, Pallas kernels for 10% -> 9%
where the time goes in v5:
time: 180 us
  starting transfers between devices  61.5 us (34%)
  blocking collectives  45.1 us (25%)
  waiting for transfers between devices  43.8 us (24%)
  Pallas kernels  23.3 us (13%)
  local copies, waits for them, and re-layouts  5.62 us (3%)
    all_to_all x1, blocking collectives, exchange(): lax.all_to_all(array, axes, split_axis=0, concat_axis=0, tiled=True, **kw...  45.1 us
    all_to_all x3, waiting for transfers between devices, exchange(): lax.all_to_all(array, axes, split_axis=0, concat_axis=0, tiled=True, **kw...  28.5 us
    all_to_all x3, starting transfers between devices, exchange(): lax.all_to_all(array, axes, split_axis=0, concat_axis=0, tiled=True, **kw...  26.2 us
    pallas_call x16, Pallas kernels, call(): pl.pallas_call(kernel, out_shape=outs, in_specs=[spec(far_in, i - scalars...  23.3 us
    ppermute x3, starting transfers between devices, shards(): state = state + lax.ppermute(outgoing, 'seq', pairs)  8.18 us
    ppermute x1, waiting for transfers between devices, shards(): right = lax.ppermute(weights, 'coarse', back)  7.92 us
    ppermute x1, starting transfers between devices, shards(): got = lax.ppermute(give, 'seq', swap)  7.04 us
    ppermute x1, starting transfers between devices, shards(): others = lax.ppermute(states, 'seq', swap)  4.95 us
  transfers between devices with their start and end apart: 13, of which 7 were waited for; matrix products, arithmetic and copies ran while one was open for 1% of the time, Pallas kernels for 9%

profile of v5, /device:TPU:1, one launch (start us, length us, event | category | flops | bytes accessed | tf_op | source)
XLA Modules:
  0.0 179.7 jit_solution(4826000980441521)
XLA Ops:
  0.0 1.3 shard_map.137
  1.3 5.0 %all-to-all-start = ((f32[4,16,128]{2,1,0:T(8,128)}), f32[4,16,128]{2,1,0:T(8,128)S(1)}, u32[]{:S(2)}, u32[]{:S(2)}) async-start(f32[4,16,128]{2,1,0:T(8,128)} %shard_map.137), calls=%async_computation | async-start | bytes 65536 | tf_op jit(solution)/shard_map/all_to_all | solution.py:473
  6.3 12.2 %shard_map.136 = (f32[128,256]{1,0:T(8,128)}, f32[128,256]{1,0:T(8,128)}, f32[2,512,256]{2,1,0:T(8,128)}, bf16[512,256]{1,0:T(8,128)(2,1)}, bf16[512,1280]{1,0:T(8,128)(2,1)}) custom-call(bf16[512,1024]{1,0:T(8,128)(2,1)} %bitcast.19, f32[1,1024]{1,0:T(1,128)} %bitcast.21, bf16[3,1024,256]{2,1,0:T(8,128)(2,1)} %w_far.1, bf16[2,2,1024]{2,1,0:T(2,128)(2,1)} %bitcast.20, ...), custom_call_target="tpu_custom_call" | custom-call | flops 2000000000 | bytes 20000000 | tf_op jit(solution)/shard_map/pallas_call | solution.py:431
  18.5 0.0 all-to-all-done.choice_far.choice_ref
  18.6 7.0 %collective-permute-start = (f32[128,256]{1,0:T(8,128)}, f32[128,256]{1,0:T(8,128)S(1)}, u32[]{:S(2)}, u32[]{:S(2)}) collective-permute-start(f32[128,256]{1,0:T(8,128)} %shard_map.138), channel_id=1, source_target_pairs={{0,16},{16,0},{32,48},{48,32},{64,80},{80,64},{96,112},{112,96},{1... | collective-permute-start | bytes 393224 | tf_op jit(solution)/shard_map/ppermute | solution.py:523
  25.6 1.2 collective-permute-done.got_ref
  26.8 0.0 copy-start.6
  26.8 0.9 copy-done.6
  27.7 0.9 shard_map.139
  28.6 3.4 %all-to-all-start.1 = ((bf16[4,128,256]{2,1,0:T(8,128)(2,1)}), bf16[4,128,256]{2,1,0:T(8,128)(2,1)S(1)}, u32[]{:S(2)}, u32[]{:S(2)}) async-start(bf16[4,128,256]{2,1,0:T(8,128)(2,1)} %get-tuple-element.28), calls=%async_computation.1 | async-start | bytes 524288 | tf_op jit(solution)/shard_map/all_to_all | solution.py:473
  32.0 4.8 %collective-permute-start.6 = (bf16[512,1280]{1,0:T(8,128)(2,1)}, bf16[512,1280]{1,0:T(8,128)(2,1)S(1)}, u32[]{:S(2)}, u32[]{:S(2)}) collective-permute-start(bf16[512,1280]{1,0:T(8,128)(2,1)} %get-tuple-element.35.own_ref), channel_id=1, source_target_pairs={{4,0},{8,4},{12,8},{0,12},{5,1},{9,5},{13,9},{1,13},{6,2},{10,6},{... | collective-permute-start | bytes 3932168 | tf_op jit(solution)/shard_map/ppermute | solution.py:541
  36.9 1.9 %collective-permute-start.5 = (bf16[512,1280]{1,0:T(8,128)(2,1)}, bf16[512,1280]{1,0:T(8,128)(2,1)S(1)}, u32[]{:S(2)}, u32[]{:S(2)}) collective-permute-start(bf16[512,1280]{1,0:T(8,128)(2,1)} %get-tuple-element.35.own_ref), channel_id=1, source_target_pairs={{0,4},{4,8},{8,12},{12,0},{1,5},{5,9},{9,13},{13,1},{2,6},{6,10},{... | collective-permute-start | bytes 3932168 | tf_op jit(solution)/shard_map/ppermute | solution.py:540
  38.8 0.6 all-to-all-done.1.got_ref
  39.4 0.0 copy-start.7
  39.4 0.6 shard_map.140
  40.1 6.9 %collective-permute-start.1 = (bf16[128,128]{1,0:T(8,128)(2,1)S(1)}, bf16[128,128]{1,0:T(8,128)(2,1)S(1)}, u32[]{:S(2)}, u32[]{:S(2)}) collective-permute-start(bf16[128,128]{1,0:T(8,128)(2,1)S(1)} %slice.17), channel_id=1, source_target_pairs={{0,128},{16,144},{32,160},{48,176},{64,192},{80,208},{96,224},{112... | collective-permute-start | bytes 98312 | tf_op jit(solution)/shard_map/ppermute | solution.py:558
  47.0 0.0 copy-done.7
  47.0 1.4 shard_map.141
  48.3 0.0 copy-start.2
  48.4 0.8 copy-done.2
  49.1 0.0 collective-permute-done.1.state_ref
  49.1 0.2 shard_map.142
  49.3 0.7 collective-permute-start.2
  50.0 0.0 collective-permute-done.2
  50.0 0.2 shard_map.143
  50.2 0.7 collective-permute-start.3
  50.9 0.0 collective-permute-done.3
  50.9 0.0 copy-start.1
  50.9 0.0 copy-start.5
  50.9 0.0 copy-start.8
  50.9 0.4 shard_map.144.own_ref
  51.3 5.0 %collective-permute-start.4 = (f32[2,128,128]{2,1,0:T(8,128)S(1)}, f32[2,128,128]{2,1,0:T(8,128)S(1)}, u32[]{:S(2)}, u32[]{:S(2)}) collective-permute-start(f32[2,128,128]{2,1,0:T(8,128)S(1)} %shard_map.144.own_ref), channel_id=1, source_target_pairs={{0,16},{16,0},{32,48},{48,32},{64,80},{80,64},{96,112},{112,96},{1... | collective-permute-start | bytes 393224 | tf_op jit(solution)/shard_map/ppermute | solution.py:560
  56.3 0.2 shard_map.145.rank_ref
  56.4 0.6 collective-permute-done.4.got_ref
  57.0 7.9 %collective-permute-done.6.right_far.right_ref = bf16[512,1280]{1,0:T(8,128)(2,1)S(1)} collective-permute-done((bf16[512,1280]{1,0:T(8,128)(2,1)}, bf16[512,1280]{1,0:T(8,128)(2,1)S(1)}, u32[]{:S(2)}, u32[]{:S(2)}) %collective-permute-start.6) | collective-permute-done | bytes 1310752 | tf_op jit(solution)/shard_map/ppermute | solution.py:541
  65.0 4.9 %collective-permute-done.5.left_far.left_ref = bf16[512,1280]{1,0:T(8,128)(2,1)S(1)} collective-permute-done((bf16[512,1280]{1,0:T(8,128)(2,1)}, bf16[512,1280]{1,0:T(8,128)(2,1)S(1)}, u32[]{:S(2)}, u32[]{:S(2)}) %collective-permute-start.5) | collective-permute-done | bytes 1310752 | tf_op jit(solution)/shard_map/ppermute | solution.py:540
  69.9 0.0 copy-done.1
  69.9 0.0 copy-done.5
  69.9 0.0 copy-done.8
  69.9 1.0 shard_map.146
  70.8 0.0 copy-start.4
  70.9 0.8 copy-done.4
  71.7 17.8 %all-to-all-start.2 = ((bf16[512,2,256]{2,1,0:T(2,128)(2,1)}), bf16[512,2,256]{2,1,0:T(2,128)(2,1)S(1)}, u32[]{:S(2)}, u32[]{:S(2)}) async-start(bf16[512,2,256]{2,1,0:T(2,128)(2,1)} %copy-done.4), calls=%async_computation.2 | async-start | bytes 1048576 | tf_op jit(solution)/shard_map/all_to_all | solution.py:473
  89.4 0.0 copy-start.9
  89.5 0.9 slice.15
  90.3 4.5 %collective-permute-start.8 = (bf16[256,1280]{1,0:T(8,128)(2,1)}, bf16[256,1280]{1,0:T(8,128)(2,1)}, u32[]{:S(2)}, u32[]{:S(2)}) collective-permute-start(bf16[256,1280]{1,0:T(8,128)(2,1)} %slice.15), channel_id=1, source_target_pairs={{4,0},{8,4},{12,8},{0,12},{5,1},{9,5},{13,9},{1,13},{6,2},{10,6},{... | collective-permute-start | bytes 1966088 | tf_op jit(solution)/shard_map/ppermute | solution.py:542
  94.9 0.9 slice.14
  95.8 1.9 %collective-permute-start.7 = (bf16[256,1280]{1,0:T(8,128)(2,1)}, bf16[256,1280]{1,0:T(8,128)(2,1)}, u32[]{:S(2)}, u32[]{:S(2)}) collective-permute-start(bf16[256,1280]{1,0:T(8,128)(2,1)} %slice.14), channel_id=1, source_target_pairs={{0,4},{4,8},{8,12},{12,0},{1,5},{5,9},{9,13},{13,1},{2,6},{6,10},{... | collective-permute-start | bytes 1966088 | tf_op jit(solution)/shard_map/ppermute | solution.py:542
  97.7 0.0 copy-done.9
  97.7 27.9 %all-to-all-done.2.rows_ref = bf16[512,2,256]{2,1,0:T(2,128)(2,1)S(1)} async-done(((bf16[512,2,256]{2,1,0:T(2,128)(2,1)}), bf16[512,2,256]{2,1,0:T(2,128)(2,1)S(1)}, u32[]{:S(2)}, u32[]{:S(2)}) %all-to-all-start.2) | async-done | bytes 524320 | tf_op jit(solution)/shard_map/all_to_all | solution.py:473
  125.6 0.0 copy-start
  125.6 1.3 copy-done
  126.9 1.2 shard_map.147
  128.1 0.0 collective-permute-done.8.lower_ref
  128.1 0.0 collective-permute-done.7.upper_ref
  128.1 2.2 %shard_map.148 = bf16[512,2,256]{2,1,0:T(2,128)(2,1)S(1)} custom-call(s32[1]{0:T(128)} %bitcast.12.coarse_ref, bf16[512,2,256]{2,1,0:T(2,128)(2,1)S(1)} %all-to-all-done.2.rows_ref, bf16[4,1,256]{2,1,0:T(2,128)(2,1)S(1)} %reshape.4.ext_ref, f32[256,1024]{1,0:T(8,128)S(1)} %get-tuple-element.39.near_ref, f32[16,1024]{1,0:T(8,128)S(1)} %get-tuple-element.40.near_offset_ref, ...), custom_call_target="tpu_custom_call" | custom-call | flops 100000 | bytes 1000 | tf_op jit(solution)/shard_map/pallas_call | solution.py:431
  130.4 0.0 copy-start.3
  130.4 45.1 %all_to_all.20.back_ref = bf16[512,2,256]{2,1,0:T(2,128)(2,1)S(1)} all-to-all(bf16[512,2,256]{2,1,0:T(2,128)(2,1)S(1)} %shard_map.148), channel_id=1, replica_groups=mesh['seq'=32,'coarse'=4,'exp'=4] {'coarse','seq','exp'}, dimensions={0} | all-to-all | bytes 1048576 | tf_op jit(solution)/shard_map/all_to_all | solution.py:473
  175.5 0.0 copy-done.3
  175.5 0.4 shard_map.149
  175.8 1.9 %collective-permute-start.9 = (f32[1,256]{1,0:T(1,128)S(1)}, f32[1,256]{1,0:T(1,128)S(1)}, u32[]{:S(2)}, u32[]{:S(2)}) collective-permute-start(f32[1,256]{1,0:T(1,128)S(1)} %get-tuple-element.44), channel_id=1, source_target_pairs={{0,16},{16,32},{32,48},{48,64},{64,80},{80,96},{96,112},{112,128},... | collective-permute-start | bytes 3080 | tf_op jit(solution)/shard_map/ppermute | solution.py:588
  177.8 0.3 shard_map.150
  178.1 0.8 collective-permute-done.9.prev_ref
  178.9 0.8 shard_map.151
  (5 shorter events, 0.0 us)
Async XLA Ops:
  1.3 17.2 %all-to-all-start = ((f32[4,16,128]{2,1,0:T(8,128)}), f32[4,16,128]{2,1,0:T(8,128)S(1)}, u32[]{:S(2)}, u32[]{:S(2)}) async-start(f32[4,16,128]{2,1,0:T(8,128)} %shard_map.137), calls=%async_computation | async-start | bytes 65536 | tf_op jit(solution)/shard_map/all_to_all | solution.py:473
  18.6 8.2 %collective-permute-start = (f32[128,256]{1,0:T(8,128)}, f32[128,256]{1,0:T(8,128)S(1)}, u32[]{:S(2)}, u32[]{:S(2)}) collective-permute-start(f32[128,256]{1,0:T(8,128)} %shard_map.138), channel_id=1, source_target_pairs={{0,16},{16,0},{32,48},{48,32},{64,80},{80,64},{96,112},{112,96},{1... | collective-permute-start | bytes 393224 | tf_op jit(solution)/shard_map/ppermute | solution.py:523
  26.8 0.9 copy-start.6
  28.6 10.8 %all-to-all-start.1 = ((bf16[4,128,256]{2,1,0:T(8,128)(2,1)}), bf16[4,128,256]{2,1,0:T(8,128)(2,1)S(1)}, u32[]{:S(2)}, u32[]{:S(2)}) async-start(bf16[4,128,256]{2,1,0:T(8,128)(2,1)} %get-tuple-element.28), calls=%async_computation.1 | async-start | bytes 524288 | tf_op jit(solution)/shard_map/all_to_all | solution.py:473
  32.0 32.9 %collective-permute-start.6 = (bf16[512,1280]{1,0:T(8,128)(2,1)}, bf16[512,1280]{1,0:T(8,128)(2,1)S(1)}, u32[]{:S(2)}, u32[]{:S(2)}) collective-permute-start(bf16[512,1280]{1,0:T(8,128)(2,1)} %get-tuple-element.35.own_ref), channel_id=1, source_target_pairs={{4,0},{8,4},{12,8},{0,12},{5,1},{9,5},{13,9},{1,13},{6,2},{10,6},{... | collective-permute-start | bytes 3932168 | tf_op jit(solution)/shard_map/ppermute | solution.py:541
  36.9 33.0 %collective-permute-start.5 = (bf16[512,1280]{1,0:T(8,128)(2,1)}, bf16[512,1280]{1,0:T(8,128)(2,1)S(1)}, u32[]{:S(2)}, u32[]{:S(2)}) collective-permute-start(bf16[512,1280]{1,0:T(8,128)(2,1)} %get-tuple-element.35.own_ref), channel_id=1, source_target_pairs={{0,4},{4,8},{8,12},{12,0},{1,5},{5,9},{9,13},{13,1},{2,6},{6,10},{... | collective-permute-start | bytes 3932168 | tf_op jit(solution)/shard_map/ppermute | solution.py:540
  39.4 7.5 %copy-start.7 = (s32[1,512]{1,0:T(1,128)S(1)}, s32[1,512]{1,0:T(1,128)}, u32[]{:S(2)}) copy-start(s32[1,512]{1,0:T(1,128)} %mask_ref.7) | copy-start | bytes 6148
  40.1 9.0 %collective-permute-start.1 = (bf16[128,128]{1,0:T(8,128)(2,1)S(1)}, bf16[128,128]{1,0:T(8,128)(2,1)S(1)}, u32[]{:S(2)}, u32[]{:S(2)}) collective-permute-start(bf16[128,128]{1,0:T(8,128)(2,1)S(1)} %slice.17), channel_id=1, source_target_pairs={{0,128},{16,144},{32,160},{48,176},{64,192},{80,208},{96,224},{112... | collective-permute-start | bytes 98312 | tf_op jit(solution)/shard_map/ppermute | solution.py:558
  48.3 0.8 copy-start.2
  49.3 0.7 collective-permute-start.2
  50.2 0.7 collective-permute-start.3
  50.9 19.0 %copy-start.1 = (f32[2,512,256]{2,1,0:T(8,128)S(1)}, f32[2,512,256]{2,1,0:T(8,128)}, u32[]{:S(2)}) copy-start(f32[2,512,256]{2,1,0:T(8,128)} %get-tuple-element.25.local_ref) | copy-start | bytes 3145732
  50.9 19.0 %copy-start.5 = (bf16[512,256]{1,0:T(8,128)(2,1)S(1)}, bf16[512,256]{1,0:T(8,128)(2,1)}, u32[]{:S(2)}) copy-start(bf16[512,256]{1,0:T(8,128)(2,1)} %get-tuple-element.33.x_ref) | copy-start | bytes 786436
  50.9 19.0 %copy-start.8 = (f32[256]{0:T(256)S(1)}, f32[256]{0:T(256)}, u32[]{:S(2)}) copy-start(f32[256]{0:T(256)} %param.20) | copy-start | bytes 3076
  51.3 5.7 %collective-permute-start.4 = (f32[2,128,128]{2,1,0:T(8,128)S(1)}, f32[2,128,128]{2,1,0:T(8,128)S(1)}, u32[]{:S(2)}, u32[]{:S(2)}) collective-permute-start(f32[2,128,128]{2,1,0:T(8,128)S(1)} %shard_map.144.own_ref), channel_id=1, source_target_pairs={{0,16},{16,0},{32,48},{48,32},{64,80},{80,64},{96,112},{112,96},{1... | collective-permute-start | bytes 393224 | tf_op jit(solution)/shard_map/ppermute | solution.py:560
  70.8 0.8 copy-start.4
  71.7 53.9 %all-to-all-start.2 = ((bf16[512,2,256]{2,1,0:T(2,128)(2,1)}), bf16[512,2,256]{2,1,0:T(2,128)(2,1)S(1)}, u32[]{:S(2)}, u32[]{:S(2)}) async-start(bf16[512,2,256]{2,1,0:T(2,128)(2,1)} %copy-done.4), calls=%async_computation.2 | async-start | bytes 1048576 | tf_op jit(solution)/shard_map/all_to_all | solution.py:473
  89.4 8.3 %copy-start.9 = (bf16[1024]{0:T(1024)(128)(2,1)S(1)}, bf16[1024]{0:T(1024)(128)(2,1)}, u32[]{:S(2)}) copy-start(bf16[1024]{0:T(1024)(128)(2,1)} %param.24) | copy-start | bytes 6148
  90.3 37.8 %collective-permute-start.8 = (bf16[256,1280]{1,0:T(8,128)(2,1)}, bf16[256,1280]{1,0:T(8,128)(2,1)}, u32[]{:S(2)}, u32[]{:S(2)}) collective-permute-start(bf16[256,1280]{1,0:T(8,128)(2,1)} %slice.15), channel_id=1, source_target_pairs={{4,0},{8,4},{12,8},{0,12},{5,1},{9,5},{13,9},{1,13},{6,2},{10,6},{... | collective-permute-start | bytes 1966088 | tf_op jit(solution)/shard_map/ppermute | solution.py:542
  95.8 32.3 %collective-permute-start.7 = (bf16[256,1280]{1,0:T(8,128)(2,1)}, bf16[256,1280]{1,0:T(8,128)(2,1)}, u32[]{:S(2)}, u32[]{:S(2)}) collective-permute-start(bf16[256,1280]{1,0:T(8,128)(2,1)} %slice.14), channel_id=1, source_target_pairs={{0,4},{4,8},{8,12},{12,0},{1,5},{5,9},{9,13},{13,1},{2,6},{6,10},{... | collective-permute-start | bytes 1966088 | tf_op jit(solution)/shard_map/ppermute | solution.py:542
  125.6 1.3 copy-start
  130.4 45.1 %copy-start.3 = (f32[4,256,32]{2,1,0:T(8,128)S(1)}, f32[4,256,32]{2,1,0:T(8,128)}, u32[]{:S(2)}) copy-start(f32[4,256,32]{2,1,0:T(8,128)} %copy-done.2) | copy-start | bytes 393220
  175.8 3.0 %collective-permute-start.9 = (f32[1,256]{1,0:T(1,128)S(1)}, f32[1,256]{1,0:T(1,128)S(1)}, u32[]{:S(2)}, u32[]{:S(2)}) collective-permute-start(f32[1,256]{1,0:T(1,128)S(1)} %get-tuple-element.44), channel_id=1, source_target_pairs={{0,16},{16,32},{32,48},{48,64},{64,80},{80,96},{96,112},{112,128},... | collective-permute-start | bytes 3080 | tf_op jit(solution)/shard_map/ppermute | solution.py:588

commit v6 on v5

--- a/solution.py
+++ b/solution.py
@@ -9,6 +9,7 @@
 bf16 = jnp.bfloat16
 HALF = 256
 GROUP = 4
+PIECES = 4
 
 
 def mm(a, b, dims=((1,), (0,))):
@@ -75,24 +76,33 @@
 ):
     rows = x_ref.shape[0]
     dim = HALF // 2
-    pairs = [(x_far, x_ref), (gain_far, gain_ref), (gw_far, gw_ref), (rate_far, rate_ref), (bias_far, bias_ref)]
-    pairs.append((w_far, w_ref))
+    pairs = [(gain_far, gain_ref), (gw_far, gw_ref), (rate_far, rate_ref), (bias_far, bias_ref), (w_far, w_ref)]
     start = 0
     for far in (egate_far, eup_far, edown_far):
         size = far.shape[2]
         pairs.append((far.at[0], weights_ref.at[:, pl.ds(start, size)]))
         start += size
     moves = [pltpu.make_async_copy(a, b, sems.at[n]) for n, (a, b) in enumerate(pairs)]
-    for move in moves:
+    size = rows // PIECES
+    bytes_in = []
+    for n in range(PIECES):
+        spot = pl.ds(n * size, size)
+        bytes_in.append(pltpu.make_async_copy(x_far.at[spot], x_ref.at[spot], sems.at[10 + n]))
+    for move in bytes_in + moves:
         move.start()
-    for move in moves[:5]:
+    for move in moves[:4]:
         move.wait()
+    gain = gain_ref[...]
+    parts = []
+    for n in range(PIECES):
+        bytes_in[n].wait()
+        x = x_ref[n * size : (n + 1) * size].astype(f32)
+        parts.append((x * lax.rsqrt(jnp.mean(x * x, -1, keepdims=True) + 1e-05) * gain).astype(bf16))
+    normed = jnp.concatenate(parts, axis=0)
     first = pl.multiple_of(lax.axis_index("coarse") * HALF, HALF)
-    moves.append(pltpu.make_async_copy(x_ref.at[:, pl.ds(first, HALF)], share_ref, sems.at[9]))
-    moves[9].start()
-
-    x = x_ref[...].astype(f32)
-    normed = (x * lax.rsqrt(jnp.mean(x * x, -1, keepdims=True) + 1e-05) * gain_ref[...]).astype(bf16)
+    moves.append(pltpu.make_async_copy(x_ref.at[:, pl.ds(first, HALF)], share_ref, sems.at[8]))
+    moves[8].start()
+
     linear = mm(normed, jnp.concatenate([gw_ref[0], gw_ref[1]], axis=0), ((1,), (1,)))
     decay_in, write_in = linear[:, :2], linear[:, 2:]
     write = jax.nn.sigmoid(write_in + bias_ref[...])
@@ -106,16 +116,16 @@
     sums = mm(tri, jnp.concatenate([part_h, part_m, part_l], axis=1))
     cum = sums[:, 0:2] + (sums[:, 2:4] + sums[:, 4:6])
 
-    moves[5].wait()
+    moves[4].wait()
 
     def act(index):
         value = mm(normed, w_ref[index])
         return value / (1.0 + jnp.exp(-value))
 
     q_all, k_all, v_all = act(0), act(1), act(2)
-    for move in moves[6:9]:
+    for move in moves[5:8]:
         move.wait()
-    leave = pltpu.make_async_copy(weights_ref, weights_far, sems.at[10])
+    leave = pltpu.make_async_copy(weights_ref, weights_far, sems.at[9])
     leave.start()
     strict = iota((HALF, HALF), 0) > iota((HALF, HALF), 1)
     causal = iota((HALF, HALF), 0) >= iota((HALF, HALF), 1)
@@ -203,7 +213,7 @@
     lead = lax.rem(lax.axis_index("seq"), 2) == 0
     own_ref[...] = jnp.where(lead, keep[0], keep[1])
     give_ref[...] = jnp.where(lead, keep[1], keep[0])
-    moves[9].wait()
+    moves[8].wait()
     leave.wait()
 
 
@@ -211,6 +221,10 @@
     dim = late.shape[0]
     both = mm3(split(late[:, :dim]), split(early))
     return jnp.concatenate([both[:, :dim], both[:, dim:] + late[:, dim:]], axis=1)
+
+
+def stage_kernel(own_ref, out_ref):
+    out_ref[...] = own_ref[...]
 
 
 def pair_kernel(core_ref, own_ref, got_ref, msg_ref, first_ref):
@@ -270,7 +284,9 @@
     right_far,
     hidden_ref,
     send_ref,
+    token_ref,
 ):
+    token_ref[...] = jnp.zeros_like(token_ref)
     del left_far, right_far
     dim = HALF // 2
     lead = core_ref[0] == 0
@@ -301,24 +317,34 @@
     rank_ref[...] = mm(wide, tri)[:1].astype(jnp.int32) - 1
 
 
-def route_kernel(mask_ref, choice_ref, take_ref, weigh_ref, token_ref):
-    quarters, total, slots = take_ref.shape
+def placed_rows(mask_ref, choice_ref, quarter, shape):
+    total, slots = shape
     top = choice_ref.shape[1] // 2
-    count = jnp.sum(mask_ref[...])
-    line = iota((total, slots), 0)
+    line = iota(shape, 0)
     expert = (line >> 1).astype(f32)
     earlier = jnp.where(iota((slots, slots), 0) < iota((slots, slots), 1), 1.0, 0.0).astype(bf16)
-    for quarter in range(quarters):
-        live = quarter * slots + iota((total, slots), 1) < count
-        hit = jnp.zeros((total, slots), f32)
-        weight = jnp.zeros((total, slots), f32)
-        for pick in range(top):
-            same = (expert == choice_ref[quarter, pick : pick + 1, :slots]) & live
-            hit = hit + jnp.where(same, 1.0, 0.0)
-            weight = weight + jnp.where(same, choice_ref[quarter, top + pick : top + pick + 1, :slots], 0.0)
-        arrival = mm(hit.astype(bf16), earlier).astype(jnp.int32)
-        found = (hit > 0.0) & (arrival == (line & 1))
+    live = quarter * slots + iota(shape, 1) < jnp.sum(mask_ref[...])
+    hit = jnp.zeros(shape, f32)
+    weight = jnp.zeros(shape, f32)
+    for pick in range(top):
+        same = (expert == choice_ref[quarter, pick : pick + 1, :slots]) & live
+        hit = hit + jnp.where(same, 1.0, 0.0)
+        weight = weight + jnp.where(same, choice_ref[quarter, top + pick : top + pick + 1, :slots], 0.0)
+    arrival = mm(hit.astype(bf16), earlier).astype(jnp.int32)
+    return (hit > 0.0) & (arrival == (line & 1)), weight
+
+
+def route_kernel(mask_ref, choice_ref, take_ref, token_ref):
+    token_ref[...] = jnp.zeros_like(token_ref)
+    for quarter in range(take_ref.shape[0]):
+        found, _ = placed_rows(mask_ref, choice_ref, quarter, take_ref.shape[1:])
         take_ref[quarter] = jnp.where(found, 1.0, 0.0).astype(bf16)
+
+
+def weigh_kernel(mask_ref, choice_ref, token_ref, weigh_ref, done_ref):
+    done_ref[...] = token_ref[...]
+    for quarter in range(weigh_ref.shape[0]):
+        found, weight = placed_rows(mask_ref, choice_ref, quarter, weigh_ref.shape[1:])
         weigh_ref[quarter] = jnp.where(found, weight, 0.0)
 
 
@@ -342,35 +368,29 @@
                 offset[...] += mm(ext, ref[n * width : (n + 1) * width, :inner])
 
 
-def near_kernel(coarse_ref, rows_ref, ext_ref, own_ref, left_ref, right_ref, total_ref, offset_ref):
-    total_ref[...] = jnp.zeros_like(total_ref)
-    offset_ref[...] = jnp.zeros_like(offset_ref)
-    pieces = ((own_ref, 0, (0, 1)), (left_ref, GROUP - 1, (0, 1)), (right_ref, 1, (0, 1)))
-    expert_part(coarse_ref, rows_ref, ext_ref, pieces, total_ref, offset_ref)
-
-
 def expert_kernel(
     coarse_ref,
     rows_ref,
     ext_ref,
-    near_ref,
-    near_offset_ref,
     own_ref,
     left_ref,
     right_ref,
     upper_ref,
     lower_ref,
+    token_ref,
     out_ref,
     total,
     offset,
 ):
+    del token_ref
     width = rows_ref.shape[2]
     count = rows_ref.shape[0] // GROUP
     inner = total.shape[1]
     hidden = inner // 2
-    total[...] = near_ref[...]
-    offset[...] = near_offset_ref[...]
-    pieces = ((upper_ref, 2, (0,)), (lower_ref, 2, (1,)))
+    total[...] = jnp.zeros_like(total)
+    offset[...] = jnp.zeros_like(offset)
+    pieces = [(own_ref, 0, (0, 1)), (left_ref, GROUP - 1, (0, 1)), (right_ref, 1, (0, 1))]
+    pieces += [(upper_ref, 2, (0,)), (lower_ref, 2, (1,))]
     expert_part(coarse_ref, rows_ref, ext_ref, pieces, total, offset)
     gate = total[:, :hidden] + offset[:1, :hidden]
     up = total[:, hidden:] + offset[:1, hidden:]
@@ -509,7 +529,7 @@
             pltpu.VMEM((1, 2), f32),
             pltpu.VMEM((8, dim, HALF), bf16),
             pltpu.VMEM((8, dim, dim), f32),
-            pltpu.SemaphoreType.DMA((11,)),
+            pltpu.SemaphoreType.DMA((10 + PIECES,)),
         ),
         flops=2 * 10**9,
         megabytes=60,
@@ -521,12 +541,12 @@
 
     swap = [(i, i ^ 1) for i in range(seq_total)]
     got = lax.ppermute(give, "seq", swap)
+    own = call(stage_kernel, sds(own.shape, f32), (own,))
     rank = call(rank_kernel, sds((1, rows), jnp.int32), (boundaries,))
-    take, weigh, routed = call(
+    take, routed = call(
         route_kernel,
         (
             sds((GROUP, pair_total, local_slots), bf16),
-            sds((GROUP, pair_total, local_slots), f32),
             sds((8, dim), f32),
         ),
         (boundaries, choice),
@@ -561,23 +581,25 @@
 
     devices = lax.axis_size(everywhere)
     capacity = GROUP * pair_total // devices
-    hidden, outgoing = call(
+    hidden, outgoing, picked = call(
         finish_kernel,
-        (sds((rows, HALF), bf16), sds((devices, capacity, HALF), bf16)),
+        (sds((rows, HALF), bf16), sds((devices, capacity, HALF), bf16), sds((8, dim), f32)),
         (core, local, states, others, x_share, head_gain[None], boundaries, rank, take, left, right),
         scalars=1,
         far_in=(8, 9),
     )
     received = exchange(outgoing, everywhere)
-    parts = (sds((pair_total, 2 * hidden_units), f32), sds((16, 2 * hidden_units), f32))
-    extra_rows = extension.reshape(width // HALF, 1, HALF)
-    near = call(near_kernel, parts, (spot, received, extra_rows, weights, left, right), scalars=1)
+    weigh, weighed = call(
+        weigh_kernel,
+        (sds((GROUP, pair_total, local_slots), f32), sds((8, dim), f32)),
+        (boundaries, choice, picked),
+    )
     value = call(
         expert_kernel,
         sds((devices, capacity, HALF), bf16),
-        (spot, received, extra_rows, *near, weights, left, right, *facing),
+        (spot, received, extension.reshape(width // HALF, 1, HALF), weights, left, right, *facing, weighed),
         scalars=1,
-        scratch=tuple(pltpu.VMEM(part.shape, part.dtype) for part in parts),
+        scratch=(pltpu.VMEM((pair_total, 2 * hidden_units), f32), pltpu.VMEM((16, 2 * hidden_units), f32)),
     )
     returned = exchange(value, everywhere)
     stretch, last = call(

time: 180 us -> 181 us (level)
  waiting for transfers between devices: 43.8 us -> 39.9 us
  blocking collectives: 45.1 us -> 47.7 us
  starting transfers between devices: 61.5 us -> 63.6 us
    all_to_all x3, waiting for transfers between devices: 28.5 us -> 12.2 us  [exchange(): lax.all_to_all(array, axes, split_axis=0, concat_axis=0, tiled=True, **kw...]
    ppermute x1, waiting for transfers between devices: 0.01 us -> 9.51 us  [shards(): lax.ppermute(left[:half], 'coarse', ring)]
    ppermute x1, waiting for transfers between devices: 7.92 us -> 1.55 us  [shards(): right = lax.ppermute(weights, 'coarse', back)]
    ppermute x1, waiting for transfers between devices: 0.01 us -> 4.89 us  [shards(): lax.ppermute(right[half:], 'coarse', back)]
    ppermute x1, waiting for transfers between devices: 4.9 us -> 9.58 us  [shards(): left = lax.ppermute(weights, 'coarse', ring)]
    all_to_all x1, blocking collectives: 45.1 us -> 47.7 us  [exchange(): lax.all_to_all(array, axes, split_axis=0, concat_axis=0, tiled=True, **kw...]
    all_to_all x3, starting transfers between devices: 26.2 us -> 28.3 us  [exchange(): lax.all_to_all(array, axes, split_axis=0, concat_axis=0, tiled=True, **kw...]
    unnamed x20 -> x18, local copies, waits for them, and re-layouts: 3.84 us -> 2.52 us
  transfers between devices with their start and end apart: 13 -> 13, of which waited for: 7 -> 10; matrix products, arithmetic and copies ran while one was open for 1% -> 1% of each run, Pallas kernels for 9% -> 9%
where the time goes in v6:
time: 181 us; the launch traced here: 180 us
  starting transfers between devices  63.6 us (35%)
  blocking collectives  47.7 us (26%)
  waiting for transfers between devices  39.9 us (22%)
  Pallas kernels  24.6 us (14%)
  local copies, waits for them, and re-layouts  4.32 us (2%)
    all_to_all x1, blocking collectives, exchange(): lax.all_to_all(array, axes, split_axis=0, concat_axis=0, tiled=True, **kw...  47.7 us
    all_to_all x3, starting transfers between devices, exchange(): lax.all_to_all(array, axes, split_axis=0, concat_axis=0, tiled=True, **kw...  28.3 us
    pallas_call x17, Pallas kernels, call(): pl.pallas_call(kernel, out_shape=outs, in_specs=[spec(far_in, i - scalars...  24.6 us
    all_to_all x3, waiting for transfers between devices, exchange(): lax.all_to_all(array, axes, split_axis=0, concat_axis=0, tiled=True, **kw...  12.2 us
    ppermute x1, waiting for transfers between devices, shards(): left = lax.ppermute(weights, 'coarse', ring)  9.58 us
    ppermute x1, waiting for transfers between devices, shards(): lax.ppermute(left[:half], 'coarse', ring)  9.51 us
    ppermute x3, starting transfers between devices, shards(): state = state + lax.ppermute(outgoing, 'seq', pairs)  8.16 us
    ppermute x1, starting transfers between devices, shards(): got = lax.ppermute(give, 'seq', swap)  7.07 us
  transfers between devices with their start and end apart: 13, of which 10 were waited for; matrix products, arithmetic and copies ran while one was open for 1% of the time, Pallas kernels for 9%

profile of v6, /device:TPU:1, one launch (start us, length us, event | category | flops | bytes accessed | tf_op | source)
XLA Modules:
  0.0 180.5 jit_solution(3213135753887988059)
XLA Ops:
  0.0 1.3 shard_map.138
  1.3 5.0 %all-to-all-start = ((f32[4,16,128]{2,1,0:T(8,128)}), f32[4,16,128]{2,1,0:T(8,128)S(1)}, u32[]{:S(2)}, u32[]{:S(2)}) async-start(f32[4,16,128]{2,1,0:T(8,128)} %shard_map.138), calls=%async_computation | async-start | bytes 65536 | tf_op jit(solution)/shard_map/all_to_all | solution.py:493
  6.3 12.5 %shard_map.136 = (f32[128,256]{1,0:T(8,128)}, f32[128,256]{1,0:T(8,128)}, f32[2,512,256]{2,1,0:T(8,128)}, bf16[512,256]{1,0:T(8,128)(2,1)}, bf16[512,1280]{1,0:T(8,128)(2,1)}) custom-call(bf16[512,1024]{1,0:T(8,128)(2,1)} %bitcast.19, f32[1,1024]{1,0:T(1,128)} %bitcast.21, bf16[3,1024,256]{2,1,0:T(8,128)(2,1)} %w_far.1, bf16[2,2,1024]{2,1,0:T(2,128)(2,1)} %bitcast.20, ...), custom_call_target="tpu_custom_call" | custom-call | flops 2000000000 | bytes 20000000 | tf_op jit(solution)/shard_map/pallas_call | solution.py:451
  18.9 0.0 all-to-all-done.choice_far.choice_ref
  18.9 7.1 %collective-permute-start = (f32[128,256]{1,0:T(8,128)}, f32[128,256]{1,0:T(8,128)S(1)}, u32[]{:S(2)}, u32[]{:S(2)}) collective-permute-start(f32[128,256]{1,0:T(8,128)} %shard_map.139), channel_id=1, source_target_pairs={{0,16},{16,0},{32,48},{48,32},{64,80},{80,64},{96,112},{112,96},{1... | collective-permute-start | bytes 393224 | tf_op jit(solution)/shard_map/ppermute | solution.py:543
  26.0 0.0 copy-start.5
  26.0 0.9 copy-done.5
  26.9 0.2 collective-permute-done.got_ref
  27.1 0.9 shard_map.140
  28.1 3.4 %all-to-all-start.1 = ((bf16[4,128,256]{2,1,0:T(8,128)(2,1)}), bf16[4,128,256]{2,1,0:T(8,128)(2,1)S(1)}, u32[]{:S(2)}, u32[]{:S(2)}) async-start(bf16[4,128,256]{2,1,0:T(8,128)(2,1)} %get-tuple-element.28), calls=%async_computation.1 | async-start | bytes 524288 | tf_op jit(solution)/shard_map/all_to_all | solution.py:493
  31.5 3.6 %collective-permute-start.5 = (bf16[512,1280]{1,0:T(8,128)(2,1)}, bf16[512,1280]{1,0:T(8,128)(2,1)S(1)}, u32[]{:S(2)}, u32[]{:S(2)}) collective-permute-start(bf16[512,1280]{1,0:T(8,128)(2,1)} %get-tuple-element.35.own_ref), channel_id=1, source_target_pairs={{0,4},{4,8},{8,12},{12,0},{1,5},{5,9},{9,13},{13,1},{2,6},{6,10},{... | collective-permute-start | bytes 3932168 | tf_op jit(solution)/shard_map/ppermute | solution.py:560
  35.1 3.1 %collective-permute-start.6 = (bf16[512,1280]{1,0:T(8,128)(2,1)}, bf16[512,1280]{1,0:T(8,128)(2,1)S(1)}, u32[]{:S(2)}, u32[]{:S(2)}) collective-permute-start(bf16[512,1280]{1,0:T(8,128)(2,1)} %get-tuple-element.35.own_ref), channel_id=1, source_target_pairs={{4,0},{8,4},{12,8},{0,12},{5,1},{9,5},{13,9},{1,13},{6,2},{10,6},{... | collective-permute-start | bytes 3932168 | tf_op jit(solution)/shard_map/ppermute | solution.py:561
  38.3 0.9 all-to-all-done.1.got_ref
  39.2 0.0 copy-start.6
  39.2 0.6 shard_map.141
  39.9 6.8 %collective-permute-start.1 = (bf16[128,128]{1,0:T(8,128)(2,1)S(1)}, bf16[128,128]{1,0:T(8,128)(2,1)S(1)}, u32[]{:S(2)}, u32[]{:S(2)}) collective-permute-start(bf16[128,128]{1,0:T(8,128)(2,1)S(1)} %slice.17), channel_id=1, source_target_pairs={{0,128},{16,144},{32,160},{48,176},{64,192},{80,208},{96,224},{112... | collective-permute-start | bytes 98312 | tf_op jit(solution)/shard_map/ppermute | solution.py:578
  46.7 0.0 copy-done.6
  46.7 0.7 shard_map.142
  47.4 0.3 collective-permute-done.1.state_ref
  47.7 0.2 shard_map.143
  47.9 0.7 collective-permute-start.2
  48.5 0.0 collective-permute-done.2
  48.6 0.2 shard_map.144
  48.8 0.7 collective-permute-start.3
  49.4 0.0 collective-permute-done.3
  49.5 0.0 copy-start
  49.5 0.0 copy-start.4
  49.5 0.0 copy-start.7
  49.5 0.4 shard_map.145.own_ref
  49.9 4.9 %collective-permute-start.4 = (f32[2,128,128]{2,1,0:T(8,128)S(1)}, f32[2,128,128]{2,1,0:T(8,128)S(1)}, u32[]{:S(2)}, u32[]{:S(2)}) collective-permute-start(f32[2,128,128]{2,1,0:T(8,128)S(1)} %shard_map.145.own_ref), channel_id=1, source_target_pairs={{0,16},{16,0},{32,48},{48,32},{64,80},{80,64},{96,112},{112,96},{1... | collective-permute-start | bytes 393224 | tf_op jit(solution)/shard_map/ppermute | solution.py:580
  54.8 0.2 shard_map.146.rank_ref
  55.0 0.8 collective-permute-done.4.got_ref
  55.8 9.6 %collective-permute-done.5.left_far.left_ref = bf16[512,1280]{1,0:T(8,128)(2,1)S(1)} collective-permute-done((bf16[512,1280]{1,0:T(8,128)(2,1)}, bf16[512,1280]{1,0:T(8,128)(2,1)S(1)}, u32[]{:S(2)}, u32[]{:S(2)}) %collective-permute-start.5) | collective-permute-done | bytes 1310752 | tf_op jit(solution)/shard_map/ppermute | solution.py:560
  65.3 1.6 collective-permute-done.6.right_far.right_ref
  66.9 0.0 copy-done
  66.9 0.0 copy-done.4
  66.9 0.0 copy-done.7
  66.9 1.0 shard_map.147
  67.9 0.0 copy-start.1
  67.9 0.8 copy-done.1
  68.7 19.9 %all-to-all-start.2 = ((bf16[512,2,256]{2,1,0:T(2,128)(2,1)}), bf16[512,2,256]{2,1,0:T(2,128)(2,1)S(1)}, u32[]{:S(2)}, u32[]{:S(2)}) async-start(bf16[512,2,256]{2,1,0:T(2,128)(2,1)} %copy-done.1), calls=%async_computation.2 | async-start | bytes 1048576 | tf_op jit(solution)/shard_map/all_to_all | solution.py:493
  88.6 0.0 copy-start.8
  88.6 0.9 slice.14
  89.5 3.3 %collective-permute-start.7 = (bf16[256,1280]{1,0:T(8,128)(2,1)}, bf16[256,1280]{1,0:T(8,128)(2,1)}, u32[]{:S(2)}, u32[]{:S(2)}) collective-permute-start(bf16[256,1280]{1,0:T(8,128)(2,1)} %slice.14), channel_id=1, source_target_pairs={{0,4},{4,8},{8,12},{12,0},{1,5},{5,9},{9,13},{13,1},{2,6},{6,10},{... | collective-permute-start | bytes 1966088 | tf_op jit(solution)/shard_map/ppermute | solution.py:562
  92.8 0.9 slice.15
  93.7 3.2 %collective-permute-start.8 = (bf16[256,1280]{1,0:T(8,128)(2,1)}, bf16[256,1280]{1,0:T(8,128)(2,1)}, u32[]{:S(2)}, u32[]{:S(2)}) collective-permute-start(bf16[256,1280]{1,0:T(8,128)(2,1)} %slice.15), channel_id=1, source_target_pairs={{4,0},{8,4},{12,8},{0,12},{5,1},{9,5},{13,9},{1,13},{6,2},{10,6},{... | collective-permute-start | bytes 1966088 | tf_op jit(solution)/shard_map/ppermute | solution.py:562
  96.9 0.0 copy-done.8
  96.9 1.3 shard_map.148
  98.3 0.0 copy-start.2
  98.3 0.8 copy-done.2
  99.1 9.5 %collective-permute-done.7.upper_ref = bf16[256,1280]{1,0:T(8,128)(2,1)} collective-permute-done((bf16[256,1280]{1,0:T(8,128)(2,1)}, bf16[256,1280]{1,0:T(8,128)(2,1)}, u32[]{:S(2)}, u32[]{:S(2)}) %collective-permute-start.7) | collective-permute-done | bytes 655392 | tf_op jit(solution)/shard_map/ppermute | solution.py:562
  108.6 4.9 %collective-permute-done.8.lower_ref = bf16[256,1280]{1,0:T(8,128)(2,1)} collective-permute-done((bf16[256,1280]{1,0:T(8,128)(2,1)}, bf16[256,1280]{1,0:T(8,128)(2,1)}, u32[]{:S(2)}, u32[]{:S(2)}) %collective-permute-start.8) | collective-permute-done | bytes 655392 | tf_op jit(solution)/shard_map/ppermute | solution.py:562
  113.5 11.3 %all-to-all-done.2.rows_ref = bf16[512,2,256]{2,1,0:T(2,128)(2,1)S(1)} async-done(((bf16[512,2,256]{2,1,0:T(2,128)(2,1)}), bf16[512,2,256]{2,1,0:T(2,128)(2,1)S(1)}, u32[]{:S(2)}, u32[]{:S(2)}) %all-to-all-start.2) | async-done | bytes 524320 | tf_op jit(solution)/shard_map/all_to_all | solution.py:493
  124.7 3.8 %shard_map.149 = bf16[512,2,256]{2,1,0:T(2,128)(2,1)S(1)} custom-call(s32[1]{0:T(128)} %bitcast.12.coarse_ref, bf16[512,2,256]{2,1,0:T(2,128)(2,1)S(1)} %all-to-all-done.2.rows_ref, bf16[4,1,256]{2,1,0:T(2,128)(2,1)S(1)} %reshape.4.ext_ref, bf16[512,1280]{1,0:T(8,128)(2,1)} %get-tuple-element.35.own_ref, ...), custom_call_target="tpu_custom_call" | custom-call | flops 100000 | bytes 1000 | tf_op jit(solution)/shard_map/pallas_call | solution.py:451
  128.5 0.0 copy-start.3
  128.5 47.7 %all_to_all.20.back_ref = bf16[512,2,256]{2,1,0:T(2,128)(2,1)S(1)} all-to-all(bf16[512,2,256]{2,1,0:T(2,128)(2,1)S(1)} %shard_map.149), channel_id=1, replica_groups=mesh['seq'=32,'coarse'=4,'exp'=4] {'coarse','seq','exp'}, dimensions={0} | all-to-all | bytes 1048576 | tf_op jit(solution)/shard_map/all_to_all | solution.py:493
  176.2 0.0 copy-done.3
  176.2 0.4 shard_map.150
  176.6 1.9 %collective-permute-start.9 = (f32[1,256]{1,0:T(1,128)S(1)}, f32[1,256]{1,0:T(1,128)S(1)}, u32[]{:S(2)}, u32[]{:S(2)}) collective-permute-start(f32[1,256]{1,0:T(1,128)S(1)} %get-tuple-element.44), channel_id=1, source_target_pairs={{0,16},{16,32},{32,48},{48,64},{64,80},{80,96},{96,112},{112,128},... | collective-permute-start | bytes 3080 | tf_op jit(solution)/shard_map/ppermute | solution.py:610
  178.5 0.3 shard_map.151
  178.9 0.8 collective-permute-done.9.prev_ref
  179.6 0.8 shard_map.152
  (6 shorter events, 0.1 us)
Async XLA Ops:
  1.3 17.5 %all-to-all-start = ((f32[4,16,128]{2,1,0:T(8,128)}), f32[4,16,128]{2,1,0:T(8,128)S(1)}, u32[]{:S(2)}, u32[]{:S(2)}) async-start(f32[4,16,128]{2,1,0:T(8,128)} %shard_map.138), calls=%async_computation | async-start | bytes 65536 | tf_op jit(solution)/shard_map/all_to_all | solution.py:493
  18.9 8.3 %collective-permute-start = (f32[128,256]{1,0:T(8,128)}, f32[128,256]{1,0:T(8,128)S(1)}, u32[]{:S(2)}, u32[]{:S(2)}) collective-permute-start(f32[128,256]{1,0:T(8,128)} %shard_map.139), channel_id=1, source_target_pairs={{0,16},{16,0},{32,48},{48,32},{64,80},{80,64},{96,112},{112,96},{1... | collective-permute-start | bytes 393224 | tf_op jit(solution)/shard_map/ppermute | solution.py:543
  26.0 0.9 copy-start.5
  28.1 11.1 %all-to-all-start.1 = ((bf16[4,128,256]{2,1,0:T(8,128)(2,1)}), bf16[4,128,256]{2,1,0:T(8,128)(2,1)S(1)}, u32[]{:S(2)}, u32[]{:S(2)}) async-start(bf16[4,128,256]{2,1,0:T(8,128)(2,1)} %get-tuple-element.28), calls=%async_computation.1 | async-start | bytes 524288 | tf_op jit(solution)/shard_map/all_to_all | solution.py:493
  31.5 33.8 %collective-permute-start.5 = (bf16[512,1280]{1,0:T(8,128)(2,1)}, bf16[512,1280]{1,0:T(8,128)(2,1)S(1)}, u32[]{:S(2)}, u32[]{:S(2)}) collective-permute-start(bf16[512,1280]{1,0:T(8,128)(2,1)} %get-tuple-element.35.own_ref), channel_id=1, source_target_pairs={{0,4},{4,8},{8,12},{12,0},{1,5},{5,9},{9,13},{13,1},{2,6},{6,10},{... | collective-permute-start | bytes 3932168 | tf_op jit(solution)/shard_map/ppermute | solution.py:560
  35.1 31.8 %collective-permute-start.6 = (bf16[512,1280]{1,0:T(8,128)(2,1)}, bf16[512,1280]{1,0:T(8,128)(2,1)S(1)}, u32[]{:S(2)}, u32[]{:S(2)}) collective-permute-start(bf16[512,1280]{1,0:T(8,128)(2,1)} %get-tuple-element.35.own_ref), channel_id=1, source_target_pairs={{4,0},{8,4},{12,8},{0,12},{5,1},{9,5},{13,9},{1,13},{6,2},{10,6},{... | collective-permute-start | bytes 3932168 | tf_op jit(solution)/shard_map/ppermute | solution.py:561
  39.2 7.5 %copy-start.6 = (s32[1,512]{1,0:T(1,128)S(1)}, s32[1,512]{1,0:T(1,128)}, u32[]{:S(2)}) copy-start(s32[1,512]{1,0:T(1,128)} %mask_ref.9) | copy-start | bytes 6148
  39.9 7.8 %collective-permute-start.1 = (bf16[128,128]{1,0:T(8,128)(2,1)S(1)}, bf16[128,128]{1,0:T(8,128)(2,1)S(1)}, u32[]{:S(2)}, u32[]{:S(2)}) collective-permute-start(bf16[128,128]{1,0:T(8,128)(2,1)S(1)} %slice.17), channel_id=1, source_target_pairs={{0,128},{16,144},{32,160},{48,176},{64,192},{80,208},{96,224},{112... | collective-permute-start | bytes 98312 | tf_op jit(solution)/shard_map/ppermute | solution.py:578
  47.9 0.7 collective-permute-start.2
  48.8 0.7 collective-permute-start.3
  49.5 17.4 %copy-start = (f32[2,512,256]{2,1,0:T(8,128)S(1)}, f32[2,512,256]{2,1,0:T(8,128)}, u32[]{:S(2)}) copy-start(f32[2,512,256]{2,1,0:T(8,128)} %get-tuple-element.25.local_ref) | copy-start | bytes 3145732
  49.5 17.4 %copy-start.4 = (bf16[512,256]{1,0:T(8,128)(2,1)S(1)}, bf16[512,256]{1,0:T(8,128)(2,1)}, u32[]{:S(2)}) copy-start(bf16[512,256]{1,0:T(8,128)(2,1)} %get-tuple-element.33.x_ref) | copy-start | bytes 786436
  49.5 17.4 %copy-start.7 = (f32[256]{0:T(256)S(1)}, f32[256]{0:T(256)}, u32[]{:S(2)}) copy-start(f32[256]{0:T(256)} %param.20) | copy-start | bytes 3076
  49.9 5.9 %collective-permute-start.4 = (f32[2,128,128]{2,1,0:T(8,128)S(1)}, f32[2,128,128]{2,1,0:T(8,128)S(1)}, u32[]{:S(2)}, u32[]{:S(2)}) collective-permute-start(f32[2,128,128]{2,1,0:T(8,128)S(1)} %shard_map.145.own_ref), channel_id=1, source_target_pairs={{0,16},{16,0},{32,48},{48,32},{64,80},{80,64},{96,112},{112,96},{1... | collective-permute-start | bytes 393224 | tf_op jit(solution)/shard_map/ppermute | solution.py:580
  67.9 0.8 copy-start.1
  68.7 56.1 %all-to-all-start.2 = ((bf16[512,2,256]{2,1,0:T(2,128)(2,1)}), bf16[512,2,256]{2,1,0:T(2,128)(2,1)S(1)}, u32[]{:S(2)}, u32[]{:S(2)}) async-start(bf16[512,2,256]{2,1,0:T(2,128)(2,1)} %copy-done.1), calls=%async_computation.2 | async-start | bytes 1048576 | tf_op jit(solution)/shard_map/all_to_all | solution.py:493
  88.6 8.3 %copy-start.8 = (bf16[1024]{0:T(1024)(128)(2,1)S(1)}, bf16[1024]{0:T(1024)(128)(2,1)}, u32[]{:S(2)}) copy-start(bf16[1024]{0:T(1024)(128)(2,1)} %param.24) | copy-start | bytes 6148
  89.5 19.0 %collective-permute-start.7 = (bf16[256,1280]{1,0:T(8,128)(2,1)}, bf16[256,1280]{1,0:T(8,128)(2,1)}, u32[]{:S(2)}, u32[]{:S(2)}) collective-permute-start(bf16[256,1280]{1,0:T(8,128)(2,1)} %slice.14), channel_id=1, source_target_pairs={{0,4},{4,8},{8,12},{12,0},{1,5},{5,9},{9,13},{13,1},{2,6},{6,10},{... | collective-permute-start | bytes 1966088 | tf_op jit(solution)/shard_map/ppermute | solution.py:562
  93.7 19.8 %collective-permute-start.8 = (bf16[256,1280]{1,0:T(8,128)(2,1)}, bf16[256,1280]{1,0:T(8,128)(2,1)}, u32[]{:S(2)}, u32[]{:S(2)}) collective-permute-start(bf16[256,1280]{1,0:T(8,128)(2,1)} %slice.15), channel_id=1, source_target_pairs={{4,0},{8,4},{12,8},{0,12},{5,1},{9,5},{13,9},{1,13},{6,2},{10,6},{... | collective-permute-start | bytes 1966088 | tf_op jit(solution)/shard_map/ppermute | solution.py:562
  98.3 0.8 copy-start.2
  128.5 47.7 %copy-start.3 = (f32[4,256,32]{2,1,0:T(8,128)S(1)}, f32[4,256,32]{2,1,0:T(8,128)}, u32[]{:S(2)}) copy-start(f32[4,256,32]{2,1,0:T(8,128)} %copy-done.2) | copy-start | bytes 393220
  176.6 3.0 %collective-permute-start.9 = (f32[1,256]{1,0:T(1,128)S(1)}, f32[1,256]{1,0:T(1,128)S(1)}, u32[]{:S(2)}, u32[]{:S(2)}) collective-permute-start(f32[1,256]{1,0:T(1,128)S(1)} %get-tuple-element.44), channel_id=1, source_target_pairs={{0,16},{16,32},{32,48},{48,64},{64,80},{80,96},{96,112},{112,128},... | collective-permute-start | bytes 3080 | tf_op jit(solution)/shard_map/ppermute | solution.py:610

commit v7 on v6

--- a/solution.py
+++ b/solution.py
@@ -9,7 +9,7 @@
 bf16 = jnp.bfloat16
 HALF = 256
 GROUP = 4
-PIECES = 4
+PIECES = 1
 
 
 def mm(a, b, dims=((1,), (0,))):
@@ -36,12 +36,25 @@
     return jnp.sum(jnp.where(eye, column, 0.0), axis=0, keepdims=True)
 
 
-def choice_kernel(picks_ref, gates_ref, out_ref):
+def choice_kernel(picks_ref, gates_ref, edown_far, out_ref, build, sems):
     top, slots = picks_ref.shape
-    out_ref[...] = jnp.zeros_like(out_ref)
-    for quarter in range(out_ref.shape[0]):
-        out_ref[quarter, :top, :slots] = picks_ref[...].astype(f32)
-        out_ref[quarter, top:, :slots] = gates_ref[...]
+    depth = edown_far.shape[1]
+    moves = [
+        pltpu.make_async_copy(edown_far.at[0], out_ref.at[n, pl.ds(0, depth)], sems.at[n]) for n in range(GROUP)
+    ]
+    for move in moves:
+        move.start()
+    build[...] = jnp.zeros_like(build)
+    gates = gates_ref[...]
+    high = gates.astype(bf16).astype(f32)
+    half = build.shape[1] // 2
+    build[:top, :slots] = picks_ref[...].astype(f32)
+    build[:top, half : half + slots] = high
+    build[top:, half : half + slots] = gates - high
+    for n in range(GROUP):
+        out_ref[n, depth:] = build[...].astype(bf16)
+    for move in moves:
+        move.wait()
 
 
 def after_kernel(choice_far, give_far, same_far):
@@ -57,7 +70,6 @@
     bias_far,
     egate_far,
     eup_far,
-    edown_far,
     own_ref,
     give_ref,
     local_ref,
@@ -78,7 +90,7 @@
     dim = HALF // 2
     pairs = [(gain_far, gain_ref), (gw_far, gw_ref), (rate_far, rate_ref), (bias_far, bias_ref), (w_far, w_ref)]
     start = 0
-    for far in (egate_far, eup_far, edown_far):
+    for far in (egate_far, eup_far):
         size = far.shape[2]
         pairs.append((far.at[0], weights_ref.at[:, pl.ds(start, size)]))
         start += size
@@ -101,7 +113,7 @@
     normed = jnp.concatenate(parts, axis=0)
     first = pl.multiple_of(lax.axis_index("coarse") * HALF, HALF)
     moves.append(pltpu.make_async_copy(x_ref.at[:, pl.ds(first, HALF)], share_ref, sems.at[8]))
-    moves[8].start()
+    moves[7].start()
 
     linear = mm(normed, jnp.concatenate([gw_ref[0], gw_ref[1]], axis=0), ((1,), (1,)))
     decay_in, write_in = linear[:, :2], linear[:, 2:]
@@ -123,7 +135,7 @@
         return value / (1.0 + jnp.exp(-value))
 
     q_all, k_all, v_all = act(0), act(1), act(2)
-    for move in moves[5:8]:
+    for move in moves[5:7]:
         move.wait()
     leave = pltpu.make_async_copy(weights_ref, weights_far, sems.at[9])
     leave.start()
@@ -213,7 +225,7 @@
     lead = lax.rem(lax.axis_index("seq"), 2) == 0
     own_ref[...] = jnp.where(lead, keep[0], keep[1])
     give_ref[...] = jnp.where(lead, keep[1], keep[0])
-    moves[8].wait()
+    moves[7].wait()
     leave.wait()
 
 
@@ -317,6 +329,13 @@
     rank_ref[...] = mm(wide, tri)[:1].astype(jnp.int32) - 1
 
 
+def fetch(shared_far, table, sem):
+    depth = shared_far.shape[1] - table.shape[1]
+    move = pltpu.make_async_copy(shared_far.at[:, pl.ds(depth, table.shape[1])], table, sem)
+    move.start()
+    move.wait()
+
+
 def placed_rows(mask_ref, choice_ref, quarter, shape):
     total, slots = shape
     top = choice_ref.shape[1] // 2
@@ -326,22 +345,28 @@
     live = quarter * slots + iota(shape, 1) < jnp.sum(mask_ref[...])
     hit = jnp.zeros(shape, f32)
     weight = jnp.zeros(shape, f32)
+    table = choice_ref[quarter].astype(f32)
+    half = table.shape[1] // 2
+    names = table[:top, :slots]
+    gates = table[:top, half : half + slots] + table[top:, half : half + slots]
     for pick in range(top):
-        same = (expert == choice_ref[quarter, pick : pick + 1, :slots]) & live
+        same = (expert == names[pick : pick + 1]) & live
         hit = hit + jnp.where(same, 1.0, 0.0)
-        weight = weight + jnp.where(same, choice_ref[quarter, top + pick : top + pick + 1, :slots], 0.0)
+        weight = weight + jnp.where(same, gates[pick : pick + 1], 0.0)
     arrival = mm(hit.astype(bf16), earlier).astype(jnp.int32)
     return (hit > 0.0) & (arrival == (line & 1)), weight
 
 
-def route_kernel(mask_ref, choice_ref, take_ref, token_ref):
+def route_kernel(mask_ref, shared_far, take_ref, token_ref, choice_ref, sem):
+    fetch(shared_far, choice_ref, sem)
     token_ref[...] = jnp.zeros_like(token_ref)
     for quarter in range(take_ref.shape[0]):
         found, _ = placed_rows(mask_ref, choice_ref, quarter, take_ref.shape[1:])
         take_ref[quarter] = jnp.where(found, 1.0, 0.0).astype(bf16)
 
 
-def weigh_kernel(mask_ref, choice_ref, token_ref, weigh_ref, done_ref):
+def weigh_kernel(mask_ref, shared_far, token_ref, weigh_ref, done_ref, choice_ref, sem):
+    fetch(shared_far, choice_ref, sem)
     done_ref[...] = token_ref[...]
     for quarter in range(weigh_ref.shape[0]):
         found, weight = placed_rows(mask_ref, choice_ref, quarter, weigh_ref.shape[1:])
@@ -377,6 +402,7 @@
     right_ref,
     upper_ref,
     lower_ref,
+    down_ref,
     token_ref,
     out_ref,
     total,
@@ -396,13 +422,9 @@
     up = total[:, hidden:] + offset[:1, hidden:]
     act = (gate / (1.0 + jnp.exp(-gate)) * up).astype(bf16)
 
-    def put(step, value):
-        c = lax.rem(coarse_ref[0] + step, GROUP)
-        out_ref[pl.ds(c * count, count)] = value.astype(bf16).reshape(count, *out_ref.shape[1:])
-
-    for ref, step in ((own_ref, 0), (left_ref, GROUP - 1), (right_ref, 1)):
-        put(step, mm(act, ref[:, inner:]))
-    put(2, mm(act[:, :width], upper_ref[:, inner:]) + mm(act[:, width:], lower_ref[:, inner:]))
+    for c in range(GROUP):
+        value = mm(act, down_ref[c, :hidden]).astype(bf16)
+        out_ref[c * count : (c + 1) * count] = value.reshape(count, *out_ref.shape[1:])
 
 
 def combine_kernel(mask_ref, weigh_ref, back_ref, out_ref, last_ref):
@@ -493,11 +515,19 @@
         return lax.all_to_all(array, axes, split_axis=0, concat_axis=0, tiled=True, **kwargs)
 
     top = picks.shape[2]
-    choice = call(choice_kernel, sds((GROUP, 2 * top, dim), f32), (picks[0].T, pick_gates[0].T), megabytes=63)
-    choice = exchange(choice, "coarse")
+    shared = call(
+        choice_kernel,
+        sds((GROUP, expert_down.shape[1] + 2 * top, HALF), bf16),
+        (picks[0].T, pick_gates[0].T, expert_down),
+        scratch=(pltpu.VMEM((2 * top, HALF), f32), pltpu.SemaphoreType.DMA((GROUP,))),
+        megabytes=63,
+        far_in=(2,),
+    )
+    shared = exchange(shared, "coarse")
+    table = (pltpu.VMEM((GROUP, 2 * top, HALF), bf16), pltpu.SemaphoreType.DMA)
 
     depth, hidden_units = expert_gate.shape[1:]
-    columns = 2 * hidden_units + expert_down.shape[2]
+    columns = 2 * hidden_units
     gate_rows = gate_weight_enc.transpose(0, 2, 1)
     own, give, local, x_share, weights = call(
         delta_kernel,
@@ -517,7 +547,6 @@
             write_bias[None],
             expert_gate,
             expert_up,
-            expert_down,
         ),
         scratch=(
             pltpu.VMEM((depth, columns), bf16),
@@ -533,11 +562,11 @@
         ),
         flops=2 * 10**9,
         megabytes=60,
-        far_in=range(9),
+        far_in=range(8),
         far_out=(4,),
     )
 
-    give = call(after_kernel, sds(give.shape, f32), (choice, give), far_in=(0, 1), far_out=(0,), same={1: 0})
+    give = call(after_kernel, sds(give.shape, f32), (shared, give), far_in=(0, 1), far_out=(0,), same={1: 0})
 
     swap = [(i, i ^ 1) for i in range(seq_total)]
     got = lax.ppermute(give, "seq", swap)
@@ -549,7 +578,9 @@
             sds((GROUP, pair_total, local_slots), bf16),
             sds((8, dim), f32),
         ),
-        (boundaries, choice),
+        (boundaries, shared),
+        scratch=table,
+        far_in=(1,),
     )
     message, first = call(
         pair_kernel, (sds((GROUP, dim, HALF), bf16), sds((dim, HALF), f32)), (core, own, got), scalars=1
@@ -592,12 +623,14 @@
     weigh, weighed = call(
         weigh_kernel,
         (sds((GROUP, pair_total, local_slots), f32), sds((8, dim), f32)),
-        (boundaries, choice, picked),
+        (boundaries, shared, picked),
+        scratch=table,
+        far_in=(1,),
     )
     value = call(
         expert_kernel,
         sds((devices, capacity, HALF), bf16),
-        (spot, received, extension.reshape(width // HALF, 1, HALF), weights, left, right, *facing, weighed),
+        (spot, received, extension.reshape(width // HALF, 1, HALF), weights, left, right, *facing, shared, weighed),
         scalars=1,
         scratch=(pltpu.VMEM((pair_total, 2 * hidden_units), f32), pltpu.VMEM((16, 2 * hidden_units), f32)),
     )

time: 181 us -> 179 us (0.989)
  waiting for transfers between devices: 39.9 us -> 30.8 us
  starting transfers between devices: 63.6 us -> 70.8 us
    ppermute x1, waiting for transfers between devices: 9.58 us -> 1.74 us  [shards(): left = lax.ppermute(weights, 'coarse', ring)]
    all_to_all x3, starting transfers between devices: 28.3 us -> 33.3 us  [exchange(): lax.all_to_all(array, axes, split_axis=0, concat_axis=0, tiled=True, **kw...]
    ppermute x1, waiting for transfers between devices: 9.51 us -> 6.28 us  [shards(): lax.ppermute(left[:half], 'coarse', ring)]
    all_to_all x3, waiting for transfers between devices: 12.2 us -> 14.3 us  [exchange(): lax.all_to_all(array, axes, split_axis=0, concat_axis=0, tiled=True, **kw...]
    ppermute x3, starting transfers between devices: 8.16 us -> 10.1 us  [shards(): state = state + lax.ppermute(outgoing, 'seq', pairs)]
  transfers between devices with their start and end apart: 13 -> 13, of which waited for: 10 -> 9; matrix products, arithmetic and copies ran while one was open for 1% -> 1% of each run, Pallas kernels for 9% -> 9%
where the time goes in v7:
time: 179 us
  starting transfers between devices  70.8 us (40%)
  blocking collectives  46.3 us (26%)
  waiting for transfers between devices  30.8 us (17%)
  Pallas kernels  26.3 us (15%)
  local copies, waits for them, and re-layouts  3.97 us (2%)
    all_to_all x1, blocking collectives, exchange(): lax.all_to_all(array, axes, split_axis=0, concat_axis=0, tiled=True, **kw...  46.3 us
    all_to_all x3, starting transfers between devices, exchange(): lax.all_to_all(array, axes, split_axis=0, concat_axis=0, tiled=True, **kw...  33.3 us
    pallas_call x17, Pallas kernels, call(): pl.pallas_call(kernel, out_shape=outs, in_specs=[spec(far_in, i - scalars...  26.3 us
    all_to_all x3, waiting for transfers between devices, exchange(): lax.all_to_all(array, axes, split_axis=0, concat_axis=0, tiled=True, **kw...  14.3 us
    ppermute x3, starting transfers between devices, shards(): state = state + lax.ppermute(outgoing, 'seq', pairs)  10.1 us
    ppermute x1, starting transfers between devices, shards(): got = lax.ppermute(give, 'seq', swap)  7.43 us
    ppermute x1, waiting for transfers between devices, shards(): lax.ppermute(left[:half], 'coarse', ring)  6.28 us
    ppermute x1, starting transfers between devices, shards(): others = lax.ppermute(states, 'seq', swap)  5.05 us
  transfers between devices with their start and end apart: 13, of which 9 were waited for; matrix products, arithmetic and copies ran while one was open for 1% of the time, Pallas kernels for 9%

profile of v7, /device:TPU:1, one launch (start us, length us, event | category | flops | bytes accessed | tf_op | source)
XLA Modules:
  0.0 178.6 jit_solution(5848297467059909345)
XLA Ops:
  0.0 3.1 %shard_map.138 = bf16[4,528,256]{2,1,0:T(8,128)(2,1)} custom-call(s32[8,32]{1,0:T(8,128)} %bitcast.17, f32[8,32]{1,0:T(8,128)} %bitcast.18, bf16[1,512,256]{2,1,0:T(8,128)(2,1)} %edown_far.1), custom_call_target="tpu_custom_call" | custom-call | flops 100000 | bytes 1000 | tf_op jit(solution)/shard_map/pallas_call | solution.py:473
  3.1 5.0 %all-to-all-start = ((bf16[4,528,256]{2,1,0:T(8,128)(2,1)}), bf16[4,528,256]{2,1,0:T(8,128)(2,1)S(1)}, u32[]{:S(2)}, u32[]{:S(2)}) async-start(bf16[4,528,256]{2,1,0:T(8,128)(2,1)} %shard_map.138), calls=%async_computation | async-start | bytes 2162688 | tf_op jit(solution)/shard_map/all_to_all | solution.py:515
  8.1 12.4 %shard_map.136 = (f32[128,256]{1,0:T(8,128)}, f32[128,256]{1,0:T(8,128)}, f32[2,512,256]{2,1,0:T(8,128)}, bf16[512,256]{1,0:T(8,128)(2,1)}, bf16[512,1024]{1,0:T(8,128)(2,1)}) custom-call(bf16[512,1024]{1,0:T(8,128)(2,1)} %bitcast.19, f32[1,1024]{1,0:T(1,128)} %bitcast.21, bf16[3,1024,256]{2,1,0:T(8,128)(2,1)} %w_far.1, bf16[2,2,1024]{2,1,0:T(2,128)(2,1)} %bitcast.20, ...), custom_call_target="tpu_custom_call" | custom-call | flops 2000000000 | bytes 20000000 | tf_op jit(solution)/shard_map/pallas_call | solution.py:473
  20.6 0.0 copy-start.5
  20.6 0.0 all-to-all-done.choice_far.shared_far.down_ref
  20.6 7.4 %collective-permute-start = (f32[128,256]{1,0:T(8,128)}, f32[128,256]{1,0:T(8,128)S(1)}, u32[]{:S(2)}, u32[]{:S(2)}) collective-permute-start(f32[128,256]{1,0:T(8,128)} %shard_map.139), channel_id=1, source_target_pairs={{0,16},{16,0},{32,48},{48,32},{64,80},{80,64},{96,112},{112,96},{1... | collective-permute-start | bytes 393224 | tf_op jit(solution)/shard_map/ppermute | solution.py:572
  28.1 0.0 copy-done.5
  28.1 1.1 collective-permute-done.got_ref
  29.2 0.9 shard_map.140
  30.2 0.0 copy-start.8
  30.2 0.7 copy-done.8
  30.8 4.0 %all-to-all-start.1 = ((bf16[4,128,256]{2,1,0:T(8,128)(2,1)}), bf16[4,128,256]{2,1,0:T(8,128)(2,1)S(1)}, u32[]{:S(2)}, u32[]{:S(2)}) async-start(bf16[4,128,256]{2,1,0:T(8,128)(2,1)} %get-tuple-element.28), calls=%async_computation.1 | async-start | bytes 524288 | tf_op jit(solution)/shard_map/all_to_all | solution.py:515
  34.8 3.0 %collective-permute-start.5 = (bf16[512,1024]{1,0:T(8,128)(2,1)}, bf16[512,1024]{1,0:T(8,128)(2,1)S(1)}, u32[]{:S(2)}, u32[]{:S(2)}) collective-permute-start(bf16[512,1024]{1,0:T(8,128)(2,1)} %get-tuple-element.35.own_ref), channel_id=1, source_target_pairs={{0,4},{4,8},{8,12},{12,0},{1,5},{5,9},{9,13},{13,1},{2,6},{6,10},{... | collective-permute-start | bytes 3145736 | tf_op jit(solution)/shard_map/ppermute | solution.py:591
  37.9 3.5 %collective-permute-start.6 = (bf16[512,1024]{1,0:T(8,128)(2,1)}, bf16[512,1024]{1,0:T(8,128)(2,1)S(1)}, u32[]{:S(2)}, u32[]{:S(2)}) collective-permute-start(bf16[512,1024]{1,0:T(8,128)(2,1)} %get-tuple-element.35.own_ref), channel_id=1, source_target_pairs={{4,0},{8,4},{12,8},{0,12},{5,1},{9,5},{13,9},{1,13},{6,2},{10,6},{... | collective-permute-start | bytes 3145736 | tf_op jit(solution)/shard_map/ppermute | solution.py:592
  41.3 1.2 all-to-all-done.1.got_ref
  42.5 0.6 shard_map.141
  43.2 8.8 %collective-permute-start.1 = (bf16[128,128]{1,0:T(8,128)(2,1)S(1)}, bf16[128,128]{1,0:T(8,128)(2,1)S(1)}, u32[]{:S(2)}, u32[]{:S(2)}) collective-permute-start(bf16[128,128]{1,0:T(8,128)(2,1)S(1)} %slice.17), channel_id=1, source_target_pairs={{0,128},{16,144},{32,160},{48,176},{64,192},{80,208},{96,224},{112... | collective-permute-start | bytes 98312 | tf_op jit(solution)/shard_map/ppermute | solution.py:609
  52.0 0.0 copy-done.6
  52.0 0.7 shard_map.142
  52.7 0.3 collective-permute-done.1.state_ref
  53.0 0.2 shard_map.143
  53.2 0.7 collective-permute-start.2
  53.9 0.0 collective-permute-done.2
  53.9 0.0 copy-start.9
  53.9 0.2 shard_map.144
  54.1 0.7 collective-permute-start.3
  54.8 0.0 collective-permute-done.3
  54.8 0.0 copy-done.9
  54.8 0.0 copy-start.4
  54.8 0.0 copy-start.7
  54.8 0.4 shard_map.145.own_ref
  55.2 5.1 %collective-permute-start.4 = (f32[2,128,128]{2,1,0:T(8,128)S(1)}, f32[2,128,128]{2,1,0:T(8,128)S(1)}, u32[]{:S(2)}, u32[]{:S(2)}) collective-permute-start(f32[2,128,128]{2,1,0:T(8,128)S(1)} %shard_map.145.own_ref), channel_id=1, source_target_pairs={{0,16},{16,0},{32,48},{48,32},{64,80},{80,64},{96,112},{112,96},{1... | collective-permute-start | bytes 393224 | tf_op jit(solution)/shard_map/ppermute | solution.py:611
  60.3 0.2 shard_map.146.rank_ref
  60.5 1.7 collective-permute-done.5.left_far.left_ref
  62.2 1.8 %collective-permute-done.6.right_far.right_ref = bf16[512,1024]{1,0:T(8,128)(2,1)S(1)} collective-permute-done((bf16[512,1024]{1,0:T(8,128)(2,1)}, bf16[512,1024]{1,0:T(8,128)(2,1)S(1)}, u32[]{:S(2)}, u32[]{:S(2)}) %collective-permute-start.6) | collective-permute-done | bytes 1048608 | tf_op jit(solution)/shard_map/ppermute | solution.py:592
  64.0 0.0 collective-permute-done.4.got_ref
  64.0 0.0 copy-done
  64.0 0.0 copy-done.4
  64.0 0.0 copy-done.7
  64.0 1.0 shard_map.147
  65.0 0.0 copy-start.1
  65.0 0.8 copy-done.1
  65.8 24.3 %all-to-all-start.2 = ((bf16[512,2,256]{2,1,0:T(2,128)(2,1)}), bf16[512,2,256]{2,1,0:T(2,128)(2,1)}, u32[]{:S(2)}, u32[]{:S(2)}) async-start(bf16[512,2,256]{2,1,0:T(2,128)(2,1)} %copy-done.1), calls=%async_computation.2 | async-start | bytes 1048576 | tf_op jit(solution)/shard_map/all_to_all | solution.py:515
  90.1 0.0 copy-start.10
  90.1 0.8 slice.14
  90.9 3.3 %collective-permute-start.7 = (bf16[256,1024]{1,0:T(8,128)(2,1)}, bf16[256,1024]{1,0:T(8,128)(2,1)}, u32[]{:S(2)}, u32[]{:S(2)}) collective-permute-start(bf16[256,1024]{1,0:T(8,128)(2,1)} %slice.14), channel_id=1, source_target_pairs={{0,4},{4,8},{8,12},{12,0},{1,5},{5,9},{9,13},{13,1},{2,6},{6,10},{... | collective-permute-start | bytes 1572872 | tf_op jit(solution)/shard_map/ppermute | solution.py:593
  94.2 0.9 slice.15
  95.1 3.2 %collective-permute-start.8 = (bf16[256,1024]{1,0:T(8,128)(2,1)}, bf16[256,1024]{1,0:T(8,128)(2,1)}, u32[]{:S(2)}, u32[]{:S(2)}) collective-permute-start(bf16[256,1024]{1,0:T(8,128)(2,1)} %slice.15), channel_id=1, source_target_pairs={{4,0},{8,4},{12,8},{0,12},{5,1},{9,5},{13,9},{1,13},{6,2},{10,6},{... | collective-permute-start | bytes 1572872 | tf_op jit(solution)/shard_map/ppermute | solution.py:593
  98.3 0.0 copy-done.10
  98.3 1.4 shard_map.148
  99.7 0.0 copy-start.2
  99.7 0.8 copy-done.2
  100.5 6.3 %collective-permute-done.7.upper_ref = bf16[256,1024]{1,0:T(8,128)(2,1)} collective-permute-done((bf16[256,1024]{1,0:T(8,128)(2,1)}, bf16[256,1024]{1,0:T(8,128)(2,1)}, u32[]{:S(2)}, u32[]{:S(2)}) %collective-permute-start.7) | collective-permute-done | bytes 524320 | tf_op jit(solution)/shard_map/ppermute | solution.py:593
  106.7 4.4 %collective-permute-done.8.lower_ref = bf16[256,1024]{1,0:T(8,128)(2,1)} collective-permute-done((bf16[256,1024]{1,0:T(8,128)(2,1)}, bf16[256,1024]{1,0:T(8,128)(2,1)}, u32[]{:S(2)}, u32[]{:S(2)}) %collective-permute-start.8) | collective-permute-done | bytes 524320 | tf_op jit(solution)/shard_map/ppermute | solution.py:593
  111.2 13.1 %all-to-all-done.2.rows_ref = bf16[512,2,256]{2,1,0:T(2,128)(2,1)} async-done(((bf16[512,2,256]{2,1,0:T(2,128)(2,1)}), bf16[512,2,256]{2,1,0:T(2,128)(2,1)}, u32[]{:S(2)}, u32[]{:S(2)}) %all-to-all-start.2) | async-done | bytes 524320 | tf_op jit(solution)/shard_map/all_to_all | solution.py:515
  124.2 3.7 %shard_map.149 = bf16[512,2,256]{2,1,0:T(2,128)(2,1)S(1)} custom-call(s32[1]{0:T(128)} %bitcast.12.coarse_ref, bf16[512,2,256]{2,1,0:T(2,128)(2,1)} %all-to-all-done.2.rows_ref, bf16[4,1,256]{2,1,0:T(2,128)(2,1)S(1)} %reshape.4.ext_ref, bf16[512,1024]{1,0:T(8,128)(2,1)} %get-tuple-element.35.own_ref, ...), custom_call_target="tpu_custom_call" | custom-call | flops 100000 | bytes 1000 | tf_op jit(solution)/shard_map/pallas_call | solution.py:473
  128.0 0.0 copy-start.3
  128.0 46.3 %all_to_all.20.back_ref = bf16[512,2,256]{2,1,0:T(2,128)(2,1)S(1)} all-to-all(bf16[512,2,256]{2,1,0:T(2,128)(2,1)S(1)} %shard_map.149), channel_id=1, replica_groups=mesh['seq'=32,'coarse'=4,'exp'=4] {'coarse','seq','exp'}, dimensions={0} | all-to-all | bytes 1048576 | tf_op jit(solution)/shard_map/all_to_all | solution.py:515
  174.3 0.0 copy-done.3
  174.3 0.4 shard_map.150
  174.7 1.9 %collective-permute-start.9 = (f32[1,256]{1,0:T(1,128)S(1)}, f32[1,256]{1,0:T(1,128)S(1)}, u32[]{:S(2)}, u32[]{:S(2)}) collective-permute-start(f32[1,256]{1,0:T(1,128)S(1)} %get-tuple-element.44), channel_id=1, source_target_pairs={{0,16},{16,32},{32,48},{48,64},{64,80},{80,96},{96,112},{112,128},... | collective-permute-start | bytes 3080 | tf_op jit(solution)/shard_map/ppermute | solution.py:643
  176.6 0.3 shard_map.151
  176.9 0.8 collective-permute-done.9.prev_ref
  177.7 0.8 shard_map.152
  (8 shorter events, 0.1 us)
Async XLA Ops:
  3.1 17.5 %all-to-all-start = ((bf16[4,528,256]{2,1,0:T(8,128)(2,1)}), bf16[4,528,256]{2,1,0:T(8,128)(2,1)S(1)}, u32[]{:S(2)}, u32[]{:S(2)}) async-start(bf16[4,528,256]{2,1,0:T(8,128)(2,1)} %shard_map.138), calls=%async_computation | async-start | bytes 2162688 | tf_op jit(solution)/shard_map/all_to_all | solution.py:515
  20.6 7.5 %copy-start.5 = (f32[128,256]{1,0:T(8,128)S(1)}, f32[128,256]{1,0:T(8,128)}, u32[]{:S(2)}) copy-start(f32[128,256]{1,0:T(8,128)} %get-tuple-element.26.own_ref) | copy-start | bytes 393220
  20.6 8.6 %collective-permute-start = (f32[128,256]{1,0:T(8,128)}, f32[128,256]{1,0:T(8,128)S(1)}, u32[]{:S(2)}, u32[]{:S(2)}) collective-permute-start(f32[128,256]{1,0:T(8,128)} %shard_map.139), channel_id=1, source_target_pairs={{0,16},{16,0},{32,48},{48,32},{64,80},{80,64},{96,112},{112,96},{1... | collective-permute-start | bytes 393224 | tf_op jit(solution)/shard_map/ppermute | solution.py:572
  30.2 0.7 copy-start.8
  30.8 11.7 %all-to-all-start.1 = ((bf16[4,128,256]{2,1,0:T(8,128)(2,1)}), bf16[4,128,256]{2,1,0:T(8,128)(2,1)S(1)}, u32[]{:S(2)}, u32[]{:S(2)}) async-start(bf16[4,128,256]{2,1,0:T(8,128)(2,1)} %get-tuple-element.28), calls=%async_computation.1 | async-start | bytes 524288 | tf_op jit(solution)/shard_map/all_to_all | solution.py:515
  34.8 27.4 %collective-permute-start.5 = (bf16[512,1024]{1,0:T(8,128)(2,1)}, bf16[512,1024]{1,0:T(8,128)(2,1)S(1)}, u32[]{:S(2)}, u32[]{:S(2)}) collective-permute-start(bf16[512,1024]{1,0:T(8,128)(2,1)} %get-tuple-element.35.own_ref), channel_id=1, source_target_pairs={{0,4},{4,8},{8,12},{12,0},{1,5},{5,9},{9,13},{13,1},{2,6},{6,10},{... | collective-permute-start | bytes 3145736 | tf_op jit(solution)/shard_map/ppermute | solution.py:591
  37.9 26.2 %collective-permute-start.6 = (bf16[512,1024]{1,0:T(8,128)(2,1)}, bf16[512,1024]{1,0:T(8,128)(2,1)S(1)}, u32[]{:S(2)}, u32[]{:S(2)}) collective-permute-start(bf16[512,1024]{1,0:T(8,128)(2,1)} %get-tuple-element.35.own_ref), channel_id=1, source_target_pairs={{4,0},{8,4},{12,8},{0,12},{5,1},{9,5},{13,9},{1,13},{6,2},{10,6},{... | collective-permute-start | bytes 3145736 | tf_op jit(solution)/shard_map/ppermute | solution.py:592
  42.5 9.5 %copy-start.6 = (s32[1,512]{1,0:T(1,128)S(1)}, s32[1,512]{1,0:T(1,128)}, u32[]{:S(2)}) copy-start(s32[1,512]{1,0:T(1,128)} %mask_ref.9) | copy-start | bytes 6148
  43.2 9.8 %collective-permute-start.1 = (bf16[128,128]{1,0:T(8,128)(2,1)S(1)}, bf16[128,128]{1,0:T(8,128)(2,1)S(1)}, u32[]{:S(2)}, u32[]{:S(2)}) collective-permute-start(bf16[128,128]{1,0:T(8,128)(2,1)S(1)} %slice.17), channel_id=1, source_target_pairs={{0,128},{16,144},{32,160},{48,176},{64,192},{80,208},{96,224},{112... | collective-permute-start | bytes 98312 | tf_op jit(solution)/shard_map/ppermute | solution.py:609
  53.2 0.7 collective-permute-start.2
  53.9 0.9 copy-start.9
  54.1 0.7 collective-permute-start.3
  54.8 9.2 %copy-start = (f32[2,512,256]{2,1,0:T(8,128)S(1)}, f32[2,512,256]{2,1,0:T(8,128)}, u32[]{:S(2)}) copy-start(f32[2,512,256]{2,1,0:T(8,128)} %get-tuple-element.25.local_ref) | copy-start | bytes 3145732
  54.8 9.2 %copy-start.4 = (bf16[512,256]{1,0:T(8,128)(2,1)S(1)}, bf16[512,256]{1,0:T(8,128)(2,1)}, u32[]{:S(2)}) copy-start(bf16[512,256]{1,0:T(8,128)(2,1)} %get-tuple-element.33.x_ref) | copy-start | bytes 786436
  54.8 9.2 %copy-start.7 = (f32[256]{0:T(256)S(1)}, f32[256]{0:T(256)}, u32[]{:S(2)}) copy-start(f32[256]{0:T(256)} %param.20) | copy-start | bytes 3076
  55.2 8.8 %collective-permute-start.4 = (f32[2,128,128]{2,1,0:T(8,128)S(1)}, f32[2,128,128]{2,1,0:T(8,128)S(1)}, u32[]{:S(2)}, u32[]{:S(2)}) collective-permute-start(f32[2,128,128]{2,1,0:T(8,128)S(1)} %shard_map.145.own_ref), channel_id=1, source_target_pairs={{0,16},{16,0},{32,48},{48,32},{64,80},{80,64},{96,112},{112,96},{1... | collective-permute-start | bytes 393224 | tf_op jit(solution)/shard_map/ppermute | solution.py:611
  65.0 0.8 copy-start.1
  65.8 58.4 %all-to-all-start.2 = ((bf16[512,2,256]{2,1,0:T(2,128)(2,1)}), bf16[512,2,256]{2,1,0:T(2,128)(2,1)}, u32[]{:S(2)}, u32[]{:S(2)}) async-start(bf16[512,2,256]{2,1,0:T(2,128)(2,1)} %copy-done.1), calls=%async_computation.2 | async-start | bytes 1048576 | tf_op jit(solution)/shard_map/all_to_all | solution.py:515
  90.1 8.2 %copy-start.10 = (bf16[1024]{0:T(1024)(128)(2,1)S(1)}, bf16[1024]{0:T(1024)(128)(2,1)}, u32[]{:S(2)}) copy-start(bf16[1024]{0:T(1024)(128)(2,1)} %param.24) | copy-start | bytes 6148
  90.9 15.8 %collective-permute-start.7 = (bf16[256,1024]{1,0:T(8,128)(2,1)}, bf16[256,1024]{1,0:T(8,128)(2,1)}, u32[]{:S(2)}, u32[]{:S(2)}) collective-permute-start(bf16[256,1024]{1,0:T(8,128)(2,1)} %slice.14), channel_id=1, source_target_pairs={{0,4},{4,8},{8,12},{12,0},{1,5},{5,9},{9,13},{13,1},{2,6},{6,10},{... | collective-permute-start | bytes 1572872 | tf_op jit(solution)/shard_map/ppermute | solution.py:593
  95.1 16.1 %collective-permute-start.8 = (bf16[256,1024]{1,0:T(8,128)(2,1)}, bf16[256,1024]{1,0:T(8,128)(2,1)}, u32[]{:S(2)}, u32[]{:S(2)}) collective-permute-start(bf16[256,1024]{1,0:T(8,128)(2,1)} %slice.15), channel_id=1, source_target_pairs={{4,0},{8,4},{12,8},{0,12},{5,1},{9,5},{13,9},{1,13},{6,2},{10,6},{... | collective-permute-start | bytes 1572872 | tf_op jit(solution)/shard_map/ppermute | solution.py:593
  99.7 0.8 copy-start.2
  128.0 46.3 %copy-start.3 = (f32[4,256,32]{2,1,0:T(8,128)S(1)}, f32[4,256,32]{2,1,0:T(8,128)}, u32[]{:S(2)}) copy-start(f32[4,256,32]{2,1,0:T(8,128)} %copy-done.2) | copy-start | bytes 393220
  174.7 3.0 %collective-permute-start.9 = (f32[1,256]{1,0:T(1,128)S(1)}, f32[1,256]{1,0:T(1,128)S(1)}, u32[]{:S(2)}, u32[]{:S(2)}) collective-permute-start(f32[1,256]{1,0:T(1,128)S(1)} %get-tuple-element.44), channel_id=1, source_target_pairs={{0,16},{16,32},{32,48},{48,64},{64,80},{80,96},{96,112},{112,128},... | collective-permute-start | bytes 3080 | tf_op jit(solution)/shard_map/ppermute | solution.py:643

commit v8 on v7

--- a/solution.py
+++ b/solution.py
@@ -36,14 +36,11 @@
     return jnp.sum(jnp.where(eye, column, 0.0), axis=0, keepdims=True)
 
 
-def choice_kernel(picks_ref, gates_ref, edown_far, out_ref, build, sems):
+def choice_kernel(picks_ref, gates_ref, edown_far, out_far, build, tile, sems):
     top, slots = picks_ref.shape
     depth = edown_far.shape[1]
-    moves = [
-        pltpu.make_async_copy(edown_far.at[0], out_ref.at[n, pl.ds(0, depth)], sems.at[n]) for n in range(GROUP)
-    ]
-    for move in moves:
-        move.start()
+    arrive = pltpu.make_async_copy(edown_far.at[0], tile.at[pl.ds(0, depth)], sems.at[GROUP])
+    arrive.start()
     build[...] = jnp.zeros_like(build)
     gates = gates_ref[...]
     high = gates.astype(bf16).astype(f32)
@@ -51,8 +48,11 @@
     build[:top, :slots] = picks_ref[...].astype(f32)
     build[:top, half : half + slots] = high
     build[top:, half : half + slots] = gates - high
-    for n in range(GROUP):
-        out_ref[n, depth:] = build[...].astype(bf16)
+    tile[depth:] = build[...].astype(bf16)
+    arrive.wait()
+    moves = [pltpu.make_async_copy(tile, out_far.at[n], sems.at[n]) for n in range(GROUP)]
+    for move in moves:
+        move.start()
     for move in moves:
         move.wait()
 
@@ -519,9 +519,14 @@
         choice_kernel,
         sds((GROUP, expert_down.shape[1] + 2 * top, HALF), bf16),
         (picks[0].T, pick_gates[0].T, expert_down),
-        scratch=(pltpu.VMEM((2 * top, HALF), f32), pltpu.SemaphoreType.DMA((GROUP,))),
+        scratch=(
+            pltpu.VMEM((2 * top, HALF), f32),
+            pltpu.VMEM((expert_down.shape[1] + 2 * top, HALF), bf16),
+            pltpu.SemaphoreType.DMA((GROUP + 1,)),
+        ),
         megabytes=63,
         far_in=(2,),
+        far_out=(0,),
     )
     shared = exchange(shared, "coarse")
     table = (pltpu.VMEM((GROUP, 2 * top, HALF), bf16), pltpu.SemaphoreType.DMA)

time: 179 us -> 179 us (level)
  no operation moved by 1% of the time
where the time goes in v8:
time: 179 us; the launch traced here: 178 us
  starting transfers between devices  70.8 us (40%)
  blocking collectives  46.3 us (26%)
  waiting for transfers between devices  30.8 us (17%)
  Pallas kernels  25.9 us (14%)
  local copies, waits for them, and re-layouts  3.97 us (2%)
    all_to_all x1, blocking collectives, exchange(): lax.all_to_all(array, axes, split_axis=0, concat_axis=0, tiled=True, **kw...  46.3 us
    all_to_all x3, starting transfers between devices, exchange(): lax.all_to_all(array, axes, split_axis=0, concat_axis=0, tiled=True, **kw...  33.3 us
    pallas_call x17, Pallas kernels, call(): pl.pallas_call(kernel, out_shape=outs, in_specs=[spec(far_in, i - scalars...  25.9 us
    all_to_all x3, waiting for transfers between devices, exchange(): lax.all_to_all(array, axes, split_axis=0, concat_axis=0, tiled=True, **kw...  14.3 us
    ppermute x3, starting transfers between devices, shards(): state = state + lax.ppermute(outgoing, 'seq', pairs)  10.1 us
    ppermute x1, starting transfers between devices, shards(): got = lax.ppermute(give, 'seq', swap)  7.44 us
    ppermute x1, waiting for transfers between devices, shards(): lax.ppermute(left[:half], 'coarse', ring)  6.28 us
    ppermute x1, starting transfers between devices, shards(): others = lax.ppermute(states, 'seq', swap)  5.06 us
  transfers between devices with their start and end apart: 13, of which 9 were waited for; matrix products, arithmetic and copies ran while one was open for 1% of the time, Pallas kernels for 9%

profile of v8, /device:TPU:1, one launch (start us, length us, event | category | flops | bytes accessed | tf_op | source)
XLA Modules:
  0.0 178.1 jit_solution(14486197770630513545)
XLA Ops:
  0.0 2.7 %shard_map.138 = bf16[4,528,256]{2,1,0:T(8,128)(2,1)} custom-call(s32[8,32]{1,0:T(8,128)} %bitcast.17, f32[8,32]{1,0:T(8,128)} %bitcast.18, bf16[1,512,256]{2,1,0:T(8,128)(2,1)} %edown_far.1), custom_call_target="tpu_custom_call" | custom-call | flops 100000 | bytes 1000 | tf_op jit(solution)/shard_map/pallas_call | solution.py:473
  2.7 5.0 %all-to-all-start = ((bf16[4,528,256]{2,1,0:T(8,128)(2,1)}), bf16[4,528,256]{2,1,0:T(8,128)(2,1)S(1)}, u32[]{:S(2)}, u32[]{:S(2)}) async-start(bf16[4,528,256]{2,1,0:T(8,128)(2,1)} %shard_map.138), calls=%async_computation | async-start | bytes 2162688 | tf_op jit(solution)/shard_map/all_to_all | solution.py:515
  7.7 12.4 %shard_map.136 = (f32[128,256]{1,0:T(8,128)}, f32[128,256]{1,0:T(8,128)}, f32[2,512,256]{2,1,0:T(8,128)}, bf16[512,256]{1,0:T(8,128)(2,1)}, bf16[512,1024]{1,0:T(8,128)(2,1)}) custom-call(bf16[512,1024]{1,0:T(8,128)(2,1)} %bitcast.19, f32[1,1024]{1,0:T(1,128)} %bitcast.21, bf16[3,1024,256]{2,1,0:T(8,128)(2,1)} %w_far.1, bf16[2,2,1024]{2,1,0:T(2,128)(2,1)} %bitcast.20, ...), custom_call_target="tpu_custom_call" | custom-call | flops 2000000000 | bytes 20000000 | tf_op jit(solution)/shard_map/pallas_call | solution.py:473
  20.2 0.0 copy-start.5
  20.2 0.0 all-to-all-done.choice_far.shared_far.down_ref
  20.2 7.4 %collective-permute-start = (f32[128,256]{1,0:T(8,128)}, f32[128,256]{1,0:T(8,128)S(1)}, u32[]{:S(2)}, u32[]{:S(2)}) collective-permute-start(f32[128,256]{1,0:T(8,128)} %shard_map.139), channel_id=1, source_target_pairs={{0,16},{16,0},{32,48},{48,32},{64,80},{80,64},{96,112},{112,96},{1... | collective-permute-start | bytes 393224 | tf_op jit(solution)/shard_map/ppermute | solution.py:577
  27.6 0.0 copy-done.5
  27.7 1.1 collective-permute-done.got_ref
  28.8 0.9 shard_map.140
  29.7 0.0 copy-start.8
  29.7 0.7 copy-done.8
  30.4 4.0 %all-to-all-start.1 = ((bf16[4,128,256]{2,1,0:T(8,128)(2,1)}), bf16[4,128,256]{2,1,0:T(8,128)(2,1)S(1)}, u32[]{:S(2)}, u32[]{:S(2)}) async-start(bf16[4,128,256]{2,1,0:T(8,128)(2,1)} %get-tuple-element.28), calls=%async_computation.1 | async-start | bytes 524288 | tf_op jit(solution)/shard_map/all_to_all | solution.py:515
  34.4 3.0 %collective-permute-start.5 = (bf16[512,1024]{1,0:T(8,128)(2,1)}, bf16[512,1024]{1,0:T(8,128)(2,1)S(1)}, u32[]{:S(2)}, u32[]{:S(2)}) collective-permute-start(bf16[512,1024]{1,0:T(8,128)(2,1)} %get-tuple-element.35.own_ref), channel_id=1, source_target_pairs={{0,4},{4,8},{8,12},{12,0},{1,5},{5,9},{9,13},{13,1},{2,6},{6,10},{... | collective-permute-start | bytes 3145736 | tf_op jit(solution)/shard_map/ppermute | solution.py:596
  37.4 3.5 %collective-permute-start.6 = (bf16[512,1024]{1,0:T(8,128)(2,1)}, bf16[512,1024]{1,0:T(8,128)(2,1)S(1)}, u32[]{:S(2)}, u32[]{:S(2)}) collective-permute-start(bf16[512,1024]{1,0:T(8,128)(2,1)} %get-tuple-element.35.own_ref), channel_id=1, source_target_pairs={{4,0},{8,4},{12,8},{0,12},{5,1},{9,5},{13,9},{1,13},{6,2},{10,6},{... | collective-permute-start | bytes 3145736 | tf_op jit(solution)/shard_map/ppermute | solution.py:597
  40.9 1.2 all-to-all-done.1.got_ref
  42.1 0.6 shard_map.141
  42.8 8.8 %collective-permute-start.1 = (bf16[128,128]{1,0:T(8,128)(2,1)S(1)}, bf16[128,128]{1,0:T(8,128)(2,1)S(1)}, u32[]{:S(2)}, u32[]{:S(2)}) collective-permute-start(bf16[128,128]{1,0:T(8,128)(2,1)S(1)} %slice.17), channel_id=1, source_target_pairs={{0,128},{16,144},{32,160},{48,176},{64,192},{80,208},{96,224},{112... | collective-permute-start | bytes 98312 | tf_op jit(solution)/shard_map/ppermute | solution.py:614
  51.6 0.0 copy-done.6
  51.6 0.7 shard_map.142
  52.3 0.3 collective-permute-done.1.state_ref
  52.6 0.2 shard_map.143
  52.8 0.7 collective-permute-start.2
  53.4 0.0 collective-permute-done.2
  53.5 0.0 copy-start.9
  53.5 0.2 shard_map.144
  53.7 0.7 collective-permute-start.3
  54.3 0.0 collective-permute-done.3
  54.4 0.0 copy-done.9
  54.4 0.0 copy-start.4
  54.4 0.0 copy-start.7
  54.4 0.4 shard_map.145.own_ref
  54.8 5.1 %collective-permute-start.4 = (f32[2,128,128]{2,1,0:T(8,128)S(1)}, f32[2,128,128]{2,1,0:T(8,128)S(1)}, u32[]{:S(2)}, u32[]{:S(2)}) collective-permute-start(f32[2,128,128]{2,1,0:T(8,128)S(1)} %shard_map.145.own_ref), channel_id=1, source_target_pairs={{0,16},{16,0},{32,48},{48,32},{64,80},{80,64},{96,112},{112,96},{1... | collective-permute-start | bytes 393224 | tf_op jit(solution)/shard_map/ppermute | solution.py:616
  59.8 0.2 shard_map.146.rank_ref
  60.0 1.7 collective-permute-done.5.left_far.left_ref
  61.8 1.8 %collective-permute-done.6.right_far.right_ref = bf16[512,1024]{1,0:T(8,128)(2,1)S(1)} collective-permute-done((bf16[512,1024]{1,0:T(8,128)(2,1)}, bf16[512,1024]{1,0:T(8,128)(2,1)S(1)}, u32[]{:S(2)}, u32[]{:S(2)}) %collective-permute-start.6) | collective-permute-done | bytes 1048608 | tf_op jit(solution)/shard_map/ppermute | solution.py:597
  63.6 0.0 collective-permute-done.4.got_ref
  63.6 0.0 copy-done
  63.6 0.0 copy-done.4
  63.6 0.0 copy-done.7
  63.6 1.0 shard_map.147
  64.6 0.0 copy-start.1
  64.6 0.8 copy-done.1
  65.4 24.3 %all-to-all-start.2 = ((bf16[512,2,256]{2,1,0:T(2,128)(2,1)}), bf16[512,2,256]{2,1,0:T(2,128)(2,1)}, u32[]{:S(2)}, u32[]{:S(2)}) async-start(bf16[512,2,256]{2,1,0:T(2,128)(2,1)} %copy-done.1), calls=%async_computation.2 | async-start | bytes 1048576 | tf_op jit(solution)/shard_map/all_to_all | solution.py:515
  89.7 0.0 copy-start.10
  89.7 0.8 slice.14
  90.5 3.3 %collective-permute-start.7 = (bf16[256,1024]{1,0:T(8,128)(2,1)}, bf16[256,1024]{1,0:T(8,128)(2,1)}, u32[]{:S(2)}, u32[]{:S(2)}) collective-permute-start(bf16[256,1024]{1,0:T(8,128)(2,1)} %slice.14), channel_id=1, source_target_pairs={{0,4},{4,8},{8,12},{12,0},{1,5},{5,9},{9,13},{13,1},{2,6},{6,10},{... | collective-permute-start | bytes 1572872 | tf_op jit(solution)/shard_map/ppermute | solution.py:598
  93.8 0.9 slice.15
  94.6 3.2 %collective-permute-start.8 = (bf16[256,1024]{1,0:T(8,128)(2,1)}, bf16[256,1024]{1,0:T(8,128)(2,1)}, u32[]{:S(2)}, u32[]{:S(2)}) collective-permute-start(bf16[256,1024]{1,0:T(8,128)(2,1)} %slice.15), channel_id=1, source_target_pairs={{4,0},{8,4},{12,8},{0,12},{5,1},{9,5},{13,9},{1,13},{6,2},{10,6},{... | collective-permute-start | bytes 1572872 | tf_op jit(solution)/shard_map/ppermute | solution.py:598
  97.8 0.0 copy-done.10
  97.9 1.4 shard_map.148
  99.2 0.0 copy-start.2
  99.2 0.8 copy-done.2
  100.0 6.3 %collective-permute-done.7.upper_ref = bf16[256,1024]{1,0:T(8,128)(2,1)} collective-permute-done((bf16[256,1024]{1,0:T(8,128)(2,1)}, bf16[256,1024]{1,0:T(8,128)(2,1)}, u32[]{:S(2)}, u32[]{:S(2)}) %collective-permute-start.7) | collective-permute-done | bytes 524320 | tf_op jit(solution)/shard_map/ppermute | solution.py:598
  106.3 4.4 %collective-permute-done.8.lower_ref = bf16[256,1024]{1,0:T(8,128)(2,1)} collective-permute-done((bf16[256,1024]{1,0:T(8,128)(2,1)}, bf16[256,1024]{1,0:T(8,128)(2,1)}, u32[]{:S(2)}, u32[]{:S(2)}) %collective-permute-start.8) | collective-permute-done | bytes 524320 | tf_op jit(solution)/shard_map/ppermute | solution.py:598
  110.7 13.1 %all-to-all-done.2.rows_ref = bf16[512,2,256]{2,1,0:T(2,128)(2,1)} async-done(((bf16[512,2,256]{2,1,0:T(2,128)(2,1)}), bf16[512,2,256]{2,1,0:T(2,128)(2,1)}, u32[]{:S(2)}, u32[]{:S(2)}) %all-to-all-start.2) | async-done | bytes 524320 | tf_op jit(solution)/shard_map/all_to_all | solution.py:515
  123.8 3.7 %shard_map.149 = bf16[512,2,256]{2,1,0:T(2,128)(2,1)S(1)} custom-call(s32[1]{0:T(128)} %bitcast.12.coarse_ref, bf16[512,2,256]{2,1,0:T(2,128)(2,1)} %all-to-all-done.2.rows_ref, bf16[4,1,256]{2,1,0:T(2,128)(2,1)S(1)} %reshape.4.ext_ref, bf16[512,1024]{1,0:T(8,128)(2,1)} %get-tuple-element.35.own_ref, ...), custom_call_target="tpu_custom_call" | custom-call | flops 100000 | bytes 1000 | tf_op jit(solution)/shard_map/pallas_call | solution.py:473
  127.6 0.0 copy-start.3
  127.6 46.3 %all_to_all.20.back_ref = bf16[512,2,256]{2,1,0:T(2,128)(2,1)S(1)} all-to-all(bf16[512,2,256]{2,1,0:T(2,128)(2,1)S(1)} %shard_map.149), channel_id=1, replica_groups=mesh['seq'=32,'coarse'=4,'exp'=4] {'coarse','seq','exp'}, dimensions={0} | all-to-all | bytes 1048576 | tf_op jit(solution)/shard_map/all_to_all | solution.py:515
  173.8 0.0 copy-done.3
  173.8 0.4 shard_map.150
  174.2 1.9 %collective-permute-start.9 = (f32[1,256]{1,0:T(1,128)S(1)}, f32[1,256]{1,0:T(1,128)S(1)}, u32[]{:S(2)}, u32[]{:S(2)}) collective-permute-start(f32[1,256]{1,0:T(1,128)S(1)} %get-tuple-element.44), channel_id=1, source_target_pairs={{0,16},{16,32},{32,48},{48,64},{64,80},{80,96},{96,112},{112,128},... | collective-permute-start | bytes 3080 | tf_op jit(solution)/shard_map/ppermute | solution.py:648
  176.2 0.3 shard_map.151
  176.5 0.8 collective-permute-done.9.prev_ref
  177.3 0.8 shard_map.152
  (8 shorter events, 0.1 us)
Async XLA Ops:
  2.7 17.5 %all-to-all-start = ((bf16[4,528,256]{2,1,0:T(8,128)(2,1)}), bf16[4,528,256]{2,1,0:T(8,128)(2,1)S(1)}, u32[]{:S(2)}, u32[]{:S(2)}) async-start(bf16[4,528,256]{2,1,0:T(8,128)(2,1)} %shard_map.138), calls=%async_computation | async-start | bytes 2162688 | tf_op jit(solution)/shard_map/all_to_all | solution.py:515
  20.2 7.5 %copy-start.5 = (f32[128,256]{1,0:T(8,128)S(1)}, f32[128,256]{1,0:T(8,128)}, u32[]{:S(2)}) copy-start(f32[128,256]{1,0:T(8,128)} %get-tuple-element.26.own_ref) | copy-start | bytes 393220
  20.2 8.6 %collective-permute-start = (f32[128,256]{1,0:T(8,128)}, f32[128,256]{1,0:T(8,128)S(1)}, u32[]{:S(2)}, u32[]{:S(2)}) collective-permute-start(f32[128,256]{1,0:T(8,128)} %shard_map.139), channel_id=1, source_target_pairs={{0,16},{16,0},{32,48},{48,32},{64,80},{80,64},{96,112},{112,96},{1... | collective-permute-start | bytes 393224 | tf_op jit(solution)/shard_map/ppermute | solution.py:577
  29.7 0.7 copy-start.8
  30.4 11.7 %all-to-all-start.1 = ((bf16[4,128,256]{2,1,0:T(8,128)(2,1)}), bf16[4,128,256]{2,1,0:T(8,128)(2,1)S(1)}, u32[]{:S(2)}, u32[]{:S(2)}) async-start(bf16[4,128,256]{2,1,0:T(8,128)(2,1)} %get-tuple-element.28), calls=%async_computation.1 | async-start | bytes 524288 | tf_op jit(solution)/shard_map/all_to_all | solution.py:515
  34.4 27.4 %collective-permute-start.5 = (bf16[512,1024]{1,0:T(8,128)(2,1)}, bf16[512,1024]{1,0:T(8,128)(2,1)S(1)}, u32[]{:S(2)}, u32[]{:S(2)}) collective-permute-start(bf16[512,1024]{1,0:T(8,128)(2,1)} %get-tuple-element.35.own_ref), channel_id=1, source_target_pairs={{0,4},{4,8},{8,12},{12,0},{1,5},{5,9},{9,13},{13,1},{2,6},{6,10},{... | collective-permute-start | bytes 3145736 | tf_op jit(solution)/shard_map/ppermute | solution.py:596
  37.4 26.2 %collective-permute-start.6 = (bf16[512,1024]{1,0:T(8,128)(2,1)}, bf16[512,1024]{1,0:T(8,128)(2,1)S(1)}, u32[]{:S(2)}, u32[]{:S(2)}) collective-permute-start(bf16[512,1024]{1,0:T(8,128)(2,1)} %get-tuple-element.35.own_ref), channel_id=1, source_target_pairs={{4,0},{8,4},{12,8},{0,12},{5,1},{9,5},{13,9},{1,13},{6,2},{10,6},{... | collective-permute-start | bytes 3145736 | tf_op jit(solution)/shard_map/ppermute | solution.py:597
  42.1 9.5 %copy-start.6 = (s32[1,512]{1,0:T(1,128)S(1)}, s32[1,512]{1,0:T(1,128)}, u32[]{:S(2)}) copy-start(s32[1,512]{1,0:T(1,128)} %mask_ref.9) | copy-start | bytes 6148
  42.8 9.8 %collective-permute-start.1 = (bf16[128,128]{1,0:T(8,128)(2,1)S(1)}, bf16[128,128]{1,0:T(8,128)(2,1)S(1)}, u32[]{:S(2)}, u32[]{:S(2)}) collective-permute-start(bf16[128,128]{1,0:T(8,128)(2,1)S(1)} %slice.17), channel_id=1, source_target_pairs={{0,128},{16,144},{32,160},{48,176},{64,192},{80,208},{96,224},{112... | collective-permute-start | bytes 98312 | tf_op jit(solution)/shard_map/ppermute | solution.py:614
  52.8 0.7 collective-permute-start.2
  53.5 0.9 copy-start.9
  53.7 0.7 collective-permute-start.3
  54.4 9.2 %copy-start = (f32[2,512,256]{2,1,0:T(8,128)S(1)}, f32[2,512,256]{2,1,0:T(8,128)}, u32[]{:S(2)}) copy-start(f32[2,512,256]{2,1,0:T(8,128)} %get-tuple-element.25.local_ref) | copy-start | bytes 3145732
  54.4 9.2 %copy-start.4 = (bf16[512,256]{1,0:T(8,128)(2,1)S(1)}, bf16[512,256]{1,0:T(8,128)(2,1)}, u32[]{:S(2)}) copy-start(bf16[512,256]{1,0:T(8,128)(2,1)} %get-tuple-element.33.x_ref) | copy-start | bytes 786436
  54.4 9.2 %copy-start.7 = (f32[256]{0:T(256)S(1)}, f32[256]{0:T(256)}, u32[]{:S(2)}) copy-start(f32[256]{0:T(256)} %param.20) | copy-start | bytes 3076
  54.8 8.8 %collective-permute-start.4 = (f32[2,128,128]{2,1,0:T(8,128)S(1)}, f32[2,128,128]{2,1,0:T(8,128)S(1)}, u32[]{:S(2)}, u32[]{:S(2)}) collective-permute-start(f32[2,128,128]{2,1,0:T(8,128)S(1)} %shard_map.145.own_ref), channel_id=1, source_target_pairs={{0,16},{16,0},{32,48},{48,32},{64,80},{80,64},{96,112},{112,96},{1... | collective-permute-start | bytes 393224 | tf_op jit(solution)/shard_map/ppermute | solution.py:616
  64.6 0.8 copy-start.1
  65.4 58.4 %all-to-all-start.2 = ((bf16[512,2,256]{2,1,0:T(2,128)(2,1)}), bf16[512,2,256]{2,1,0:T(2,128)(2,1)}, u32[]{:S(2)}, u32[]{:S(2)}) async-start(bf16[512,2,256]{2,1,0:T(2,128)(2,1)} %copy-done.1), calls=%async_computation.2 | async-start | bytes 1048576 | tf_op jit(solution)/shard_map/all_to_all | solution.py:515
  89.7 8.2 %copy-start.10 = (bf16[1024]{0:T(1024)(128)(2,1)S(1)}, bf16[1024]{0:T(1024)(128)(2,1)}, u32[]{:S(2)}) copy-start(bf16[1024]{0:T(1024)(128)(2,1)} %param.24) | copy-start | bytes 6148
  90.5 15.8 %collective-permute-start.7 = (bf16[256,1024]{1,0:T(8,128)(2,1)}, bf16[256,1024]{1,0:T(8,128)(2,1)}, u32[]{:S(2)}, u32[]{:S(2)}) collective-permute-start(bf16[256,1024]{1,0:T(8,128)(2,1)} %slice.14), channel_id=1, source_target_pairs={{0,4},{4,8},{8,12},{12,0},{1,5},{5,9},{9,13},{13,1},{2,6},{6,10},{... | collective-permute-start | bytes 1572872 | tf_op jit(solution)/shard_map/ppermute | solution.py:598
  94.6 16.1 %collective-permute-start.8 = (bf16[256,1024]{1,0:T(8,128)(2,1)}, bf16[256,1024]{1,0:T(8,128)(2,1)}, u32[]{:S(2)}, u32[]{:S(2)}) collective-permute-start(bf16[256,1024]{1,0:T(8,128)(2,1)} %slice.15), channel_id=1, source_target_pairs={{4,0},{8,4},{12,8},{0,12},{5,1},{9,5},{13,9},{1,13},{6,2},{10,6},{... | collective-permute-start | bytes 1572872 | tf_op jit(solution)/shard_map/ppermute | solution.py:598
  99.2 0.8 copy-start.2
  127.6 46.3 %copy-start.3 = (f32[4,256,32]{2,1,0:T(8,128)S(1)}, f32[4,256,32]{2,1,0:T(8,128)}, u32[]{:S(2)}) copy-start(f32[4,256,32]{2,1,0:T(8,128)} %copy-done.2) | copy-start | bytes 393220
  174.2 3.0 %collective-permute-start.9 = (f32[1,256]{1,0:T(1,128)S(1)}, f32[1,256]{1,0:T(1,128)S(1)}, u32[]{:S(2)}, u32[]{:S(2)}) collective-permute-start(f32[1,256]{1,0:T(1,128)S(1)} %get-tuple-element.44), channel_id=1, source_target_pairs={{0,16},{16,32},{32,48},{48,64},{64,80},{80,96},{96,112},{112,128},... | collective-permute-start | bytes 3080 | tf_op jit(solution)/shard_map/ppermute | solution.py:648
